TPU v7x, 128 devices: a whole 4x4x4 slice. The times are simulated.
128 devices in a mesh: gx: 16 (over y, z), gy: 8 (over x, core).
Axes of the slice: x: 4, y: 4, z: 4, core: 2. Of those that a mesh axis runs over, the one named last changes fastest.
Arguments:
- inputs: float32 [2, 128, 8192], P(None, 'gy', 'gx'), may hold values from -56 to 56
- positions: int32 [128], P(('gx', 'gy')), may hold values from 1024 to 4095
- attn_gain: float32 [8192], P('gx'), may hold values from 0.5 to 1.5
- ffn_gain: float32 [8192], P('gx'), may hold values from 0.5 to 1.5
- qkv_weight: bfloat16 [8192, 10240], P('gx', 'gy'), may hold values from -0.0625 to 0.0625
- out_weight: bfloat16 [8192, 8192], P('gy', 'gx'), may hold values from -0.0625 to 0.0625
- gate_weight: bfloat16 [8192, 28672], P('gx', 'gy'), may hold values from -0.0625 to 0.0625
- up_weight: bfloat16 [8192, 28672], P('gx', 'gy'), may hold values from -0.0625 to 0.0625
- down_weight: bfloat16 [28672, 8192], P('gy', 'gx'), may hold values from -0.03125 to 0.03125
- k_cache: bfloat16 [128, 8, 1024, 128], P(('gx', 'gy')), may hold values from -400 to 400
- v_cache: bfloat16 [128, 8, 1024, 128], P(('gx', 'gy')), may hold values from -12 to 12
Outputs:
- outputs: float32 [2, 128, 8192], P(None, 'gy', 'gx')
- new_kv: bfloat16 [128, 2, 8, 256], P(('gx', 'gy'))
All inputs are finite; a program needn't handle non-finite values.
Results may differ from a plain program's by a relative error of at most 0.0065.
Values may be sent and summed in bfloat16 or wider, within the bound.
No kernel may reach another device: no remote copies, remote signals or barrier semaphores. Data moves between devices by JAX's collectives and lax.ppermute only.
A program may use at most 128 MiB of HBM per device.

v0:
```python
import jax
import jax.numpy as jnp
from jax import lax
from jax.sharding import PartitionSpec as P

D = 8192
KVH = 8
HD = 128
CACHE = 1024
GQ = 8


EPSILON = 1e-05
THETA = 500000.0


def rotate(vectors, angle_pos):
    half_size = vectors.shape[-1] // 2
    frequency = jnp.exp(
        jnp.arange(half_size, dtype=jnp.float32) * (-2.0 / vectors.shape[-1]) * jnp.log(THETA)
    )
    angles = angle_pos[..., None] * frequency
    cosine = jnp.cos(angles)
    sine_part = jnp.sin(angles)
    first_half = vectors[..., :half_size]
    second_half = vectors[..., half_size:]
    return jnp.concatenate(
        [
            first_half * cosine - second_half * sine_part,
            second_half * cosine + first_half * sine_part,
        ],
        -1,
    )


def normalize(residual, gain):
    squares = lax.psum(jnp.sum(residual * residual, axis=1), "gx")
    scale_rows = lax.rsqrt(squares / D + EPSILON)
    return (residual * scale_rows[:, None] * gain).astype(jnp.bfloat16)


def gather_rows_gy(normed):
    return lax.all_gather(normed, "gy", axis=0, tiled=True)


def gather_rows_gx(block):
    return lax.all_gather(block, "gx", axis=0, tiled=True)


def sum_over_gx(all_rows, weights):
    row_share = all_rows.shape[0] // lax.axis_size("gx")

    def partial_term(start, row_count):
        return jnp.concatenate(
            [jnp.dot(all_rows, matrix, preferred_element_type=jnp.float32) for matrix in weights], 1
        )

    return lax.psum_scatter(
        partial_term(jnp.int32(0), lax.axis_size("gx") * row_share),
        "gx",
        scatter_dimension=0,
        tiled=True,
    )


def sum_over_gy(all_rows, matrix):
    row_share = all_rows.shape[0] // lax.axis_size("gy")

    def partial_term(start, row_count):
        return jnp.dot(all_rows, matrix, preferred_element_type=jnp.float32)

    return lax.psum_scatter(
        partial_term(jnp.int32(0), row_share * lax.axis_size("gy")).astype(jnp.bfloat16),
        "gy",
        scatter_dimension=0,
        tiled=True,
    ).astype(jnp.float32)


def regroup(blocks):
    return lax.all_to_all(blocks, "gy", split_axis=0, concat_axis=0, tiled=True)


def per_device(
    inputs,
    positions,
    attn_gain,
    ffn_gain,
    qkv_weight,
    out_weight,
    gate_weight,
    up_weight,
    down_weight,
    k_cache,
    v_cache,
):
    group_span = lax.axis_size("gy")
    local_groups = KVH // group_span
    row_count = k_cache.shape[0]
    cache_keys = k_cache.reshape(row_count, group_span, local_groups, CACHE, HD)
    cache_values = v_cache.reshape(row_count, group_span, local_groups, CACHE, HD)
    fresh_k = []
    fresh_v = []
    results = []
    kv_steps = []
    for step_index in range(2):
        residual = inputs[step_index]
        normed = normalize(residual, attn_gain)
        qkv = sum_over_gx(gather_rows_gy(normed), (qkv_weight,)).astype(jnp.bfloat16)
        sent = qkv.reshape(group_span, qkv.shape[0] // group_span, qkv.shape[1])
        received = regroup(sent).reshape(group_span, row_count, local_groups, GQ + 2, HD)
        angle_pos = (positions + step_index).astype(jnp.float32)
        queries = (
            rotate(received[:, :, :, :GQ].astype(jnp.float32), angle_pos[None, :, None, None])
            * HD ** (-0.5)
        ).astype(jnp.bfloat16)
        key_now = rotate(
            received[:, :, :, GQ].astype(jnp.float32), angle_pos[None, :, None]
        ).astype(jnp.bfloat16)
        value_now = received[:, :, :, GQ + 1]
        fresh_k.append(key_now)
        fresh_v.append(value_now)
        joined_kv = jnp.concatenate([key_now, value_now], -1)
        kv_steps.append(jnp.transpose(joined_kv, (1, 0, 2, 3)).reshape(row_count, KVH, 2 * HD))
        stacked_keys = jnp.stack(fresh_k, 3)
        stacked_values = jnp.stack(fresh_v, 3)
        cache_scores = jnp.einsum(
            "jnlhd,njlcd->njlhc", queries, cache_keys, preferred_element_type=jnp.float32
        )
        fresh_scores = jnp.einsum(
            "jnlhd,jnlsd->njlhs", queries, stacked_keys, preferred_element_type=jnp.float32
        )
        row_top = jnp.maximum(jnp.max(cache_scores, -1), jnp.max(fresh_scores, -1))[..., None]
        cache_exp = jnp.exp(cache_scores - row_top)
        fresh_exp = jnp.exp(fresh_scores - row_top)
        row_total = jnp.sum(cache_exp, -1, keepdims=True) + jnp.sum(fresh_exp, -1, keepdims=True)
        cache_probs = (cache_exp / row_total).astype(jnp.bfloat16)
        fresh_probs = (fresh_exp / row_total).astype(jnp.bfloat16)
        attended = jnp.einsum(
            "njlhc,njlcd->jnlhd", cache_probs, cache_values, preferred_element_type=jnp.float32
        )
        attended = attended + jnp.einsum(
            "njlhs,jnlsd->jnlhd", fresh_probs, stacked_values, preferred_element_type=jnp.float32
        )
        attended = attended.astype(jnp.bfloat16).reshape(
            group_span, row_count, local_groups * GQ * HD
        )
        head_rows = regroup(attended).reshape(group_span * row_count, local_groups * GQ * HD)
        after_attn = residual + sum_over_gy(gather_rows_gx(head_rows), out_weight)
        normed_ffn = normalize(after_attn, ffn_gain)
        all_rows = gather_rows_gy(normed_ffn)
        joined = sum_over_gx(all_rows, (gate_weight, up_weight))
        unit_count = gate_weight.shape[1]
        hidden = (jax.nn.silu(joined[:, :unit_count]) * joined[:, unit_count:]).astype(jnp.bfloat16)
        hidden_full = gather_rows_gx(hidden)
        results.append(after_attn + sum_over_gy(hidden_full, down_weight))
    return (jnp.stack(results, 0), jnp.stack(kv_steps, 1))


def solution(mesh):
    placed = (
        P(None, "gy", "gx"),
        P(("gx", "gy")),
        P("gx"),
        P("gx"),
        P("gx", "gy"),
        P("gy", "gx"),
        P("gx", "gy"),
        P("gx", "gy"),
        P("gy", "gx"),
        P(("gx", "gy"), None, None, None),
        P(("gx", "gy"), None, None, None),
    )
    return jax.shard_map(
        per_device,
        mesh=mesh,
        in_specs=placed,
        out_specs=(P(None, "gy", "gx"), P(("gx", "gy"), None, None, None)),
        check_vma=False,
    )
```

profile of v0, /device:TPU:0, one launch (start us, length us, event | category | flops | bytes accessed | tf_op | source)
XLA Modules:
  0.0 590.6 jit_solution(16734909145665369604)
XLA Ops:
  8.2 42.0 %all-reduce.6 = (f32[16]{0:T(128)S(1)}, f32[16]{0:T(128)S(1)}) all-reduce(f32[16]{0:T(128)S(1)} %get-tuple-element.4, f32[16]{0:T(128)S(1)} %get-tuple-element.5), channel_id=1, replica_groups=mesh['gx'=16,'gy'=8] {'gx'}, use_global_device_ids=true, to_apply=%region_1.0 | all-reduce | flops 32 | bytes 256 | tf_op jit(solution)/shard_map/psum | solution.py:37
  51.1 13.1 %all_gather.28 = bf16[128,512]{1,0:T(8,128)(2,1)S(1)} all-gather(bf16[16,512]{1,0:T(8,128)(2,1)S(1)} %get-tuple-element.16), channel_id=1, replica_groups=mesh['gx'=16,'gy'=8] {'gy'}, dimensions={0}, use_global_device_ids=true | all-gather | bytes 147456 | tf_op jit(solution)/shard_map/all_gather | solution.py:43
  64.2 12.7 %all_gather.24 = bf16[128,512]{1,0:T(8,128)(2,1)S(1)} all-gather(bf16[16,512]{1,0:T(8,128)(2,1)S(1)} %get-tuple-element.17), channel_id=1, replica_groups=mesh['gx'=16,'gy'=8] {'gy'}, dimensions={0}, use_global_device_ids=true | all-gather | bytes 147456 | tf_op jit(solution)/shard_map/all_gather | solution.py:43
  81.6 83.2 %all-reduce.12 = (bf16[128,1280]{1,0:T(8,128)(2,1)}, bf16[128,1280]{1,0:T(8,128)(2,1)}) all-reduce(f32[128,1280]{1,0:T(8,128)S(1)} %fusion.71, f32[128,1280]{1,0:T(8,128)S(1)} %fusion.74), channel_id=4, replica_groups=mesh['gx'=16,'gy'=8] {'gx'}, use_global_device_ids=true, to_apply=%region_2.0.clone | all-reduce | flops 327680 | bytes 1966080
  167.3 3.7 all-to-all-start
  176.4 3.3 all-to-all-start.2
  179.8 5.2 all-to-all-done.2
  190.2 3.3 all-to-all-start.1
  198.8 4.3 all-to-all-start.3
  203.3 20.8 %all-gather = bf16[128,1,1024]{2,0,1:T(8,128)(2,1)S(1)} all-gather(bf16[8,1,1024]{2,0,1:T(8,128)(2,1)S(1)} %copy.60), channel_id=2, replica_groups=mesh['gx'=16,'gy'=8] {'gx'}, dimensions={0}, use_global_device_ids=true | all-gather | bytes 278528 | tf_op jit(solution)/shard_map/all_gather | solution.py:47
  225.2 23.8 %all-gather.1 = bf16[128,1,1024]{2,0,1:T(8,128)(2,1)S(1)} all-gather(bf16[8,1,1024]{2,0,1:T(8,128)(2,1)S(1)} %copy.70), channel_id=3, replica_groups=mesh['gx'=16,'gy'=8] {'gx'}, dimensions={0}, use_global_device_ids=true | all-gather | bytes 278528 | tf_op jit(solution)/shard_map/all_gather | solution.py:47
  250.0 5.6 reduce-scatter.5.cloned.1.call-done
  255.6 31.6 %reduce-scatter.9.cloned.1.call-done = bf16[16,512]{1,0:T(8,128)(2,1)} async-done(((bf16[128,512]{1,0:T(8,128)(2,1)}), bf16[16,512]{1,0:T(8,128)(2,1)}) %reduce-scatter.9.cloned.1.call-update) | async-done | bytes 16400 | tf_op jit(solution)/shard_map/reduce_scatter | solution.py:72
  288.1 40.6 %all-reduce.4 = (f32[16]{0:T(128)S(1)}, f32[16]{0:T(128)S(1)}) all-reduce(f32[16]{0:T(128)S(1)} %get-tuple-element.3, f32[16]{0:T(128)S(1)} %get-tuple-element.2), channel_id=1, replica_groups=mesh['gx'=16,'gy'=8] {'gx'}, use_global_device_ids=true, to_apply=%region_19.20 | all-reduce | flops 32 | bytes 256 | tf_op jit(solution)/shard_map/psum | solution.py:37
  329.7 12.9 %all_gather.26 = bf16[128,512]{1,0:T(8,128)(2,1)S(1)} all-gather(bf16[16,512]{1,0:T(8,128)(2,1)S(1)} %get-tuple-element.14), channel_id=1, replica_groups=mesh['gx'=16,'gy'=8] {'gy'}, dimensions={0}, use_global_device_ids=true | all-gather | bytes 147456 | tf_op jit(solution)/shard_map/all_gather | solution.py:43
  342.6 12.7 %all_gather.30 = bf16[128,512]{1,0:T(8,128)(2,1)S(1)} all-gather(bf16[16,512]{1,0:T(8,128)(2,1)S(1)} %get-tuple-element.15), channel_id=1, replica_groups=mesh['gx'=16,'gy'=8] {'gy'}, dimensions={0}, use_global_device_ids=true | all-gather | bytes 147456 | tf_op jit(solution)/shard_map/all_gather | solution.py:43
  355.3 2.7 fusion.76
  365.8 126.9 %all-reduce.11.cloned.1.call-done = (f32[128,7168]{1,0:T(8,128)}, f32[128,7168]{1,0:T(8,128)}) async-done(((f32[128,7168]{1,0:T(8,128)}, f32[128,7168]{1,0:T(8,128)}), (f32[128,7168]{1,0:T(8,128)}, f32[128,7168]{1,0:T(8,128)})) %all-reduce.11.cloned.1.call-update) | async-done | bytes 7340048
  494.8 24.1 %all_gather.27 = bf16[128,3584]{1,0:T(8,128)(2,1)S(1)} all-gather(bf16[8,3584]{1,0:T(8,128)(2,1)S(1)} %fusion.29), channel_id=1, replica_groups=mesh['gx'=16,'gy'=8] {'gx'}, dimensions={0}, use_global_device_ids=true | all-gather | bytes 974848 | tf_op jit(solution)/shard_map/all_gather | solution.py:47
  519.0 3.3 convolution_convert_fusion.1
  522.4 22.5 %all_gather.31 = bf16[128,3584]{1,0:T(8,128)(2,1)S(1)} all-gather(bf16[8,3584]{1,0:T(8,128)(2,1)S(1)} %fusion.28), channel_id=1, replica_groups=mesh['gx'=16,'gy'=8] {'gx'}, dimensions={0}, use_global_device_ids=true | all-gather | bytes 974848 | tf_op jit(solution)/shard_map/all_gather | solution.py:47
  544.8 3.4 convolution_convert_fusion
  549.0 2.8 reduce-scatter.7.cloned.1.call-done
  551.8 30.9 %reduce-scatter.11.cloned.1.call-done = bf16[16,512]{1,0:T(8,128)(2,1)} async-done(((bf16[128,512]{1,0:T(8,128)(2,1)}), bf16[16,512]{1,0:T(8,128)(2,1)}) %reduce-scatter.11.cloned.1.call-update) | async-done | bytes 16400 | tf_op jit(solution)/shard_map/reduce_scatter | solution.py:72
  (111 shorter events, 39.5 us)
Async XLA Ops:
  7.2 178.6 %copy-start = (bf16[1,8,1024,128]{3,2,1,0:T(8,128)(2,1)S(1)}, bf16[1,8,1024,128]{3,2,1,0:T(8,128)(2,1)}, u32[]{:S(2)}) copy-start(bf16[1,8,1024,128]{3,2,1,0:T(8,128)(2,1)} %param.20) | copy-start | bytes 6291460
  7.2 73.1 %copy-start.8 = (u32[128]{0:T(128)S(1)}, u32[128]{0:T(128)}, u32[]{:S(2)}) copy-start(u32[128]{0:T(128)} %constant.29) | copy-start | bytes 1540
  167.3 9.1 %all-to-all-start = ((bf16[8,2,640]{2,1,0:T(2,128)(2,1)}), bf16[8,2,640]{2,1,0:T(2,128)(2,1)S(1)}, u32[]{:S(2)}, u32[]{:S(2)}) async-start(bf16[8,2,640]{2,1,0:T(2,128)(2,1)} %reshape.448), calls=%async_computation | async-start | bytes 40960 | tf_op jit(solution)/shard_map/all_to_all | solution.py:81
  176.4 8.6 %all-to-all-start.2 = ((bf16[8,2,640]{2,1,0:T(2,128)(2,1)}), bf16[8,2,640]{2,1,0:T(2,128)(2,1)S(1)}, u32[]{:S(2)}, u32[]{:S(2)}) async-start(bf16[8,2,640]{2,1,0:T(2,128)(2,1)} %reshape.452), calls=%async_computation.4 | async-start | bytes 40960 | tf_op jit(solution)/shard_map/all_to_all | solution.py:81
  186.7 37.4 %copy-start.3 = (bf16[1024,512]{1,0:T(8,128)(2,1)S(1)}, bf16[1024,512]{1,0:T(8,128)(2,1)}, u32[]{:S(2)}) copy-start(bf16[1024,512]{1,0:T(8,128)(2,1)} %param.16) | copy-start | bytes 3145732
  190.2 8.6 %all-to-all-start.1 = ((bf16[8,2,512]{2,1,0:T(2,128)(2,1)}), bf16[8,2,512]{2,1,0:T(2,128)(2,1)S(1)}, u32[]{:S(2)}, u32[]{:S(2)}) async-start(bf16[8,2,512]{2,1,0:T(2,128)(2,1)} %reshape.450), calls=%async_computation.1 | async-start | bytes 32768 | tf_op jit(solution)/shard_map/all_to_all | solution.py:81
  194.4 92.9 %copy-start.4 = (f32[2,16,512]{2,1,0:T(8,128)S(1)}, f32[2,16,512]{2,1,0:T(8,128)}, u32[]{:S(2)}) copy-start(f32[2,16,512]{2,1,0:T(8,128)} %param.11) | copy-start | bytes 196612
  194.4 134.4 %copy-start.7 = (f32[512]{0:T(512)S(1)}, f32[512]{0:T(512)}, u32[]{:S(2)}) copy-start(f32[512]{0:T(512)} %param.14) | copy-start | bytes 6148
  198.8 26.3 %all-to-all-start.3 = ((bf16[8,2,512]{2,1,0:T(2,128)(2,1)}), bf16[8,2,512]{2,1,0:T(2,128)(2,1)S(1)}, u32[]{:S(2)}, u32[]{:S(2)}) async-start(bf16[8,2,512]{2,1,0:T(2,128)(2,1)} %reshape.454), calls=%async_computation.5 | async-start | bytes 32768 | tf_op jit(solution)/shard_map/all_to_all | solution.py:81
  203.2 52.4 %reduce-scatter.5.cloned.1.call-start = ((), (), s32[]{:S(2)}) async-start(), calls=%async_computation.8 | async-start | bytes 147456 | tf_op jit(solution)/shard_map/reduce_scatter | solution.py:72
  225.1 62.2 %reduce-scatter.9.cloned.1.call-start = ((), (), s32[]{:S(2)}) async-start(), calls=%async_computation.10 | async-start | bytes 147456 | tf_op jit(solution)/shard_map/reduce_scatter | solution.py:72
  249.9 242.8 %all-reduce.11.cloned.1.call-start = ((), (), s32[]{:S(2)}) async-start(), calls=%async_computation.12 | async-start | bytes 14680064
  328.7 29.3 %copy-start.2 = (bf16[512,3584]{1,0:T(8,128)(2,1)S(1)}, bf16[512,3584]{1,0:T(8,128)(2,1)}, u32[]{:S(2)}) copy-start(bf16[512,3584]{1,0:T(8,128)(2,1)} %param.17) | copy-start | bytes 11010052
  358.0 2.0 copy-start.1
  365.8 186.0 %reduce-scatter.7.cloned.1.call-start = ((), (), s32[]{:S(2)}) async-start(), calls=%async_computation.9 | async-start | bytes 147456 | tf_op jit(solution)/shard_map/reduce_scatter | solution.py:72
  522.3 60.4 %copy-start.5 = (bf16[16,512]{1,0:T(8,128)(2,1)S(1)}, bf16[16,512]{1,0:T(8,128)(2,1)}, u32[]{:S(2)}) copy-start(bf16[16,512]{1,0:T(8,128)(2,1)} %reduce-scatter.5.cloned.1.call-done) | copy-start | bytes 49156
  522.3 60.4 %copy-start.6 = (bf16[16,512]{1,0:T(8,128)(2,1)S(1)}, bf16[16,512]{1,0:T(8,128)(2,1)}, u32[]{:S(2)}) copy-start(bf16[16,512]{1,0:T(8,128)(2,1)} %reduce-scatter.9.cloned.1.call-done) | copy-start | bytes 49156
  522.3 60.4 %reduce-scatter.11.cloned.1.call-start = ((), (), s32[]{:S(2)}) async-start(), calls=%async_computation.11 | async-start | bytes 147456 | tf_op jit(solution)/shard_map/reduce_scatter | solution.py:72
Sparse Core Ops, SparseCore 0:
  225.2 30.3 reduce-scatter.4
  258.1 29.1 reduce-scatter.8
  365.9 126.7 all-reduce.10
  522.4 29.2 reduce-scatter.6
  554.0 28.7 reduce-scatter.10
where the time goes:
time: 592 us; the launch traced here: 591 us
  blocking collectives  309 us (52%)
  waiting for transfers between devices  206 us (35%)
  matrix products  22.7 us (4%)
  other arithmetic  16.2 us (3%)
  between operations  15.4 us (3%)
  starting transfers between devices  14.9 us (3%)
  local copies, waits for them, and re-layouts  6.62 us (1%)
    unnamed x6, waiting for transfers between devices  127 us
    all_gather x4, blocking collectives, gather_rows_gx(): return lax.all_gather(block, 'gx', axis=0, tiled=True)  91.2 us
    unnamed x1, blocking collectives  83.2 us
    psum x2, blocking collectives, normalize(): squares = lax.psum(jnp.sum(residual * residual, axis=1), 'gx')  82.7 us
    reduce_scatter x4, waiting for transfers between devices, sum_over_gy(): lax.psum_scatter(partial_term(jnp.int32(0), row_share * lax.axis_size('gy...  71 us
    all_gather x4, blocking collectives, gather_rows_gy(): return lax.all_gather(normed, 'gy', axis=0, tiled=True)  51.5 us
    all_to_all x4, starting transfers between devices, regroup(): return lax.all_to_all(blocks, 'gy', split_axis=0, concat_axis=0, tiled=True)  14.7 us
  transfers between devices with their start and end apart: 9, of which 8 were waited for; matrix products, arithmetic and copies ran while one was open for 2% of the time, Pallas kernels for 0%

commit v1 on v0

v1 whole, which is shorter than its diff:
```python
import functools

import jax
import jax.numpy as jnp
from jax import lax
from jax.experimental import pallas as pl
from jax.experimental.pallas import tpu as pltpu
from jax.sharding import PartitionSpec as P

D = 8192
KVH = 8
HD = 128
CACHE = 1024
GQ = 8
EPSILON = 1e-05
THETA = 500000.0
NX = 16
NY = 8
WIDTH = 512
UNITS = 3584
FLOWS = 4
FW = UNITS // FLOWS
F32 = jnp.float32
BF16 = jnp.bfloat16
MIB = 1 << 20

VM = pl.BlockSpec(memory_space=pltpu.VMEM)
SM = pl.BlockSpec(memory_space=pltpu.SMEM)
ANY = pl.BlockSpec(memory_space=pl.ANY)


def swap_gx(array, bits):
    return lax.ppermute(array, "gx", [(i, i ^ bits) for i in range(NX)])


def swap_gy(array, bits):
    return lax.ppermute(array, "gy", [(i, i ^ bits) for i in range(NY)])


def gray(place):
    return ((place & 1) ^ (place >> 1)) * 2 + (place >> 1)


def call(body, outs, ins, scratch=(), limit=32):
    return pl.pallas_call(
        body,
        out_shape=outs,
        in_specs=ins,
        out_specs=jax.tree.map(lambda _: VM, outs),
        scratch_shapes=list(scratch),
        compiler_params=pltpu.CompilerParams(vmem_limit_bytes=limit * MIB),
    )


def shaped(shape, dtype):
    return jax.ShapeDtypeStruct(shape, dtype)


def qkv_body(where, near, far, gain, weight, out, lhs, rows, held, sem):
    fetch = pltpu.make_async_copy(weight, held, sem)
    fetch.start()
    mine = where[1]
    for flag, source in enumerate((near, far)):
        for k in range(4):
            block = mine ^ (2 * k + flag)
            for t in range(2):
                start = pl.multiple_of(t * 128 + block * 16, 16)
                lhs[pl.ds(start, 16), :] = source[k * 32 + t * 16 : k * 32 + t * 16 + 16, :]
    plain = lhs[...].astype(F32) / gain[...]
    squares = jnp.sum(plain * plain, axis=1, keepdims=True)
    for t in range(2):
        whole = jnp.broadcast_to(squares[t * 128 : t * 128 + 128], (128, HD))
        high = whole.astype(BF16).astype(F32)
        rows[pl.ds(20 + 2 * t, 128, stride=24), :] = high
        rows[pl.ds(21 + 2 * t, 128, stride=24), :] = whole - high
    fetch.wait()
    for pair in range(5):
        part = jnp.dot(lhs[...], held[:, pair * 256 : pair * 256 + 256], preferred_element_type=F32)
        for j in (2 * pair, 2 * pair + 1):
            for t in range(2):
                place = t * 8 + j if j < GQ else 16 + (j - GQ) * 2 + t
                column = (j - 2 * pair) * HD
                rows[pl.ds(place, 128, stride=24), :] = part[t * 128 : t * 128 + 128, column : column + HD]
    out[...] = rows[...].astype(BF16)


def qkv_partial(where, near, far, gain, weight):
    return call(
        qkv_body,
        shaped((128 * 24, HD), BF16),
        [SM, VM, VM, VM, ANY],
        [
            pltpu.VMEM((256, WIDTH), BF16),
            pltpu.VMEM((128 * 24, HD), F32),
            pltpu.VMEM((WIDTH, 1280), BF16),
            pltpu.SemaphoreType.DMA,
        ],
    )(where, near, far, gain, weight)


def turn(vectors, cosine, sine):
    return vectors * cosine + pltpu.roll(vectors, HD // 2, vectors.ndim - 1) * sine


def attend_body(angles, received, keys, values, out, fresh, scores, held_k, held_v, sem_k, sem_v):
    fetches = []
    for g in range(KVH):
        for cache, held, sem in ((keys, held_k, sem_k), (values, held_v, sem_v)):
            fetch = pltpu.make_async_copy(cache.at[0, g], held.at[g], sem.at[g])
            fetch.start()
            fetches.append(fetch)
    total = received[0].astype(F32)
    for i in range(1, NX):
        total = total + received[i].astype(F32)
    squares = total[:, 20:24, :]
    scales = []
    for t in range(2):
        square = squares[:, 2 * t : 2 * t + 1, :] + squares[:, 2 * t + 1 : 2 * t + 2, :]
        scales.append(lax.rsqrt(square / D + EPSILON))
    cosines = [angles[2 * t : 2 * t + 1, :] for t in range(2)]
    sines = [angles[2 * t + 1 : 2 * t + 2, :] for t in range(2)]
    queries, new_keys, new_values = [], [], []
    for t in range(2):
        head = (total[:, 8 * t : 8 * t + 8, :] * scales[t]).astype(BF16).astype(F32)
        flat = turn(head.reshape(64, HD), cosines[t], sines[t])
        queries.append((flat * HD**-0.5).astype(BF16).astype(F32).reshape(8, 8, HD))
        key = (total[:, 16 + t : 17 + t, :] * scales[t]).astype(BF16).astype(F32).reshape(8, HD)
        new_keys.append(turn(key, cosines[t], sines[t]).astype(BF16))
        value = (total[:, 18 + t : 19 + t, :] * scales[t]).astype(BF16).reshape(8, HD)
        new_values.append(value)
        fresh[0, t, :, :HD] = new_keys[t]
        fresh[0, t, :, HD:] = value
    both = jnp.concatenate(queries, axis=1)
    both16 = both.astype(BF16)
    for g in range(KVH):
        fetches[2 * g].wait()
        scores[g * 16 : g * 16 + 16, :] = lax.dot_general(
            both16[g], held_k[g], (((1,), (1,)), ((), ())), preferred_element_type=F32
        )
    extra = []
    step = lax.broadcasted_iota(jnp.int32, (KVH, 16, 1), 1) // GQ
    for t in range(2):
        dots = jnp.sum(both * new_keys[t].astype(F32).reshape(KVH, 1, HD), axis=2, keepdims=True)
        if t == 1:
            dots = jnp.where(step >= 1, dots, -3.0e38)
        extra.append(dots.reshape(128, 1))
    cached = scores[...]
    top = jnp.maximum(jnp.max(cached, axis=1, keepdims=True), jnp.maximum(extra[0], extra[1]))
    cached = jnp.exp(cached - top)
    extra = [jnp.exp(value - top) for value in extra]
    share = 1.0 / (jnp.sum(cached, axis=1, keepdims=True) + extra[0] + extra[1])
    probs = (cached * share).astype(BF16)
    extra = [(value * share).astype(BF16).astype(F32).reshape(KVH, 16, 1) for value in extra]
    for g in range(KVH):
        fetches[2 * g + 1].wait()
        mixed = jnp.dot(probs[g * 16 : g * 16 + 16, :], held_v[g], preferred_element_type=F32)
        for t in range(2):
            mixed = mixed + extra[t][g] * new_values[t][g : g + 1, :].astype(F32)
        mixed = mixed.astype(BF16)
        for i in range(NX):
            out[i, g] = mixed


def attend(angles, received, keys, values):
    return call(
        attend_body,
        (shaped((NX, KVH, 16, HD), BF16), shaped((1, 2, KVH, 2 * HD), BF16)),
        [VM, VM, ANY, ANY],
        [
            pltpu.VMEM((KVH * 16, CACHE), F32),
            pltpu.VMEM((KVH, CACHE, HD), BF16),
            pltpu.VMEM((KVH, CACHE, HD), BF16),
            pltpu.SemaphoreType.DMA((KVH,)),
            pltpu.SemaphoreType.DMA((KVH,)),
        ],
    )(angles, received, keys, values)


def out_body(where, received, weight, keep, send, wide, lhs, held, sem):
    fetch = pltpu.make_async_copy(weight, held, sem)
    fetch.start()
    mine = where[1]
    wide[...] = received[...].astype(F32)
    for flag in range(2):
        for k in range(4):
            block = mine ^ (2 * k + flag)
            for t in range(2):
                place = flag * 128 + k * 32 + t * 16
                for h in range(GQ):
                    start = block * 256 + t * 8 + h
                    lhs[place : place + 16, h * HD : h * HD + HD] = wide[
                        pl.ds(start, 16, stride=16), :
                    ].astype(BF16)
    fetch.wait()
    keep[...] = jnp.dot(lhs[:128, :], held[...], preferred_element_type=F32)
    send[...] = jnp.dot(lhs[128:, :], held[...], preferred_element_type=F32).astype(BF16)


def out_partial(where, received, weight):
    return call(
        out_body,
        (shaped((128, WIDTH), F32), shaped((128, WIDTH), BF16)),
        [SM, VM, ANY],
        [
            pltpu.VMEM((128 * 16, HD), F32),
            pltpu.VMEM((256, KVH * HD), BF16),
            pltpu.VMEM((KVH * HD, WIDTH), BF16),
            pltpu.SemaphoreType.DMA,
        ],
    )(where, received, weight)


def split_body(keep, other, own, *sends):
    whole = keep[...] + other[...].astype(F32)
    own[...] = whole[:32]
    for k, send in enumerate(sends):
        send[...] = whole[32 * k + 32 : 32 * k + 64].astype(BF16)


def sum_over_gy(keep, send):
    other = swap_gy(send, 1)
    own, *sends = call(
        split_body,
        (shaped((32, WIDTH), F32),) + (shaped((32, WIDTH), BF16),) * 3,
        [VM, VM],
    )(keep, other)
    return [own] + [swap_gy(piece, 2 * (k + 1)) for k, piece in enumerate(sends)]


def residual_body(residual, gain, own, one, two, three, after, normed):
    whole = residual[...] + (own[...] + one[...].astype(F32) + two[...].astype(F32) + three[...].astype(F32))
    after[...] = whole
    normed[...] = (whole * gain[...]).astype(BF16)


def final_body(residual, own, one, two, three, out):
    out[...] = residual[...] + (own[...] + one[...].astype(F32) + two[...].astype(F32) + three[...].astype(F32))


def stack_body(*refs):
    *pieces, out = refs
    rows = pieces[0].shape[0]
    for k, piece in enumerate(pieces):
        out[k * rows : k * rows + rows, :] = piece[...]


def gather_gy(own):
    pieces = [own] + [swap_gy(own, 2 * k) for k in (1, 2, 3)]
    near = call(stack_body, shaped((128, WIDTH), BF16), [VM] * 4)(*pieces)
    return near, swap_gy(near, 1)


def rotate_left(value, by):
    return ((value << by) | (value >> (4 - by))) & 15 if by else value


def widths():
    return [2 * FW + (HD if f == 0 else 0) for f in range(FLOWS)]


def gate_body(where, near, far, gain, gate, up, *refs):
    outs, (lhs, held, sem) = refs[: 2 * FLOWS], refs[2 * FLOWS :]
    fetches = []
    for f in range(FLOWS):
        for i, weight in enumerate((gate, up)):
            fetch = pltpu.make_async_copy(weight.at[:, pl.ds(f * FW, FW)], held.at[f, i], sem.at[f, i])
            fetch.start()
            fetches.append(fetch)
    for f in range(FLOWS):
        for flag, source in enumerate((near, far)):
            for k in range(4):
                block = where[1] ^ (2 * k + flag)
                for t in range(2):
                    place = rotate_left((2 * block + t) ^ where[0], f)
                    start = pl.multiple_of(place * 16, 16)
                    lhs[f, pl.ds(start, 16), :] = source[k * 32 + t * 16 : k * 32 + t * 16 + 16, :]
    for f in range(FLOWS):
        keep, send = outs[2 * f], outs[2 * f + 1]
        if f == 0:
            plain = lhs[0].astype(F32) / gain[...]
            squares = jnp.sum(plain * plain, axis=1, keepdims=True)
            keep[:, 2 * FW :] = jnp.broadcast_to(squares[:128], (128, HD))
            send[:, 2 * FW :] = two_parts(jnp.broadcast_to(squares[128:], (128, HD)))
        for i in range(2):
            fetches[2 * f + i].wait()
            columns = slice(i * FW, i * FW + FW)
            keep[:, columns] = jnp.dot(lhs[f, :128, :], held[f, i], preferred_element_type=F32)
            send[:, columns] = jnp.dot(lhs[f, 128:, :], held[f, i], preferred_element_type=F32).astype(BF16)


def two_parts(squares):
    high = squares.astype(BF16).astype(F32)
    first = lax.broadcasted_iota(jnp.int32, squares.shape, 1) < HD // 2
    return jnp.where(first, high, squares - high).astype(BF16)


def one_part(parts):
    wide = parts.astype(F32)
    return wide + pltpu.roll(wide, HD // 2, 1)


def gate_partial(where, near, far, gain, gate, up):
    outs = []
    for width in widths():
        outs += [shaped((128, width), F32), shaped((128, width), BF16)]
    return call(
        gate_body,
        tuple(outs),
        [SM, VM, VM, VM, ANY, ANY],
        [
            pltpu.VMEM((FLOWS, 256, WIDTH), BF16),
            pltpu.VMEM((FLOWS, 2, WIDTH, FW), BF16),
            pltpu.SemaphoreType.DMA((FLOWS, 2)),
        ],
        limit=40,
    )(where, near, far, gain, gate, up)


def halve_body(*refs):
    ins, outs = refs[: 2 * FLOWS], refs[2 * FLOWS :]
    for f in range(FLOWS):
        keep, other = ins[2 * f], ins[2 * f + 1]
        half = keep.shape[0] // 2
        whole = keep[:, : 2 * FW] + other[:, : 2 * FW].astype(F32)
        outs[2 * f][:, : 2 * FW] = whole[:half]
        outs[2 * f + 1][:, : 2 * FW] = whole[half:].astype(BF16)
        if f == 0:
            squares = keep[:, 2 * FW :] + one_part(other[:, 2 * FW :])
            outs[0][:, 2 * FW :] = squares[:half]
            outs[1][:, 2 * FW :] = two_parts(squares[half:])


def hidden_body(*refs):
    ins, outs = refs[: 2 * FLOWS], refs[2 * FLOWS :]
    squares = ins[0][:, 2 * FW :] + one_part(ins[1][:, 2 * FW :])
    scale = lax.rsqrt(squares / D + EPSILON)[:, :1]
    for f in range(FLOWS):
        whole = (ins[2 * f][:, : 2 * FW] + ins[2 * f + 1][:, : 2 * FW].astype(F32)) * scale
        gate, up = whole[:, :FW], whole[:, FW:]
        units = (gate / (1.0 + jnp.exp(-gate)) * up).astype(BF16)
        outs[f // 2][:, (f % 2) * FW : (f % 2) * FW + FW] = units


def hidden_units(where, near, far, gain, gate, up):
    parts = gate_partial(where, near, far, gain, gate, up)
    steps = (4, 12, 1, 3)
    rows = 128
    for step in range(4):
        moved = list(parts)
        for f in range(FLOWS):
            moved[2 * f + 1] = swap_gx(parts[2 * f + 1], steps[(step + f) % 4])
        if step == 3:
            break
        rows //= 2
        outs = []
        for width in widths():
            outs += [shaped((rows, width), F32), shaped((rows, width), BF16)]
        parts = call(halve_body, tuple(outs), [VM] * (2 * FLOWS))(*moved)
    return call(hidden_body, (shaped((16, 2 * FW), BF16),) * 2, [VM] * (2 * FLOWS))(*moved)


def stack_two_body(*refs):
    ins, outs = refs[:8], refs[8:]
    for side in range(2):
        for k in range(4):
            outs[side][k * 16 : k * 16 + 16, :] = ins[4 * side + k][...]


def down_body(where, *refs):
    pieces, (weight, keep, send, lhs, held, sem) = refs[:8], refs[8:]
    half = 2 * FW
    fetches = []
    for side in range(2):
        fetch = pltpu.make_async_copy(weight.at[pl.ds(side * half, half)], held.at[side], sem.at[side])
        fetch.start()
        fetches.append(fetch)
    for side in range(2):
        for m in range(4):
            for k in range(4):
                y, z = (k, m) if side == 0 else (m, k)
                place = where[0] ^ (gray(y) * 4 + gray(z))
                block = (place >> 1) ^ where[1]
                start = (block & 1) * 128 + (block >> 1) * 32 + (place & 1) * 16
                start = pl.multiple_of(start, 16)
                lhs[side, pl.ds(start, 16), :] = pieces[4 * side + m][k * 16 : k * 16 + 16, :]
    for fetch in fetches:
        fetch.wait()
    keep[...] = jnp.dot(lhs[0, :128, :], held[0], preferred_element_type=F32) + jnp.dot(
        lhs[1, :128, :], held[1], preferred_element_type=F32
    )
    send[...] = (
        jnp.dot(lhs[0, 128:, :], held[0], preferred_element_type=F32)
        + jnp.dot(lhs[1, 128:, :], held[1], preferred_element_type=F32)
    ).astype(BF16)


def down_partial(where, units, weight):
    ups = [units[0]] + [swap_gx(units[0], 4 * k) for k in (1, 2, 3)]
    zs = [units[1]] + [swap_gx(units[1], k) for k in (1, 2, 3)]
    first, second = call(stack_two_body, (shaped((64, 2 * FW), BF16),) * 2, [VM] * 8)(*ups, *zs)
    ups = [first] + [swap_gx(first, k) for k in (1, 2, 3)]
    zs = [second] + [swap_gx(second, 4 * k) for k in (1, 2, 3)]
    return call(
        down_body,
        (shaped((128, WIDTH), F32), shaped((128, WIDTH), BF16)),
        [SM] + [VM] * 8 + [ANY],
        [
            pltpu.VMEM((2, 256, 2 * FW), BF16),
            pltpu.VMEM((2, 2 * FW, WIDTH), BF16),
            pltpu.SemaphoreType.DMA((2,)),
        ],
    )(where, *ups, *zs, weight)


def rotations(positions):
    frequency = jnp.exp(jnp.arange(HD // 2, dtype=F32) * (-2.0 / HD) * jnp.log(THETA))
    rows = []
    for t in range(2):
        angles = (positions + t).astype(F32) * frequency
        cosine, sine = jnp.cos(angles), jnp.sin(angles)
        rows += [jnp.concatenate([cosine, cosine]), jnp.concatenate([-sine, sine])]
    return jnp.stack(rows)


def per_device(
    inputs,
    positions,
    attn_gain,
    ffn_gain,
    qkv_weight,
    out_weight,
    gate_weight,
    up_weight,
    down_weight,
    k_cache,
    v_cache,
):
    gx, gy = lax.axis_index("gx"), lax.axis_index("gy")
    where = jnp.stack([gray(gx >> 2) * 4 + gray(gx & 3), gy]).astype(jnp.int32)
    angles = rotations(positions)
    residual = inputs.reshape(32, WIDTH)
    attn_gain, ffn_gain = attn_gain.reshape(1, WIDTH), ffn_gain.reshape(1, WIDTH)

    near, far = gather_gy((residual * attn_gain).astype(BF16))
    partial = qkv_partial(where, near, far, attn_gain, qkv_weight).reshape(128, 24, HD)
    received = lax.all_to_all(partial, ("gx", "gy"), 0, 0, tiled=True).reshape(NX, NY, 24, HD)
    attended, new_kv = attend(angles, received, k_cache, v_cache)
    heads = lax.all_to_all(attended.reshape(128, 16, HD), ("gx", "gy"), 0, 0, tiled=True)
    pieces = sum_over_gy(*out_partial(where, heads.reshape(128 * 16, HD), out_weight))
    after_attn, normed = call(
        residual_body, (shaped((32, WIDTH), F32), shaped((32, WIDTH), BF16)), [VM] * 6
    )(residual, ffn_gain, *pieces)

    near, far = gather_gy(normed)
    units = hidden_units(where, near, far, ffn_gain, gate_weight, up_weight)
    pieces = sum_over_gy(*down_partial(where, units, down_weight))
    outputs = call(final_body, shaped((32, WIDTH), F32), [VM] * 5)(after_attn, *pieces)
    return outputs.reshape(2, 16, WIDTH), new_kv


def solution(mesh):
    placed = (
        P(None, "gy", "gx"),
        P(("gx", "gy")),
        P("gx"),
        P("gx"),
        P("gx", "gy"),
        P("gy", "gx"),
        P("gx", "gy"),
        P("gx", "gy"),
        P("gy", "gx"),
        P(("gx", "gy"), None, None, None),
        P(("gx", "gy"), None, None, None),
    )
    return jax.shard_map(
        per_device,
        mesh=mesh,
        in_specs=placed,
        out_specs=(P(None, "gy", "gx"), P(("gx", "gy"), None, None, None)),
        check_vma=False,
    )
```

time: 592 us -> 176 us (0.30)
  blocking collectives: 309 us -> 18 us
  waiting for transfers between devices: 206 us -> 75.7 us
  starting transfers between devices: 14.9 us -> 57 us
  matrix products: 22.7 us -> 0 us
  Pallas kernels: 0 us -> 17 us
  other arithmetic: 16.2 us -> 1.61 us
  between operations: 15.4 us -> 1.54 us
    all_gather x8 -> x0, blocking collectives: 143 us -> none  [the longest x4 91.2 us: gather_rows_gx(): return lax.all_gather(block, 'gx', axis=0, tiled=True)]
    unnamed x6 -> x0, waiting for transfers between devices: 127 us -> none
    unnamed x1 -> x0, blocking collectives: 83.2 us -> none
    psum x2 -> x0, blocking collectives: 82.7 us -> none  [normalize(): squares = lax.psum(jnp.sum(residual * residual, axis=1), 'gx')]
    reduce_scatter x4 -> x0, waiting for transfers between devices: 71 us -> none  [sum_over_gy(): lax.psum_scatter(partial_term(jnp.int32(0), row_share * lax.axis_size('gy...]
    ppermute x0 -> x44, waiting for transfers between devices: none -> 59.8 us  [the longest x28 42 us: swap_gx(): return lax.ppermute(array, 'gx', [(i, i ^ bits) for i in range(NX)])]
    ppermute x0 -> x44, starting transfers between devices: none -> 46.9 us  [the longest x28 28.7 us: swap_gx(): return lax.ppermute(array, 'gx', [(i, i ^ bits) for i in range(NX)])]
    dot_general x17 -> x0, matrix products: 22.7 us -> none  [the longest x4 8.61 us: partial_term(): return jnp.dot(all_rows, matrix, preferred_element_type=jnp.float32)]
  transfers between devices with their start and end apart: 9 -> 45, of which waited for: 8 -> 28; matrix products, arithmetic and copies ran while one was open for 2% -> 0% of each run, Pallas kernels for 0% -> 0%
where the time goes in v1:
time: 176 us
  waiting for transfers between devices  75.7 us (43%)
  starting transfers between devices  57 us (32%)
  blocking collectives  18 us (10%)
  Pallas kernels  17 us (10%)
  local copies, waits for them, and re-layouts  4.84 us (3%)
    ppermute x28, waiting for transfers between devices, swap_gx(): return lax.ppermute(array, 'gx', [(i, i ^ bits) for i in range(NX)])  42 us
    ppermute x28, starting transfers between devices, swap_gx(): return lax.ppermute(array, 'gx', [(i, i ^ bits) for i in range(NX)])  28.7 us
    ppermute x16, starting transfers between devices, swap_gy(): return lax.ppermute(array, 'gy', [(i, i ^ bits) for i in range(NY)])  18.2 us
    all_to_all x1, blocking collectives, per_device(): lax.all_to_all(attended.reshape(128, 16, HD), ('gx', 'gy'), 0, 0, tiled=T...  18 us
    ppermute x16, waiting for transfers between devices, swap_gy(): return lax.ppermute(array, 'gy', [(i, i ^ bits) for i in range(NY)])  17.9 us
    all_to_all x1, waiting for transfers between devices, per_device(): lax.all_to_all(partial, ('gx', 'gy'), 0, 0, tiled=True)  15.9 us
    all_to_all x1, starting transfers between devices, per_device(): lax.all_to_all(partial, ('gx', 'gy'), 0, 0, tiled=True)  10.1 us
    pallas_call x1, Pallas kernels, gate_partial(): call(gate_body, tuple(outs), [SM, VM, VM, VM, ANY, ANY], [pltpu.VMEM((FLO...  5.15 us
  transfers between devices with their start and end apart: 45, of which 28 were waited for; matrix products, arithmetic and copies ran while one was open for 0% of the time, Pallas kernels for 0%

profile of v1, /device:TPU:0, one launch (start us, length us, event | category | flops | bytes accessed | tf_op | source)
XLA Modules:
  0.0 175.6 jit_solution(4723505280111501242)
XLA Ops:
  1.7 2.9 %collective-permute-start.2 = (bf16[32,512]{1,0:T(8,128)(2,1)S(1)}, bf16[32,512]{1,0:T(8,128)(2,1)S(1)}, u32[]{:S(2)}, u32[]{:S(2)}) collective-permute-start(bf16[32,512]{1,0:T(8,128)(2,1)S(1)} %multiply_convert_fusion.refs_0_), channel_id=1, source_target_pairs={{0,6},{1,7},{2,4},{3,5},{4,2},{5,3},{6,0},{7,1},{8,14},{9,15},{10,... | collective-permute-start | bytes 98312 | tf_op jit(solution)/shard_map/ppermute | solution.py:37
  6.8 3.1 %collective-permute-done.1.refs_2_ = bf16[32,512]{1,0:T(8,128)(2,1)S(1)} collective-permute-done((bf16[32,512]{1,0:T(8,128)(2,1)S(1)}, bf16[32,512]{1,0:T(8,128)(2,1)S(1)}, u32[]{:S(2)}, u32[]{:S(2)}) %collective-permute-start.1) | collective-permute-done | bytes 32800 | tf_op jit(solution)/shard_map/ppermute | solution.py:37
  13.4 2.3 %shard_map.123 = bf16[3072,128]{1,0:T(8,128)(2,1)} custom-call(s32[2]{0:T(128)S(1)} %pad_add_fusion.where, bf16[128,512]{1,0:T(8,128)(2,1)S(1)} %shard_map.122.near, bf16[128,512]{1,0:T(8,128)(2,1)S(1)} %collective-permute-done.3.far, f32[1,512]{1,0:T(1,128)S(1)} %bitcast.27, bf16[512,1280]{1,0:T(8,128)(2,1)S(1)} %copy-done.5), custom_call_target="tpu_custom_call" | custom-call | tf_op jit(solution)/shard_map/pallas_call | solution.py:88
  15.7 10.1 %all-to-all-start = ((bf16[128,24,128]{2,1,0:T(8,128)(2,1)}), bf16[128,24,128]{2,1,0:T(8,128)(2,1)S(1)}, u32[]{:S(2)}, u32[]{:S(2)}) async-start(bf16[128,24,128]{2,1,0:T(8,128)(2,1)} %bitcast.11), calls=%async_computation | async-start | bytes 1572864 | tf_op jit(solution)/shard_map/all_to_all | solution.py:446
  26.2 15.9 %all-to-all-done = bf16[128,24,128]{2,1,0:T(8,128)(2,1)S(1)} async-done(((bf16[128,24,128]{2,1,0:T(8,128)(2,1)}), bf16[128,24,128]{2,1,0:T(8,128)(2,1)S(1)}, u32[]{:S(2)}, u32[]{:S(2)}) %all-to-all-start) | async-done | bytes 786464 | tf_op jit(solution)/shard_map/all_to_all | solution.py:446
  43.7 4.1 %shard_map.124 = (bf16[16,8,16,128]{3,2,1,0:T(8,128)(2,1)S(1)}, bf16[1,2,8,256]{3,2,1,0:T(8,128)(2,1)}) custom-call(f32[4,128]{1,0:T(4,128)S(1)} %pad_maximum_fusion.angles, bf16[16,8,24,128]{3,2,1,0:T(8,128)(2,1)S(1)} %bitcast.21, bf16[1,8,1024,128]{3,2,1,0:T(8,128)(2,1)S(1)} %copy-done.3, bf16[1,8,1024,128]{3,2,1,0:T(8,128)(2,1)S(1)} %copy-done.4), custom_call_target="tpu_custom_call" | custom-call | tf_op jit(solution)/shard_map/pallas_call | solution.py:165
  47.8 18.0 %all_to_all.10 = bf16[128,16,128]{2,1,0:T(8,128)(2,1)S(1)} all-to-all(bf16[128,16,128]{2,1,0:T(8,128)(2,1)S(1)} %bitcast.23), channel_id=1, replica_groups=mesh['gx'=16,'gy'=8] {'gx','gy'}, dimensions={0} | all-to-all | bytes 1048576 | tf_op jit(solution)/shard_map/all_to_all | solution.py:448
  72.2 2.5 %collective-permute-start.7 = (bf16[32,512]{1,0:T(8,128)(2,1)S(1)}, bf16[32,512]{1,0:T(8,128)(2,1)S(1)}, u32[]{:S(2)}, u32[]{:S(2)}) collective-permute-start(bf16[32,512]{1,0:T(8,128)(2,1)S(1)} %get-tuple-element.60), channel_id=1, source_target_pairs={{0,6},{1,7},{2,4},{3,5},{4,2},{5,3},{6,0},{7,1},{8,14},{9,15},{10,... | collective-permute-start | bytes 98312 | tf_op jit(solution)/shard_map/ppermute | solution.py:37
  77.4 2.6 %collective-permute-start.10 = (bf16[32,512]{1,0:T(8,128)(2,1)S(1)}, bf16[32,512]{1,0:T(8,128)(2,1)S(1)}, u32[]{:S(2)}, u32[]{:S(2)}) collective-permute-start(bf16[32,512]{1,0:T(8,128)(2,1)S(1)} %get-tuple-element.62.refs_0_), channel_id=1, source_target_pairs={{0,6},{1,7},{2,4},{3,5},{4,2},{5,3},{6,0},{7,1},{8,14},{9,15},{10,... | collective-permute-start | bytes 98312 | tf_op jit(solution)/shard_map/ppermute | solution.py:37
  82.9 2.5 %collective-permute-done.9.refs_2_ = bf16[32,512]{1,0:T(8,128)(2,1)S(1)} collective-permute-done((bf16[32,512]{1,0:T(8,128)(2,1)S(1)}, bf16[32,512]{1,0:T(8,128)(2,1)S(1)}, u32[]{:S(2)}, u32[]{:S(2)}) %collective-permute-start.9) | collective-permute-done | bytes 32800 | tf_op jit(solution)/shard_map/ppermute | solution.py:37
  86.8 5.1 %shard_map.129 = (f32[128,1920]{1,0:T(8,128)S(1)}, bf16[128,1920]{1,0:T(8,128)(2,1)S(1)}, f32[128,1792]{1,0:T(8,128)S(1)}, bf16[128,1792]{1,0:T(8,128)(2,1)S(1)}...) custom-call(s32[2]{0:T(128)S(1)} %pad_add_fusion.where, ...), custom_call_target="tpu_custom_call" | custom-call | tf_op jit(solution)/shard_map/pallas_call | solution.py:306
  95.1 11.0 %collective-permute-done.13.refs_3_ = bf16[128,1792]{1,0:T(8,128)(2,1)S(1)} collective-permute-done((bf16[128,1792]{1,0:T(8,128)(2,1)S(1)}, bf16[128,1792]{1,0:T(8,128)(2,1)S(1)}, u32[]{:S(2)}, u32[]{:S(2)}) %collective-permute-start.13) | collective-permute-done | bytes 458784 | tf_op jit(solution)/shard_map/ppermute | solution.py:33
  107.8 2.3 %collective-permute-start.16 = (bf16[64,1920]{1,0:T(8,128)(2,1)S(1)}, bf16[64,1920]{1,0:T(8,128)(2,1)S(1)}, u32[]{:S(2)}, u32[]{:S(2)}) collective-permute-start(bf16[64,1920]{1,0:T(8,128)(2,1)S(1)} %get-tuple-element.72), channel_id=1, source_target_pairs={{0,96},{8,104},{16,112},{24,120},{32,64},{40,72},{48,80},{56,88},{... | collective-permute-start | bytes 737288 | tf_op jit(solution)/shard_map/ppermute | solution.py:33
  111.4 4.6 %collective-permute-done.17.refs_3_ = bf16[64,1792]{1,0:T(8,128)(2,1)S(1)} collective-permute-done((bf16[64,1792]{1,0:T(8,128)(2,1)S(1)}, bf16[64,1792]{1,0:T(8,128)(2,1)S(1)}, u32[]{:S(2)}, u32[]{:S(2)}) %collective-permute-start.17) | collective-permute-done | bytes 229408 | tf_op jit(solution)/shard_map/ppermute | solution.py:33
  118.8 2.2 %collective-permute-start.21 = (bf16[32,1792]{1,0:T(8,128)(2,1)S(1)}, bf16[32,1792]{1,0:T(8,128)(2,1)S(1)}, u32[]{:S(2)}, u32[]{:S(2)}) collective-permute-start(bf16[32,1792]{1,0:T(8,128)(2,1)S(1)} %get-tuple-element.82), channel_id=1, source_target_pairs={{0,24},{8,16},{16,8},{24,0},{32,56},{40,48},{48,40},{56,32},{64,88... | collective-permute-start | bytes 344072 | tf_op jit(solution)/shard_map/ppermute | solution.py:33
  122.3 2.5 %collective-permute-done.21.refs_3_ = bf16[32,1792]{1,0:T(8,128)(2,1)S(1)} collective-permute-done((bf16[32,1792]{1,0:T(8,128)(2,1)S(1)}, bf16[32,1792]{1,0:T(8,128)(2,1)S(1)}, u32[]{:S(2)}, u32[]{:S(2)}) %collective-permute-start.21) | collective-permute-done | bytes 114720 | tf_op jit(solution)/shard_map/ppermute | solution.py:33
  130.1 2.8 %collective-permute-done.25.refs_3_ = bf16[16,1792]{1,0:T(8,128)(2,1)S(1)} collective-permute-done((bf16[16,1792]{1,0:T(8,128)(2,1)S(1)}, bf16[16,1792]{1,0:T(8,128)(2,1)S(1)}, u32[]{:S(2)}, u32[]{:S(2)}) %collective-permute-start.25) | collective-permute-done | bytes 57376 | tf_op jit(solution)/shard_map/ppermute | solution.py:33
  139.3 2.4 %collective-permute-start.33 = (bf16[16,1792]{1,0:T(8,128)(2,1)S(1)}, bf16[16,1792]{1,0:T(8,128)(2,1)S(1)}, u32[]{:S(2)}, u32[]{:S(2)}) collective-permute-start(bf16[16,1792]{1,0:T(8,128)(2,1)S(1)} %get-tuple-element.96.refs_4_), channel_id=1, source_target_pairs={{0,24},{8,16},{16,8},{24,0},{32,56},{40,48},{48,40},{56,32},{64,88... | collective-permute-start | bytes 172040 | tf_op jit(solution)/shard_map/ppermute | solution.py:33
  143.4 3.4 %collective-permute-done.33.refs_7_ = bf16[16,1792]{1,0:T(8,128)(2,1)S(1)} collective-permute-done((bf16[16,1792]{1,0:T(8,128)(2,1)S(1)}, bf16[16,1792]{1,0:T(8,128)(2,1)S(1)}, u32[]{:S(2)}, u32[]{:S(2)}) %collective-permute-start.33) | collective-permute-done | bytes 57376 | tf_op jit(solution)/shard_map/ppermute | solution.py:33
  154.4 3.5 %collective-permute-done.36.refs_3_ = bf16[64,1792]{1,0:T(8,128)(2,1)S(1)} collective-permute-done((bf16[64,1792]{1,0:T(8,128)(2,1)S(1)}, bf16[64,1792]{1,0:T(8,128)(2,1)S(1)}, u32[]{:S(2)}, u32[]{:S(2)}) %collective-permute-start.36) | collective-permute-done | bytes 229408 | tf_op jit(solution)/shard_map/ppermute | solution.py:33
  158.8 3.2 %collective-permute-done.39.refs_7_ = bf16[64,1792]{1,0:T(8,128)(2,1)S(1)} collective-permute-done((bf16[64,1792]{1,0:T(8,128)(2,1)S(1)}, bf16[64,1792]{1,0:T(8,128)(2,1)S(1)}, u32[]{:S(2)}, u32[]{:S(2)}) %collective-permute-start.39) | collective-permute-done | bytes 229408 | tf_op jit(solution)/shard_map/ppermute | solution.py:33
  163.9 2.1 %shard_map.135 = (f32[128,512]{1,0:T(8,128)S(1)}, bf16[128,512]{1,0:T(8,128)(2,1)S(1)}) custom-call(s32[2]{0:T(128)S(1)} %pad_add_fusion.where, bf16[64,1792]{1,0:T(8,128)(2,1)S(1)} %get-tuple-element.97.refs_0_, bf16[64,1792]{1,0:T(8,128)(2,1)S(1)} %collective-permute-done.34.refs_1_, bf16[64,1792]{1,0:T(8,128)(2,1)S(1)} %collective-permute-done.35.refs_2_, ...), custom_call_target="tpu_custom_call" | custom-call | tf_op jit(solution)/shard_map/pallas_call | solution.py:403
  167.7 2.1 %collective-permute-start.42 = (bf16[32,512]{1,0:T(8,128)(2,1)S(1)}, bf16[32,512]{1,0:T(8,128)(2,1)S(1)}, u32[]{:S(2)}, u32[]{:S(2)}) collective-permute-start(bf16[32,512]{1,0:T(8,128)(2,1)S(1)} %get-tuple-element.103), channel_id=1, source_target_pairs={{0,4},{1,5},{2,6},{3,7},{4,0},{5,1},{6,2},{7,3},{8,12},{9,13},{10,... | collective-permute-start | bytes 98312 | tf_op jit(solution)/shard_map/ppermute | solution.py:37
  169.8 2.4 %collective-permute-start.43 = (bf16[32,512]{1,0:T(8,128)(2,1)S(1)}, bf16[32,512]{1,0:T(8,128)(2,1)S(1)}, u32[]{:S(2)}, u32[]{:S(2)}) collective-permute-start(bf16[32,512]{1,0:T(8,128)(2,1)S(1)} %get-tuple-element.104), channel_id=1, source_target_pairs={{0,6},{1,7},{2,4},{3,5},{4,2},{5,3},{6,0},{7,1},{8,14},{9,15},{10,... | collective-permute-start | bytes 98312 | tf_op jit(solution)/shard_map/ppermute | solution.py:37
  (114 shorter events, 60.6 us)
Async XLA Ops:
  15.7 26.4 %all-to-all-start = ((bf16[128,24,128]{2,1,0:T(8,128)(2,1)}), bf16[128,24,128]{2,1,0:T(8,128)(2,1)S(1)}, u32[]{:S(2)}, u32[]{:S(2)}) async-start(bf16[128,24,128]{2,1,0:T(8,128)(2,1)} %bitcast.11), calls=%async_computation | async-start | bytes 1572864 | tf_op jit(solution)/shard_map/all_to_all | solution.py:446
  92.0 15.2 %collective-permute-start.12 = (bf16[128,1920]{1,0:T(8,128)(2,1)S(1)}, bf16[128,1920]{1,0:T(8,128)(2,1)S(1)}, u32[]{:S(2)}, u32[]{:S(2)}) collective-permute-start(bf16[128,1920]{1,0:T(8,128)(2,1)S(1)} %get-tuple-element.64), channel_id=1, source_target_pairs={{0,32},{8,40},{16,48},{24,56},{32,0},{40,8},{48,16},{56,24},{64,96... | collective-permute-start | bytes 1474568 | tf_op jit(solution)/shard_map/ppermute | solution.py:33
  92.4 13.8 %collective-permute-start.13 = (bf16[128,1792]{1,0:T(8,128)(2,1)S(1)}, bf16[128,1792]{1,0:T(8,128)(2,1)S(1)}, u32[]{:S(2)}, u32[]{:S(2)}) collective-permute-start(bf16[128,1792]{1,0:T(8,128)(2,1)S(1)} %get-tuple-element.66), channel_id=1, source_target_pairs={{0,96},{8,104},{16,112},{24,120},{32,64},{40,72},{48,80},{56,88},{... | collective-permute-start | bytes 1376264 | tf_op jit(solution)/shard_map/ppermute | solution.py:33
  93.5 12.7 %collective-permute-start.14 = (bf16[128,1792]{1,0:T(8,128)(2,1)S(1)}, bf16[128,1792]{1,0:T(8,128)(2,1)S(1)}, u32[]{:S(2)}, u32[]{:S(2)}) collective-permute-start(bf16[128,1792]{1,0:T(8,128)(2,1)S(1)} %get-tuple-element.68), channel_id=1, source_target_pairs={{0,8},{8,0},{16,24},{24,16},{32,40},{40,32},{48,56},{56,48},{64,72... | collective-permute-start | bytes 1376264 | tf_op jit(solution)/shard_map/ppermute | solution.py:33
  93.9 13.2 %collective-permute-start.15 = (bf16[128,1792]{1,0:T(8,128)(2,1)S(1)}, bf16[128,1792]{1,0:T(8,128)(2,1)S(1)}, u32[]{:S(2)}, u32[]{:S(2)}) collective-permute-start(bf16[128,1792]{1,0:T(8,128)(2,1)S(1)} %get-tuple-element.70), channel_id=1, source_target_pairs={{0,24},{8,16},{16,8},{24,0},{32,56},{40,48},{48,40},{56,32},{64,88... | collective-permute-start | bytes 1376264 | tf_op jit(solution)/shard_map/ppermute | solution.py:33
  107.8 9.8 %collective-permute-start.16 = (bf16[64,1920]{1,0:T(8,128)(2,1)S(1)}, bf16[64,1920]{1,0:T(8,128)(2,1)S(1)}, u32[]{:S(2)}, u32[]{:S(2)}) collective-permute-start(bf16[64,1920]{1,0:T(8,128)(2,1)S(1)} %get-tuple-element.72), channel_id=1, source_target_pairs={{0,96},{8,104},{16,112},{24,120},{32,64},{40,72},{48,80},{56,88},{... | collective-permute-start | bytes 737288 | tf_op jit(solution)/shard_map/ppermute | solution.py:33
  110.1 6.0 %collective-permute-start.17 = (bf16[64,1792]{1,0:T(8,128)(2,1)S(1)}, bf16[64,1792]{1,0:T(8,128)(2,1)S(1)}, u32[]{:S(2)}, u32[]{:S(2)}) collective-permute-start(bf16[64,1792]{1,0:T(8,128)(2,1)S(1)} %get-tuple-element.74), channel_id=1, source_target_pairs={{0,8},{8,0},{16,24},{24,16},{32,40},{40,32},{48,56},{56,48},{64,72... | collective-permute-start | bytes 688136 | tf_op jit(solution)/shard_map/ppermute | solution.py:33
  110.3 7.2 %collective-permute-start.18 = (bf16[64,1792]{1,0:T(8,128)(2,1)S(1)}, bf16[64,1792]{1,0:T(8,128)(2,1)S(1)}, u32[]{:S(2)}, u32[]{:S(2)}) collective-permute-start(bf16[64,1792]{1,0:T(8,128)(2,1)S(1)} %get-tuple-element.76), channel_id=1, source_target_pairs={{0,24},{8,16},{16,8},{24,0},{32,56},{40,48},{48,40},{56,32},{64,88... | collective-permute-start | bytes 688136 | tf_op jit(solution)/shard_map/ppermute | solution.py:33
  111.2 6.3 %collective-permute-start.19 = (bf16[64,1792]{1,0:T(8,128)(2,1)S(1)}, bf16[64,1792]{1,0:T(8,128)(2,1)S(1)}, u32[]{:S(2)}, u32[]{:S(2)}) collective-permute-start(bf16[64,1792]{1,0:T(8,128)(2,1)S(1)} %get-tuple-element.78), channel_id=1, source_target_pairs={{0,32},{8,40},{16,48},{24,56},{32,0},{40,8},{48,16},{56,24},{64,96... | collective-permute-start | bytes 688136 | tf_op jit(solution)/shard_map/ppermute | solution.py:33
  117.8 9.5 %collective-permute-start.20 = (bf16[32,1920]{1,0:T(8,128)(2,1)S(1)}, bf16[32,1920]{1,0:T(8,128)(2,1)S(1)}, u32[]{:S(2)}, u32[]{:S(2)}) collective-permute-start(bf16[32,1920]{1,0:T(8,128)(2,1)S(1)} %get-tuple-element.80), channel_id=1, source_target_pairs={{0,8},{8,0},{16,24},{24,16},{32,40},{40,32},{48,56},{56,48},{64,72... | collective-permute-start | bytes 368648 | tf_op jit(solution)/shard_map/ppermute | solution.py:33
  118.8 6.0 %collective-permute-start.21 = (bf16[32,1792]{1,0:T(8,128)(2,1)S(1)}, bf16[32,1792]{1,0:T(8,128)(2,1)S(1)}, u32[]{:S(2)}, u32[]{:S(2)}) collective-permute-start(bf16[32,1792]{1,0:T(8,128)(2,1)S(1)} %get-tuple-element.82), channel_id=1, source_target_pairs={{0,24},{8,16},{16,8},{24,0},{32,56},{40,48},{48,40},{56,32},{64,88... | collective-permute-start | bytes 344072 | tf_op jit(solution)/shard_map/ppermute | solution.py:33
  121.2 6.0 %collective-permute-start.23 = (bf16[32,1792]{1,0:T(8,128)(2,1)S(1)}, bf16[32,1792]{1,0:T(8,128)(2,1)S(1)}, u32[]{:S(2)}, u32[]{:S(2)}) collective-permute-start(bf16[32,1792]{1,0:T(8,128)(2,1)S(1)} %get-tuple-element.86), channel_id=1, source_target_pairs={{0,96},{8,104},{16,112},{24,120},{32,64},{40,72},{48,80},{56,88},{... | collective-permute-start | bytes 344072 | tf_op jit(solution)/shard_map/ppermute | solution.py:33
  127.3 7.5 %collective-permute-start.24 = (bf16[16,1920]{1,0:T(8,128)(2,1)S(1)}, bf16[16,1920]{1,0:T(8,128)(2,1)S(1)}, u32[]{:S(2)}, u32[]{:S(2)}) collective-permute-start(bf16[16,1920]{1,0:T(8,128)(2,1)S(1)} %get-tuple-element.88), channel_id=1, source_target_pairs={{0,24},{8,16},{16,8},{24,0},{32,56},{40,48},{48,40},{56,32},{64,88... | collective-permute-start | bytes 184328 | tf_op jit(solution)/shard_map/ppermute | solution.py:33
  135.1 6.6 %collective-permute-start.30 = (bf16[16,1792]{1,0:T(8,128)(2,1)S(1)}, bf16[16,1792]{1,0:T(8,128)(2,1)S(1)}, u32[]{:S(2)}, u32[]{:S(2)}) collective-permute-start(bf16[16,1792]{1,0:T(8,128)(2,1)S(1)} %get-tuple-element.95.refs_0_), channel_id=1, source_target_pairs={{0,96},{8,104},{16,112},{24,120},{32,64},{40,72},{48,80},{56,88},{... | collective-permute-start | bytes 172040 | tf_op jit(solution)/shard_map/ppermute | solution.py:33
  136.8 6.6 %collective-permute-start.29 = (bf16[16,1792]{1,0:T(8,128)(2,1)S(1)}, bf16[16,1792]{1,0:T(8,128)(2,1)S(1)}, u32[]{:S(2)}, u32[]{:S(2)}) collective-permute-start(bf16[16,1792]{1,0:T(8,128)(2,1)S(1)} %get-tuple-element.95.refs_0_), channel_id=1, source_target_pairs={{0,64},{8,72},{16,80},{24,88},{32,96},{40,104},{48,112},{56,120},{... | collective-permute-start | bytes 172040 | tf_op jit(solution)/shard_map/ppermute | solution.py:33
  139.3 7.5 %collective-permute-start.33 = (bf16[16,1792]{1,0:T(8,128)(2,1)S(1)}, bf16[16,1792]{1,0:T(8,128)(2,1)S(1)}, u32[]{:S(2)}, u32[]{:S(2)}) collective-permute-start(bf16[16,1792]{1,0:T(8,128)(2,1)S(1)} %get-tuple-element.96.refs_4_), channel_id=1, source_target_pairs={{0,24},{8,16},{16,8},{24,0},{32,56},{40,48},{48,40},{56,32},{64,88... | collective-permute-start | bytes 172040 | tf_op jit(solution)/shard_map/ppermute | solution.py:33
  141.7 6.4 %collective-permute-start.32 = (bf16[16,1792]{1,0:T(8,128)(2,1)S(1)}, bf16[16,1792]{1,0:T(8,128)(2,1)S(1)}, u32[]{:S(2)}, u32[]{:S(2)}) collective-permute-start(bf16[16,1792]{1,0:T(8,128)(2,1)S(1)} %get-tuple-element.96.refs_4_), channel_id=1, source_target_pairs={{0,16},{8,24},{16,0},{24,8},{32,48},{40,56},{48,32},{56,40},{64,80... | collective-permute-start | bytes 172040 | tf_op jit(solution)/shard_map/ppermute | solution.py:33
  141.7 6.4 %collective-permute-start.31 = (bf16[16,1792]{1,0:T(8,128)(2,1)S(1)}, bf16[16,1792]{1,0:T(8,128)(2,1)S(1)}, u32[]{:S(2)}, u32[]{:S(2)}) collective-permute-start(bf16[16,1792]{1,0:T(8,128)(2,1)S(1)} %get-tuple-element.96.refs_4_), channel_id=1, source_target_pairs={{0,8},{8,0},{16,24},{24,16},{32,40},{40,32},{48,56},{56,48},{64,72... | collective-permute-start | bytes 172040 | tf_op jit(solution)/shard_map/ppermute | solution.py:33
  148.1 9.8 %collective-permute-start.36 = (bf16[64,1792]{1,0:T(8,128)(2,1)S(1)}, bf16[64,1792]{1,0:T(8,128)(2,1)S(1)}, u32[]{:S(2)}, u32[]{:S(2)}) collective-permute-start(bf16[64,1792]{1,0:T(8,128)(2,1)S(1)} %get-tuple-element.97.refs_0_), channel_id=1, source_target_pairs={{0,24},{8,16},{16,8},{24,0},{32,56},{40,48},{48,40},{56,32},{64,88... | collective-permute-start | bytes 688136 | tf_op jit(solution)/shard_map/ppermute | solution.py:33
  149.8 8.2 %collective-permute-start.35 = (bf16[64,1792]{1,0:T(8,128)(2,1)S(1)}, bf16[64,1792]{1,0:T(8,128)(2,1)S(1)}, u32[]{:S(2)}, u32[]{:S(2)}) collective-permute-start(bf16[64,1792]{1,0:T(8,128)(2,1)S(1)} %get-tuple-element.97.refs_0_), channel_id=1, source_target_pairs={{0,16},{8,24},{16,0},{24,8},{32,48},{40,56},{48,32},{56,40},{64,80... | collective-permute-start | bytes 688136 | tf_op jit(solution)/shard_map/ppermute | solution.py:33
  150.4 8.4 %collective-permute-start.34 = (bf16[64,1792]{1,0:T(8,128)(2,1)S(1)}, bf16[64,1792]{1,0:T(8,128)(2,1)S(1)}, u32[]{:S(2)}, u32[]{:S(2)}) collective-permute-start(bf16[64,1792]{1,0:T(8,128)(2,1)S(1)} %get-tuple-element.97.refs_0_), channel_id=1, source_target_pairs={{0,8},{8,0},{16,24},{24,16},{32,40},{40,32},{48,56},{56,48},{64,72... | collective-permute-start | bytes 688136 | tf_op jit(solution)/shard_map/ppermute | solution.py:33
  152.3 9.7 %collective-permute-start.39 = (bf16[64,1792]{1,0:T(8,128)(2,1)S(1)}, bf16[64,1792]{1,0:T(8,128)(2,1)S(1)}, u32[]{:S(2)}, u32[]{:S(2)}) collective-permute-start(bf16[64,1792]{1,0:T(8,128)(2,1)S(1)} %get-tuple-element.98.refs_4_), channel_id=1, source_target_pairs={{0,96},{8,104},{16,112},{24,120},{32,64},{40,72},{48,80},{56,88},{... | collective-permute-start | bytes 688136 | tf_op jit(solution)/shard_map/ppermute | solution.py:33
  154.3 7.7 %collective-permute-start.38 = (bf16[64,1792]{1,0:T(8,128)(2,1)S(1)}, bf16[64,1792]{1,0:T(8,128)(2,1)S(1)}, u32[]{:S(2)}, u32[]{:S(2)}) collective-permute-start(bf16[64,1792]{1,0:T(8,128)(2,1)S(1)} %get-tuple-element.98.refs_4_), channel_id=1, source_target_pairs={{0,64},{8,72},{16,80},{24,88},{32,96},{40,104},{48,112},{56,120},{... | collective-permute-start | bytes 688136 | tf_op jit(solution)/shard_map/ppermute | solution.py:33
  157.9 6.0 %collective-permute-start.37 = (bf16[64,1792]{1,0:T(8,128)(2,1)S(1)}, bf16[64,1792]{1,0:T(8,128)(2,1)S(1)}, u32[]{:S(2)}, u32[]{:S(2)}) collective-permute-start(bf16[64,1792]{1,0:T(8,128)(2,1)S(1)} %get-tuple-element.98.refs_4_), channel_id=1, source_target_pairs={{0,32},{8,40},{16,48},{24,56},{32,0},{40,8},{48,16},{56,24},{64,96... | collective-permute-start | bytes 688136 | tf_op jit(solution)/shard_map/ppermute | solution.py:33
  (31 other events, 405.9 us)

commit v2 on v1

v2 whole, which is shorter than its diff:
```python
import functools

import jax
import jax.numpy as jnp
from jax import lax
from jax.experimental import pallas as pl
from jax.experimental.pallas import tpu as pltpu
from jax.sharding import PartitionSpec as P

D = 8192
KVH = 8
HD = 128
CACHE = 1024
GQ = 8
EPSILON = 1e-05
THETA = 500000.0
NX = 16
NY = 8
WIDTH = 512
UNITS = 3584
HALF = UNITS // 2
WIDTHS = (2 * HALF + HD, 2 * HALF)
F32 = jnp.float32
BF16 = jnp.bfloat16
MIB = 1 << 20

VM = pl.BlockSpec(memory_space=pltpu.VMEM)
SM = pl.BlockSpec(memory_space=pltpu.SMEM)
HBM = pl.BlockSpec(memory_space=pltpu.HBM)
DMA = pltpu.SemaphoreType.DMA


def swap_gx(array, bits):
    return lax.ppermute(array, "gx", [(i, i ^ bits) for i in range(NX)])


def swap_gy(array, bits):
    return lax.ppermute(array, "gy", [(i, i ^ bits) for i in range(NY)])


def gray(place):
    return ((place & 1) ^ (place >> 1)) * 2 + (place >> 1)


def call(body, outs, ins, scratch=(), limit=32):
    return pl.pallas_call(
        body,
        out_shape=outs,
        in_specs=ins,
        out_specs=jax.tree.map(lambda _: VM, outs),
        scratch_shapes=list(scratch),
        compiler_params=pltpu.CompilerParams(vmem_limit_bytes=limit * MIB),
    )


def hbm(array):
    return pltpu.with_memory_space_constraint(array, pltpu.HBM)


def shaped(shape, dtype):
    return jax.ShapeDtypeStruct(shape, dtype)


def qkv_body(where, near, far, gain, weight, out, lhs, rows, held, sem):
    fetch = pltpu.make_async_copy(weight, held, sem)
    fetch.start()
    mine = where[1]
    for flag, source in enumerate((near, far)):
        for k in range(4):
            block = mine ^ (2 * k + flag)
            for t in range(2):
                start = pl.multiple_of(t * 128 + block * 16, 16)
                lhs[pl.ds(start, 16), :] = source[k * 32 + t * 16 : k * 32 + t * 16 + 16, :]
    plain = lhs[...].astype(F32) / gain[...]
    squares = jnp.sum(plain * plain, axis=1, keepdims=True)
    for t in range(2):
        whole = jnp.broadcast_to(squares[t * 128 : t * 128 + 128], (128, HD))
        high = whole.astype(BF16).astype(F32)
        rows[pl.ds(20 + 2 * t, 128, stride=24), :] = high
        rows[pl.ds(21 + 2 * t, 128, stride=24), :] = whole - high
    fetch.wait()
    for pair in range(5):
        part = jnp.dot(lhs[...], held[:, pair * 256 : pair * 256 + 256], preferred_element_type=F32)
        for j in (2 * pair, 2 * pair + 1):
            for t in range(2):
                place = t * 8 + j if j < GQ else 16 + (j - GQ) * 2 + t
                column = (j - 2 * pair) * HD
                rows[pl.ds(place, 128, stride=24), :] = part[t * 128 : t * 128 + 128, column : column + HD]
    out[...] = rows[...].astype(BF16)


def qkv_partial(where, near, far, gain, weight):
    return call(
        qkv_body,
        shaped((128 * 24, HD), BF16),
        [SM, VM, VM, VM, HBM],
        [
            pltpu.VMEM((256, WIDTH), BF16),
            pltpu.VMEM((128 * 24, HD), F32),
            pltpu.VMEM((WIDTH, 1280), BF16),
            DMA,
        ],
    )(where, near, far, gain, hbm(weight))


def turn(vectors, cosine, sine):
    return vectors * cosine + pltpu.roll(vectors, HD // 2, vectors.ndim - 1) * sine


def attend_body(angles, received, keys, values, out, fresh, scores, held, sem):
    fetch = pltpu.make_async_copy(values, held, sem)
    fetch.start()
    total = received[0].astype(F32)
    for i in range(1, NX):
        total = total + received[i].astype(F32)
    squares = total[:, 20:24, :]
    scales = []
    for t in range(2):
        square = squares[:, 2 * t : 2 * t + 1, :] + squares[:, 2 * t + 1 : 2 * t + 2, :]
        scales.append(lax.rsqrt(square / D + EPSILON))
    cosines = [angles[2 * t : 2 * t + 1, :] for t in range(2)]
    sines = [angles[2 * t + 1 : 2 * t + 2, :] for t in range(2)]
    queries, new_keys, new_values = [], [], []
    for t in range(2):
        head = (total[:, 8 * t : 8 * t + 8, :] * scales[t]).astype(BF16).astype(F32)
        flat = turn(head.reshape(64, HD), cosines[t], sines[t])
        queries.append((flat * HD**-0.5).astype(BF16).astype(F32).reshape(8, 8, HD))
        key = (total[:, 16 + t : 17 + t, :] * scales[t]).astype(BF16).astype(F32).reshape(8, HD)
        new_keys.append(turn(key, cosines[t], sines[t]).astype(BF16))
        value = (total[:, 18 + t : 19 + t, :] * scales[t]).astype(BF16).reshape(8, HD)
        new_values.append(value)
        fresh[0, t, :, :HD] = new_keys[t]
        fresh[0, t, :, HD:] = value
    both = jnp.concatenate(queries, axis=1)
    both16 = both.astype(BF16)
    for g in range(KVH):
        scores[g * 16 : g * 16 + 16, :] = lax.dot_general(
            both16[g], keys[0, g], (((1,), (1,)), ((), ())), preferred_element_type=F32
        )
    extra = []
    step = lax.broadcasted_iota(jnp.int32, (KVH, 16, 1), 1) // GQ
    for t in range(2):
        dots = jnp.sum(both * new_keys[t].astype(F32).reshape(KVH, 1, HD), axis=2, keepdims=True)
        if t == 1:
            dots = jnp.where(step >= 1, dots, -3.0e38)
        extra.append(dots.reshape(128, 1))
    cached = scores[...]
    top = jnp.maximum(jnp.max(cached, axis=1, keepdims=True), jnp.maximum(extra[0], extra[1]))
    cached = jnp.exp(cached - top)
    extra = [jnp.exp(value - top) for value in extra]
    share = 1.0 / (jnp.sum(cached, axis=1, keepdims=True) + extra[0] + extra[1])
    probs = (cached * share).astype(BF16)
    extra = [(value * share).astype(BF16).astype(F32).reshape(KVH, 16, 1) for value in extra]
    fetch.wait()
    for g in range(KVH):
        mixed = jnp.dot(probs[g * 16 : g * 16 + 16, :], held[0, g], preferred_element_type=F32)
        for t in range(2):
            mixed = mixed + extra[t][g] * new_values[t][g : g + 1, :].astype(F32)
        mixed = mixed.astype(BF16)
        for i in range(NX):
            out[i, g] = mixed


def attend(angles, received, keys, values):
    return call(
        attend_body,
        (shaped((NX, KVH, 16, HD), BF16), shaped((1, 2, KVH, 2 * HD), BF16)),
        [VM, VM, VM, HBM],
        [pltpu.VMEM((KVH * 16, CACHE), F32), pltpu.VMEM((1, KVH, CACHE, HD), BF16), DMA],
    )(angles, received, keys, hbm(values))


def out_body(where, received, weight, keep, send, wide, lhs, held, sem):
    fetch = pltpu.make_async_copy(weight, held, sem)
    fetch.start()
    mine = where[1]
    wide[...] = received[...].astype(F32)
    for flag in range(2):
        for k in range(4):
            block = mine ^ (2 * k + flag)
            for t in range(2):
                place = flag * 128 + k * 32 + t * 16
                for h in range(GQ):
                    start = block * 256 + t * 8 + h
                    lhs[place : place + 16, h * HD : h * HD + HD] = wide[
                        pl.ds(start, 16, stride=16), :
                    ].astype(BF16)
    fetch.wait()
    send[...] = jnp.dot(lhs[128:, :], held[...], preferred_element_type=F32).astype(BF16)
    keep[...] = jnp.dot(lhs[:128, :], held[...], preferred_element_type=F32)


def out_partial(where, received, weight):
    return call(
        out_body,
        (shaped((128, WIDTH), F32), shaped((128, WIDTH), BF16)),
        [SM, VM, HBM],
        [
            pltpu.VMEM((128 * 16, HD), F32),
            pltpu.VMEM((256, KVH * HD), BF16),
            pltpu.VMEM((KVH * HD, WIDTH), BF16),
            DMA,
        ],
    )(where, received, hbm(weight))


def add_body(turned, whole, other, total, send):
    for k in range(4):
        rows, theirs = slice(k * 32, k * 32 + 32), slice((k ^ turned) * 32, (k ^ turned) * 32 + 32)
        part = whole[rows, :] + other[theirs, :].astype(F32)
        total[rows, :] = part
        send[rows, :] = part.astype(BF16)


def residual_body(residual, gain, whole, other, after, normed):
    for k in range(4):
        rows, theirs = slice(k * 32, k * 32 + 32), slice((k ^ 3) * 32, (k ^ 3) * 32 + 32)
        part = residual[rows, :] + whole[rows, :] + other[theirs, :].astype(F32)
        normed[rows, :] = (part * gain[...]).astype(BF16)
        if k == 0:
            after[...] = part


def add_attention(residual, gain, keep, send):
    halves = (shaped((128, WIDTH), F32), shaped((128, WIDTH), BF16))
    whole, sent = call(functools.partial(add_body, 0), halves, [VM] * 2)(keep, swap_gy(send, 1))
    whole, sent = call(functools.partial(add_body, 1), halves, [VM] * 2)(whole, swap_gy(sent, 2))
    after, near = call(
        residual_body, (shaped((32, WIDTH), F32), shaped((128, WIDTH), BF16)), [VM] * 4
    )(residual, gain, whole, swap_gy(sent, 6))
    return after, near, swap_gy(near, 1)


def split_body(keep, other, own, *sends):
    whole = keep[...] + other[...].astype(F32)
    own[...] = whole[:32]
    for k, send in enumerate(sends):
        send[...] = whole[32 * k + 32 : 32 * k + 64].astype(BF16)


def final_body(residual, own, one, two, three, out):
    out[...] = residual[...] + (own[...] + one[...].astype(F32) + two[...].astype(F32) + three[...].astype(F32))


def add_ffn(after, keep, send):
    own, *sends = call(
        split_body,
        (shaped((32, WIDTH), F32),) + (shaped((32, WIDTH), BF16),) * 3,
        [VM, VM],
    )(keep, swap_gy(send, 1))
    pieces = [swap_gy(piece, 2 * (k + 1)) for k, piece in enumerate(sends)]
    return call(final_body, shaped((32, WIDTH), F32), [VM] * 5)(after, own, *pieces)


def rows_body(own, one, two, three, gain, residual, scaled):
    for k, piece in enumerate((own, one, two, three)):
        rows = slice(k * 32, k * 32 + 32)
        residual[rows, :] = piece[...]
        scaled[rows, :] = (piece[...] * gain[...]).astype(BF16)


def gather_rows(own, gain):
    pieces = [own] + [swap_gy(own, 2 * k) for k in (1, 2, 3)]
    residual, near = call(
        rows_body, (shaped((128, WIDTH), F32), shaped((128, WIDTH), BF16)), [VM] * 5
    )(*pieces, gain)
    return residual, near, swap_gy(near, 1)


def two_parts(squares):
    high = squares.astype(BF16).astype(F32)
    first = lax.broadcasted_iota(jnp.int32, squares.shape, 1) < HD // 2
    return jnp.where(first, high, squares - high).astype(BF16)


def one_part(parts):
    wide = parts.astype(F32)
    return wide + pltpu.roll(wide, HD // 2, 1)


def swap_by_core(array, first, second):
    pairs = []
    for i in range(NX):
        for j in range(NY):
            pairs.append((i * NY + j, (i ^ (second if j & 1 else first)) * NY + j))
    return lax.ppermute(array, ("gx", "gy"), pairs)


def place_of(flow, core, chunk):
    turned = jnp.where(core == 0, chunk, ((chunk << 2) | (chunk >> 2)) & 15)
    if flow == 1:
        turned = (turned & 3) | ((turned & 4) << 1) | ((turned & 8) >> 1)
    return turned


def gate_body(send, where, near, far, gain, gate, up, *refs):
    outs, lhs = refs[:2], refs[2]
    core = where[1] & 1
    for f in range(2):
        for flag, source in enumerate((near, far)):
            for k in range(4):
                block = where[1] ^ (2 * k + flag)
                for t in range(2):
                    place = place_of(f, core, (2 * block + t) ^ where[0])
                    start = pl.multiple_of(place * 16, 16)
                    lhs[f, pl.ds(start, 16), :] = source[k * 32 + t * 16 : k * 32 + t * 16 + 16, :]
    rows = slice(128, 256) if send else slice(0, 128)
    plain = lhs[0, rows, :].astype(F32) / gain[...]
    squares = jnp.broadcast_to(jnp.sum(plain * plain, axis=1, keepdims=True), (128, HD))
    outs[0][:, 2 * HALF :] = two_parts(squares) if send else squares
    for f in range(2):
        for i, weight in enumerate((gate, up)):
            part = jnp.dot(lhs[f, rows, :], weight[:, f * HALF : f * HALF + HALF], preferred_element_type=F32)
            outs[f][:, i * HALF : i * HALF + HALF] = part.astype(outs[f].dtype)


def gate_partial(send, *args):
    return call(
        functools.partial(gate_body, send),
        tuple(shaped((128, width), BF16 if send else F32) for width in WIDTHS),
        [SM] + [VM] * 5,
        [pltpu.VMEM((2, 256, WIDTH), BF16)],
    )(*args)


def halve_body(*refs):
    ins, outs = refs[:4], refs[4:]
    for f in range(2):
        keep, other = ins[2 * f], ins[2 * f + 1]
        whole = keep[:, : 2 * HALF] + other[:, : 2 * HALF].astype(F32)
        outs[2 * f][:, : 2 * HALF] = whole[:64]
        outs[2 * f + 1][:, : 2 * HALF] = whole[64:].astype(BF16)
        if f == 0:
            squares = keep[:, 2 * HALF :] + one_part(other[:, 2 * HALF :])
            outs[0][:, 2 * HALF :] = squares[:64]
            outs[1][:, 2 * HALF :] = two_parts(squares[64:])


def quarter_body(*refs):
    ins, outs = refs[:4], refs[4:]
    start = 0
    for f in range(2):
        keep, other = ins[2 * f], ins[2 * f + 1]
        whole = keep[:, : 2 * HALF] + other[:, : 2 * HALF].astype(F32)
        for k, out in enumerate(outs):
            rows = slice(gray(k) * 16, gray(k) * 16 + 16)
            out[:, start : start + 2 * HALF] = whole[rows].astype(out.dtype)
        if f == 0:
            squares = keep[:, 2 * HALF :] + one_part(other[:, 2 * HALF :])
            for k, out in enumerate(outs):
                part = squares[gray(k) * 16 : gray(k) * 16 + 16]
                out[:, 4 * HALF :] = part if k == 0 else two_parts(part)
        start += 2 * HALF


def hidden_body(own, one, two, three, out):
    others = (one, two, three)
    squares = own[:, 4 * HALF :] + sum(one_part(other[:, 4 * HALF :]) for other in others)
    scale = lax.rsqrt(squares / D + EPSILON)[:, :1]
    for f in range(2):
        gate, up = (
            (own[:, columns] + sum(other[:, columns].astype(F32) for other in others)) * scale
            for columns in (slice(i * HALF, i * HALF + HALF) for i in (2 * f, 2 * f + 1))
        )
        out[:, f * HALF : f * HALF + HALF] = (gate / (1.0 + jnp.exp(-gate)) * up).astype(BF16)


def hidden_units(*args):
    sends = gate_partial(True, *args)
    moved = [swap_by_core(sends[0], 4, 1), swap_by_core(sends[1], 12, 3)]
    keeps = gate_partial(False, *args)
    halves = []
    for width in WIDTHS:
        halves += [shaped((64, width), F32), shaped((64, width), BF16)]
    parts = call(halve_body, tuple(halves), [VM] * 4)(keeps[0], moved[0], keeps[1], moved[1])
    moved = [swap_by_core(parts[1], 12, 3), swap_by_core(parts[3], 4, 1)]
    wide = 4 * HALF + HD
    own, *sends = call(
        quarter_body, (shaped((16, wide), F32),) + (shaped((16, wide), BF16),) * 3, [VM] * 4
    )(parts[0], moved[0], parts[2], moved[1])
    moved = [swap_by_core(part, k, 4 * k) for k, part in zip((1, 2, 3), sends)]
    return call(hidden_body, shaped((16, UNITS), BF16), [VM] * 4)(own, *moved)


def stack_body(*refs):
    *pieces, out = refs
    rows = pieces[0].shape[0]
    for k, piece in enumerate(pieces):
        out[k * rows : k * rows + rows, :] = piece[...]


def down_body(where, *refs):
    pieces, (weight, keep, send, lhs) = refs[:4], refs[4:]
    core = where[1] & 1
    for m in range(4):
        for k in range(4):
            step = jnp.where(core == 0, gray(m) * 4 + gray(k), gray(k) * 4 + gray(m))
            place = where[0] ^ step
            block = (place >> 1) ^ where[1]
            start = (block & 1) * 128 + (block >> 1) * 32 + (place & 1) * 16
            lhs[pl.ds(pl.multiple_of(start, 16), 16), :] = pieces[m][k * 16 : k * 16 + 16, :]
    send[...] = jnp.dot(lhs[128:, :], weight[...], preferred_element_type=F32).astype(BF16)
    keep[...] = jnp.dot(lhs[:128, :], weight[...], preferred_element_type=F32)


def down_partial(where, units, weight):
    pieces = [units] + [swap_by_core(units, k, 4 * k) for k in (1, 2, 3)]
    near = call(stack_body, shaped((64, UNITS), BF16), [VM] * 4)(*pieces)
    pieces = [near] + [swap_by_core(near, 4 * k, k) for k in (1, 2, 3)]
    return call(
        down_body,
        (shaped((128, WIDTH), F32), shaped((128, WIDTH), BF16)),
        [SM] + [VM] * 5,
        [pltpu.VMEM((256, UNITS), BF16)],
    )(where, *pieces, weight)


def rotations(positions):
    frequency = jnp.exp(jnp.arange(HD // 2, dtype=F32) * (-2.0 / HD) * jnp.log(THETA))
    rows = []
    for t in range(2):
        angles = (positions + t).astype(F32) * frequency
        cosine, sine = jnp.cos(angles), jnp.sin(angles)
        rows += [jnp.concatenate([cosine, cosine]), jnp.concatenate([-sine, sine])]
    return jnp.stack(rows)


def per_device(
    inputs,
    positions,
    attn_gain,
    ffn_gain,
    qkv_weight,
    out_weight,
    gate_weight,
    up_weight,
    down_weight,
    k_cache,
    v_cache,
):
    gx, gy = lax.axis_index("gx"), lax.axis_index("gy")
    where = jnp.stack([gray(gx >> 2) * 4 + gray(gx & 3), gy]).astype(jnp.int32)
    angles = rotations(positions)
    attn_gain, ffn_gain = attn_gain.reshape(1, WIDTH), ffn_gain.reshape(1, WIDTH)

    residual, near, far = gather_rows(inputs.reshape(32, WIDTH), attn_gain)
    partial = qkv_partial(where, near, far, attn_gain, qkv_weight).reshape(128, 24, HD)
    received = lax.all_to_all(partial, ("gx", "gy"), 0, 0, tiled=True).reshape(NX, NY, 24, HD)
    attended, new_kv = attend(angles, received, k_cache, v_cache)
    heads = lax.all_to_all(attended.reshape(128, 16, HD), ("gx", "gy"), 0, 0, tiled=True)
    keep, send = out_partial(where, heads.reshape(128 * 16, HD), out_weight)
    after_attn, near, far = add_attention(residual, ffn_gain, keep, send)

    units = hidden_units(where, near, far, ffn_gain, gate_weight, up_weight)
    outputs = add_ffn(after_attn, *down_partial(where, units, down_weight))
    return outputs.reshape(2, 16, WIDTH), new_kv


def solution(mesh):
    placed = (
        P(None, "gy", "gx"),
        P(("gx", "gy")),
        P("gx"),
        P("gx"),
        P("gx", "gy"),
        P("gy", "gx"),
        P("gx", "gy"),
        P("gx", "gy"),
        P("gy", "gx"),
        P(("gx", "gy"), None, None, None),
        P(("gx", "gy"), None, None, None),
    )
    return jax.shard_map(
        per_device,
        mesh=mesh,
        in_specs=placed,
        out_specs=(P(None, "gy", "gx"), P(("gx", "gy"), None, None, None)),
        check_vma=False,
    )
```

time: 176 us -> 156 us (0.89)
  starting transfers between devices: 57 us -> 36.6 us
  waiting for transfers between devices: 75.7 us -> 81.7 us
  local copies, waits for them, and re-layouts: 4.84 us -> 1.54 us
    ppermute x28 -> x13, starting transfers between devices: 28.7 us -> 15.7 us  [swap_by_core(): return lax.ppermute(array, ('gx', 'gy'), pairs)]
    ppermute x16 -> x12, starting transfers between devices: 18.2 us -> 10.8 us  [swap_gy(): return lax.ppermute(array, 'gy', [(i, i ^ bits) for i in range(NY)])]
    ppermute x16 -> x12, waiting for transfers between devices: 17.9 us -> 22.6 us  [swap_gy(): return lax.ppermute(array, 'gy', [(i, i ^ bits) for i in range(NY)])]
    unnamed x20 -> x14, local copies, waits for them, and re-layouts: 4.84 us -> 1.54 us
    ppermute x28 -> x13, waiting for transfers between devices: 42 us -> 43.2 us  [swap_by_core(): return lax.ppermute(array, ('gx', 'gy'), pairs)]
  transfers between devices with their start and end apart: 45 -> 26, of which waited for: 28 -> 21; matrix products, arithmetic and copies ran while one was open for 0% -> 0% of each run, Pallas kernels for 0% -> 1%
where the time goes in v2:
time: 156 us
  waiting for transfers between devices  81.7 us (52%)
  starting transfers between devices  36.6 us (23%)
  blocking collectives  18 us (12%)
  Pallas kernels  16 us (10%)
    ppermute x13, waiting for transfers between devices, swap_by_core(): return lax.ppermute(array, ('gx', 'gy'), pairs)  43.2 us
    ppermute x12, waiting for transfers between devices, swap_gy(): return lax.ppermute(array, 'gy', [(i, i ^ bits) for i in range(NY)])  22.6 us
    all_to_all x1, blocking collectives, per_device(): lax.all_to_all(attended.reshape(128, 16, HD), ('gx', 'gy'), 0, 0, tiled=T...  18 us
    all_to_all x1, waiting for transfers between devices, per_device(): lax.all_to_all(partial, ('gx', 'gy'), 0, 0, tiled=True)  15.9 us
    ppermute x13, starting transfers between devices, swap_by_core(): return lax.ppermute(array, ('gx', 'gy'), pairs)  15.7 us
    ppermute x12, starting transfers between devices, swap_gy(): return lax.ppermute(array, 'gy', [(i, i ^ bits) for i in range(NY)])  10.8 us
    all_to_all x1, starting transfers between devices, per_device(): lax.all_to_all(partial, ('gx', 'gy'), 0, 0, tiled=True)  10.1 us
    pallas_call x2, Pallas kernels, gate_partial(): call(functools.partial(gate_body, send), tuple((shaped((128, width), BF16...  3.49 us
  transfers between devices with their start and end apart: 26, of which 21 were waited for; matrix products, arithmetic and copies ran while one was open for 0% of the time, Pallas kernels for 1%

profile of v2, /device:TPU:0, one launch (start us, length us, event | category | flops | bytes accessed | tf_op | source)
XLA Modules:
  0.0 155.8 jit_solution(17143401958178710986)
XLA Ops:
  0.6 2.9 %collective-permute-start.2 = (f32[32,512]{1,0:T(8,128)}, f32[32,512]{1,0:T(8,128)S(1)}, u32[]{:S(2)}, u32[]{:S(2)}) collective-permute-start(f32[32,512]{1,0:T(8,128)} %bitcast.23), channel_id=1, source_target_pairs={{0,6},{1,7},{2,4},{3,5},{4,2},{5,3},{6,0},{7,1},{8,14},{9,15},{10,... | collective-permute-start | bytes 196616 | tf_op jit(solution)/shard_map/ppermute | solution.py:38
  6.4 3.1 %collective-permute-done.1.two = f32[32,512]{1,0:T(8,128)S(1)} collective-permute-done((f32[32,512]{1,0:T(8,128)}, f32[32,512]{1,0:T(8,128)S(1)}, u32[]{:S(2)}, u32[]{:S(2)}) %collective-permute-start.1) | collective-permute-done | bytes 65568 | tf_op jit(solution)/shard_map/ppermute | solution.py:38
  12.5 3.4 %shard_map.123 = bf16[3072,128]{1,0:T(8,128)(2,1)} custom-call(s32[2]{0:T(128)S(1)} %pad_add_fusion.where, bf16[128,512]{1,0:T(8,128)(2,1)S(1)} %get-tuple-element.33.near, bf16[128,512]{1,0:T(8,128)(2,1)S(1)} %collective-permute-done.3.far, f32[1,512]{1,0:T(1,128)S(1)} %bitcast.31, bf16[512,1280]{1,0:T(8,128)(2,1)} %weight.2), custom_call_target="tpu_custom_call" | custom-call | tf_op jit(solution)/shard_map/pallas_call | solution.py:93
  15.9 10.1 %all-to-all-start = ((bf16[128,24,128]{2,1,0:T(8,128)(2,1)}), bf16[128,24,128]{2,1,0:T(8,128)(2,1)S(1)}, u32[]{:S(2)}, u32[]{:S(2)}) async-start(bf16[128,24,128]{2,1,0:T(8,128)(2,1)} %bitcast.11), calls=%async_computation | async-start | bytes 1572864 | tf_op jit(solution)/shard_map/all_to_all | solution.py:448
  26.4 15.9 %all-to-all-done = bf16[128,24,128]{2,1,0:T(8,128)(2,1)S(1)} async-done(((bf16[128,24,128]{2,1,0:T(8,128)(2,1)}), bf16[128,24,128]{2,1,0:T(8,128)(2,1)S(1)}, u32[]{:S(2)}, u32[]{:S(2)}) %all-to-all-start) | async-done | bytes 786464 | tf_op jit(solution)/shard_map/all_to_all | solution.py:448
  42.3 3.2 %shard_map.124 = (bf16[16,8,16,128]{3,2,1,0:T(8,128)(2,1)S(1)}, bf16[1,2,8,256]{3,2,1,0:T(8,128)(2,1)}) custom-call(f32[4,128]{1,0:T(4,128)S(1)} %pad_maximum_fusion.angles, bf16[16,8,24,128]{3,2,1,0:T(8,128)(2,1)S(1)} %bitcast.20, bf16[1,8,1024,128]{3,2,1,0:T(8,128)(2,1)S(1)} %copy-done.3, bf16[1,8,1024,128]{3,2,1,0:T(8,128)(2,1)} %values.1), custom_call_target="tpu_custom_call" | custom-call | tf_op jit(solution)/shard_map/pallas_call | solution.py:165
  45.5 18.0 %all_to_all.10 = bf16[128,16,128]{2,1,0:T(8,128)(2,1)S(1)} all-to-all(bf16[128,16,128]{2,1,0:T(8,128)(2,1)S(1)} %bitcast.22), channel_id=1, replica_groups=mesh['gx'=16,'gy'=8] {'gx','gy'}, dimensions={0} | all-to-all | bytes 1048576 | tf_op jit(solution)/shard_map/all_to_all | solution.py:450
  63.5 2.2 %shard_map.125 = (f32[128,512]{1,0:T(8,128)S(1)}, bf16[128,512]{1,0:T(8,128)(2,1)S(1)}) custom-call(s32[2]{0:T(128)S(1)} %pad_add_fusion.where, bf16[2048,128]{1,0:T(8,128)(2,1)S(1)} %bitcast.21, bf16[1024,512]{1,0:T(8,128)(2,1)} %weight.3), custom_call_target="tpu_custom_call" | custom-call | tf_op jit(solution)/shard_map/pallas_call | solution.py:194
  67.8 5.0 %collective-permute-done.5.other = bf16[128,512]{1,0:T(8,128)(2,1)S(1)} collective-permute-done((bf16[128,512]{1,0:T(8,128)(2,1)S(1)}, bf16[128,512]{1,0:T(8,128)(2,1)S(1)}, u32[]{:S(2)}, u32[]{:S(2)}) %collective-permute-start.5) | collective-permute-done | bytes 131104 | tf_op jit(solution)/shard_map/ppermute | solution.py:38
  73.6 5.4 %collective-permute-done.6.other = bf16[128,512]{1,0:T(8,128)(2,1)S(1)} collective-permute-done((bf16[128,512]{1,0:T(8,128)(2,1)S(1)}, bf16[128,512]{1,0:T(8,128)(2,1)S(1)}, u32[]{:S(2)}, u32[]{:S(2)}) %collective-permute-start.6) | collective-permute-done | bytes 131104 | tf_op jit(solution)/shard_map/ppermute | solution.py:38
  85.5 11.8 %collective-permute-done.9.refs_3_ = bf16[128,3584]{1,0:T(8,128)(2,1)S(1)} collective-permute-done((bf16[128,3584]{1,0:T(8,128)(2,1)S(1)}, bf16[128,3584]{1,0:T(8,128)(2,1)S(1)}, u32[]{:S(2)}, u32[]{:S(2)}) %collective-permute-start.9) | collective-permute-done | bytes 917536 | tf_op jit(solution)/shard_map/ppermute | solution.py:286
  99.0 8.5 %collective-permute-done.11.refs_3_ = bf16[64,3584]{1,0:T(8,128)(2,1)S(1)} collective-permute-done((bf16[64,3584]{1,0:T(8,128)(2,1)S(1)}, bf16[64,3584]{1,0:T(8,128)(2,1)S(1)}, u32[]{:S(2)}, u32[]{:S(2)}) %collective-permute-start.11) | collective-permute-done | bytes 458784 | tf_op jit(solution)/shard_map/ppermute | solution.py:286
  110.4 2.5 %collective-permute-start.14 = (bf16[16,7296]{1,0:T(8,128)(2,1)S(1)}, bf16[16,7296]{1,0:T(8,128)(2,1)S(1)}, u32[]{:S(2)}, u32[]{:S(2)}) collective-permute-start(bf16[16,7296]{1,0:T(8,128)(2,1)S(1)} %get-tuple-element.54), channel_id=1, source_target_pairs={{0,24},{1,97},{2,26},{3,99},{4,28},{5,101},{6,30},{7,103},{8,16},{... | collective-permute-start | bytes 700424 | tf_op jit(solution)/shard_map/ppermute | solution.py:286
  114.2 2.8 %collective-permute-done.13.two = bf16[16,7296]{1,0:T(8,128)(2,1)S(1)} collective-permute-done((bf16[16,7296]{1,0:T(8,128)(2,1)S(1)}, bf16[16,7296]{1,0:T(8,128)(2,1)S(1)}, u32[]{:S(2)}, u32[]{:S(2)}) %collective-permute-start.13) | collective-permute-done | bytes 233504 | tf_op jit(solution)/shard_map/ppermute | solution.py:286
  117.0 2.4 %collective-permute-done.14.three = bf16[16,7296]{1,0:T(8,128)(2,1)S(1)} collective-permute-done((bf16[16,7296]{1,0:T(8,128)(2,1)S(1)}, bf16[16,7296]{1,0:T(8,128)(2,1)S(1)}, u32[]{:S(2)}, u32[]{:S(2)}) %collective-permute-start.14) | collective-permute-done | bytes 233504 | tf_op jit(solution)/shard_map/ppermute | solution.py:286
  119.7 2.6 %collective-permute-start.17 = (bf16[16,3584]{1,0:T(8,128)(2,1)S(1)}, bf16[16,3584]{1,0:T(8,128)(2,1)S(1)}, u32[]{:S(2)}, u32[]{:S(2)}) collective-permute-start(bf16[16,3584]{1,0:T(8,128)(2,1)S(1)} %shard_map.133.refs_0_), channel_id=1, source_target_pairs={{0,24},{1,97},{2,26},{3,99},{4,28},{5,101},{6,30},{7,103},{8,16},{... | collective-permute-start | bytes 344072 | tf_op jit(solution)/shard_map/ppermute | solution.py:286
  123.9 1.9 %collective-permute-done.17.refs_3_ = bf16[16,3584]{1,0:T(8,128)(2,1)S(1)} collective-permute-done((bf16[16,3584]{1,0:T(8,128)(2,1)S(1)}, bf16[16,3584]{1,0:T(8,128)(2,1)S(1)}, u32[]{:S(2)}, u32[]{:S(2)}) %collective-permute-start.17) | collective-permute-done | bytes 114720 | tf_op jit(solution)/shard_map/ppermute | solution.py:286
  125.8 2.8 %collective-permute-done.16.refs_2_ = bf16[16,3584]{1,0:T(8,128)(2,1)S(1)} collective-permute-done((bf16[16,3584]{1,0:T(8,128)(2,1)S(1)}, bf16[16,3584]{1,0:T(8,128)(2,1)S(1)}, u32[]{:S(2)}, u32[]{:S(2)}) %collective-permute-start.16) | collective-permute-done | bytes 114720 | tf_op jit(solution)/shard_map/ppermute | solution.py:286
  128.6 1.9 %collective-permute-start.20 = (bf16[64,3584]{1,0:T(8,128)(2,1)S(1)}, bf16[64,3584]{1,0:T(8,128)(2,1)S(1)}, u32[]{:S(2)}, u32[]{:S(2)}) collective-permute-start(bf16[64,3584]{1,0:T(8,128)(2,1)S(1)} %shard_map.134.refs_0_), channel_id=1, source_target_pairs={{0,96},{1,25},{2,98},{3,27},{4,100},{5,29},{6,102},{7,31},{8,104},... | collective-permute-start | bytes 1376264 | tf_op jit(solution)/shard_map/ppermute | solution.py:286
  130.5 2.2 %collective-permute-start.18 = (bf16[64,3584]{1,0:T(8,128)(2,1)S(1)}, bf16[64,3584]{1,0:T(8,128)(2,1)S(1)}, u32[]{:S(2)}, u32[]{:S(2)}) collective-permute-start(bf16[64,3584]{1,0:T(8,128)(2,1)S(1)} %shard_map.134.refs_0_), channel_id=1, source_target_pairs={{0,32},{1,9},{2,34},{3,11},{4,36},{5,13},{6,38},{7,15},{8,40},{9,1... | collective-permute-start | bytes 1376264 | tf_op jit(solution)/shard_map/ppermute | solution.py:286
  132.8 10.5 %collective-permute-done.20.refs_3_ = bf16[64,3584]{1,0:T(8,128)(2,1)S(1)} collective-permute-done((bf16[64,3584]{1,0:T(8,128)(2,1)S(1)}, bf16[64,3584]{1,0:T(8,128)(2,1)S(1)}, u32[]{:S(2)}, u32[]{:S(2)}) %collective-permute-start.20) | collective-permute-done | bytes 458784 | tf_op jit(solution)/shard_map/ppermute | solution.py:286
  147.5 2.5 %collective-permute-start.23 = (bf16[32,512]{1,0:T(8,128)(2,1)S(1)}, bf16[32,512]{1,0:T(8,128)(2,1)S(1)}, u32[]{:S(2)}, u32[]{:S(2)}) collective-permute-start(bf16[32,512]{1,0:T(8,128)(2,1)S(1)} %get-tuple-element.59), channel_id=1, source_target_pairs={{0,4},{1,5},{2,6},{3,7},{4,0},{5,1},{6,2},{7,3},{8,12},{9,13},{10,... | collective-permute-start | bytes 98312 | tf_op jit(solution)/shard_map/ppermute | solution.py:38
  150.1 2.1 %collective-permute-start.24 = (bf16[32,512]{1,0:T(8,128)(2,1)S(1)}, bf16[32,512]{1,0:T(8,128)(2,1)S(1)}, u32[]{:S(2)}, u32[]{:S(2)}) collective-permute-start(bf16[32,512]{1,0:T(8,128)(2,1)S(1)} %get-tuple-element.60), channel_id=1, source_target_pairs={{0,6},{1,7},{2,4},{3,5},{4,2},{5,3},{6,0},{7,1},{8,14},{9,15},{10,... | collective-permute-start | bytes 98312 | tf_op jit(solution)/shard_map/ppermute | solution.py:38
  153.0 2.2 %collective-permute-done.24.three = bf16[32,512]{1,0:T(8,128)(2,1)S(1)} collective-permute-done((bf16[32,512]{1,0:T(8,128)(2,1)S(1)}, bf16[32,512]{1,0:T(8,128)(2,1)S(1)}, u32[]{:S(2)}, u32[]{:S(2)}) %collective-permute-start.24) | collective-permute-done | bytes 32800 | tf_op jit(solution)/shard_map/ppermute | solution.py:38
  (69 shorter events, 28.5 us)
Async XLA Ops:
  0.6 5.8 %collective-permute-start.2 = (f32[32,512]{1,0:T(8,128)}, f32[32,512]{1,0:T(8,128)S(1)}, u32[]{:S(2)}, u32[]{:S(2)}) collective-permute-start(f32[32,512]{1,0:T(8,128)} %bitcast.23), channel_id=1, source_target_pairs={{0,6},{1,7},{2,4},{3,5},{4,2},{5,3},{6,0},{7,1},{8,14},{9,15},{10,... | collective-permute-start | bytes 196616 | tf_op jit(solution)/shard_map/ppermute | solution.py:38
  3.6 6.0 %collective-permute-start.1 = (f32[32,512]{1,0:T(8,128)}, f32[32,512]{1,0:T(8,128)S(1)}, u32[]{:S(2)}, u32[]{:S(2)}) collective-permute-start(f32[32,512]{1,0:T(8,128)} %bitcast.24), channel_id=1, source_target_pairs={{0,4},{1,5},{2,6},{3,7},{4,0},{5,1},{6,2},{7,3},{8,12},{9,13},{10,... | collective-permute-start | bytes 196616 | tf_op jit(solution)/shard_map/ppermute | solution.py:38
  4.4 5.2 %collective-permute-start = (f32[32,512]{1,0:T(8,128)}, f32[32,512]{1,0:T(8,128)S(1)}, u32[]{:S(2)}, u32[]{:S(2)}) collective-permute-start(f32[32,512]{1,0:T(8,128)} %bitcast.25), channel_id=1, source_target_pairs={{0,2},{1,3},{2,0},{3,1},{4,6},{5,7},{6,4},{7,5},{8,10},{9,11},{10,... | collective-permute-start | bytes 196616 | tf_op jit(solution)/shard_map/ppermute | solution.py:38
  11.1 1.4 collective-permute-start.3
  15.9 26.4 %all-to-all-start = ((bf16[128,24,128]{2,1,0:T(8,128)(2,1)}), bf16[128,24,128]{2,1,0:T(8,128)(2,1)S(1)}, u32[]{:S(2)}, u32[]{:S(2)}) async-start(bf16[128,24,128]{2,1,0:T(8,128)(2,1)} %bitcast.11), calls=%async_computation | async-start | bytes 1572864 | tf_op jit(solution)/shard_map/all_to_all | solution.py:448
  67.2 5.6 %collective-permute-start.5 = (bf16[128,512]{1,0:T(8,128)(2,1)S(1)}, bf16[128,512]{1,0:T(8,128)(2,1)S(1)}, u32[]{:S(2)}, u32[]{:S(2)}) collective-permute-start(bf16[128,512]{1,0:T(8,128)(2,1)S(1)} %get-tuple-element.38), channel_id=1, source_target_pairs={{0,2},{1,3},{2,0},{3,1},{4,6},{5,7},{6,4},{7,5},{8,10},{9,11},{10,... | collective-permute-start | bytes 393224 | tf_op jit(solution)/shard_map/ppermute | solution.py:38
  72.8 6.3 %collective-permute-start.6 = (bf16[128,512]{1,0:T(8,128)(2,1)S(1)}, bf16[128,512]{1,0:T(8,128)(2,1)S(1)}, u32[]{:S(2)}, u32[]{:S(2)}) collective-permute-start(bf16[128,512]{1,0:T(8,128)(2,1)S(1)} %get-tuple-element.40), channel_id=1, source_target_pairs={{0,6},{1,7},{2,4},{3,5},{4,2},{5,3},{6,0},{7,1},{8,14},{9,15},{10,... | collective-permute-start | bytes 393224 | tf_op jit(solution)/shard_map/ppermute | solution.py:38
  79.1 1.4 collective-permute-start.7
  82.3 15.0 %collective-permute-start.8 = (bf16[128,3712]{1,0:T(8,128)(2,1)S(1)}, bf16[128,3712]{1,0:T(8,128)(2,1)S(1)}, u32[]{:S(2)}, u32[]{:S(2)}) collective-permute-start(bf16[128,3712]{1,0:T(8,128)(2,1)S(1)} %get-tuple-element.44), channel_id=1, source_target_pairs={{0,32},{1,9},{2,34},{3,11},{4,36},{5,13},{6,38},{7,15},{8,40},{9,1... | collective-permute-start | bytes 2850824 | tf_op jit(solution)/shard_map/ppermute | solution.py:286
  82.7 14.6 %collective-permute-start.9 = (bf16[128,3584]{1,0:T(8,128)(2,1)S(1)}, bf16[128,3584]{1,0:T(8,128)(2,1)S(1)}, u32[]{:S(2)}, u32[]{:S(2)}) collective-permute-start(bf16[128,3584]{1,0:T(8,128)(2,1)S(1)} %get-tuple-element.46), channel_id=1, source_target_pairs={{0,96},{1,25},{2,98},{3,27},{4,100},{5,29},{6,102},{7,31},{8,104},... | collective-permute-start | bytes 2752520 | tf_op jit(solution)/shard_map/ppermute | solution.py:286
  97.9 9.9 %collective-permute-start.10 = (bf16[64,3712]{1,0:T(8,128)(2,1)S(1)}, bf16[64,3712]{1,0:T(8,128)(2,1)S(1)}, u32[]{:S(2)}, u32[]{:S(2)}) collective-permute-start(bf16[64,3712]{1,0:T(8,128)(2,1)S(1)} %get-tuple-element.48), channel_id=1, source_target_pairs={{0,96},{1,25},{2,98},{3,27},{4,100},{5,29},{6,102},{7,31},{8,104},... | collective-permute-start | bytes 1425416 | tf_op jit(solution)/shard_map/ppermute | solution.py:286
  99.0 8.5 %collective-permute-start.11 = (bf16[64,3584]{1,0:T(8,128)(2,1)S(1)}, bf16[64,3584]{1,0:T(8,128)(2,1)S(1)}, u32[]{:S(2)}, u32[]{:S(2)}) collective-permute-start(bf16[64,3584]{1,0:T(8,128)(2,1)S(1)} %get-tuple-element.50), channel_id=1, source_target_pairs={{0,32},{1,9},{2,34},{3,11},{4,36},{5,13},{6,38},{7,15},{8,40},{9,1... | collective-permute-start | bytes 1376264 | tf_op jit(solution)/shard_map/ppermute | solution.py:286
  108.1 6.1 %collective-permute-start.12 = (bf16[16,7296]{1,0:T(8,128)(2,1)S(1)}, bf16[16,7296]{1,0:T(8,128)(2,1)S(1)}, u32[]{:S(2)}, u32[]{:S(2)}) collective-permute-start(bf16[16,7296]{1,0:T(8,128)(2,1)S(1)} %get-tuple-element.52), channel_id=1, source_target_pairs={{0,8},{1,33},{2,10},{3,35},{4,12},{5,37},{6,14},{7,39},{8,0},{9,41... | collective-permute-start | bytes 700424 | tf_op jit(solution)/shard_map/ppermute | solution.py:286
  109.0 8.0 %collective-permute-start.13 = (bf16[16,7296]{1,0:T(8,128)(2,1)S(1)}, bf16[16,7296]{1,0:T(8,128)(2,1)S(1)}, u32[]{:S(2)}, u32[]{:S(2)}) collective-permute-start(bf16[16,7296]{1,0:T(8,128)(2,1)S(1)} %get-tuple-element.53), channel_id=1, source_target_pairs={{0,16},{1,65},{2,18},{3,67},{4,20},{5,69},{6,22},{7,71},{8,24},{9,... | collective-permute-start | bytes 700424 | tf_op jit(solution)/shard_map/ppermute | solution.py:286
  110.4 9.0 %collective-permute-start.14 = (bf16[16,7296]{1,0:T(8,128)(2,1)S(1)}, bf16[16,7296]{1,0:T(8,128)(2,1)S(1)}, u32[]{:S(2)}, u32[]{:S(2)}) collective-permute-start(bf16[16,7296]{1,0:T(8,128)(2,1)S(1)} %get-tuple-element.54), channel_id=1, source_target_pairs={{0,24},{1,97},{2,26},{3,99},{4,28},{5,101},{6,30},{7,103},{8,16},{... | collective-permute-start | bytes 700424 | tf_op jit(solution)/shard_map/ppermute | solution.py:286
  119.7 6.1 %collective-permute-start.17 = (bf16[16,3584]{1,0:T(8,128)(2,1)S(1)}, bf16[16,3584]{1,0:T(8,128)(2,1)S(1)}, u32[]{:S(2)}, u32[]{:S(2)}) collective-permute-start(bf16[16,3584]{1,0:T(8,128)(2,1)S(1)} %shard_map.133.refs_0_), channel_id=1, source_target_pairs={{0,24},{1,97},{2,26},{3,99},{4,28},{5,101},{6,30},{7,103},{8,16},{... | collective-permute-start | bytes 344072 | tf_op jit(solution)/shard_map/ppermute | solution.py:286
  122.3 6.3 %collective-permute-start.16 = (bf16[16,3584]{1,0:T(8,128)(2,1)S(1)}, bf16[16,3584]{1,0:T(8,128)(2,1)S(1)}, u32[]{:S(2)}, u32[]{:S(2)}) collective-permute-start(bf16[16,3584]{1,0:T(8,128)(2,1)S(1)} %shard_map.133.refs_0_), channel_id=1, source_target_pairs={{0,16},{1,65},{2,18},{3,67},{4,20},{5,69},{6,22},{7,71},{8,24},{9,... | collective-permute-start | bytes 344072 | tf_op jit(solution)/shard_map/ppermute | solution.py:286
  122.3 6.3 %collective-permute-start.15 = (bf16[16,3584]{1,0:T(8,128)(2,1)S(1)}, bf16[16,3584]{1,0:T(8,128)(2,1)S(1)}, u32[]{:S(2)}, u32[]{:S(2)}) collective-permute-start(bf16[16,3584]{1,0:T(8,128)(2,1)S(1)} %shard_map.133.refs_0_), channel_id=1, source_target_pairs={{0,8},{1,33},{2,10},{3,35},{4,12},{5,37},{6,14},{7,39},{8,0},{9,41... | collective-permute-start | bytes 344072 | tf_op jit(solution)/shard_map/ppermute | solution.py:286
  128.6 14.7 %collective-permute-start.20 = (bf16[64,3584]{1,0:T(8,128)(2,1)S(1)}, bf16[64,3584]{1,0:T(8,128)(2,1)S(1)}, u32[]{:S(2)}, u32[]{:S(2)}) collective-permute-start(bf16[64,3584]{1,0:T(8,128)(2,1)S(1)} %shard_map.134.refs_0_), channel_id=1, source_target_pairs={{0,96},{1,25},{2,98},{3,27},{4,100},{5,29},{6,102},{7,31},{8,104},... | collective-permute-start | bytes 1376264 | tf_op jit(solution)/shard_map/ppermute | solution.py:286
  130.5 12.8 %collective-permute-start.19 = (bf16[64,3584]{1,0:T(8,128)(2,1)S(1)}, bf16[64,3584]{1,0:T(8,128)(2,1)S(1)}, u32[]{:S(2)}, u32[]{:S(2)}) collective-permute-start(bf16[64,3584]{1,0:T(8,128)(2,1)S(1)} %shard_map.134.refs_0_), channel_id=1, source_target_pairs={{0,64},{1,17},{2,66},{3,19},{4,68},{5,21},{6,70},{7,23},{8,72},{9,... | collective-permute-start | bytes 1376264 | tf_op jit(solution)/shard_map/ppermute | solution.py:286
  130.5 13.7 %collective-permute-start.18 = (bf16[64,3584]{1,0:T(8,128)(2,1)S(1)}, bf16[64,3584]{1,0:T(8,128)(2,1)S(1)}, u32[]{:S(2)}, u32[]{:S(2)}) collective-permute-start(bf16[64,3584]{1,0:T(8,128)(2,1)S(1)} %shard_map.134.refs_0_), channel_id=1, source_target_pairs={{0,32},{1,9},{2,34},{3,11},{4,36},{5,13},{6,38},{7,15},{8,40},{9,1... | collective-permute-start | bytes 1376264 | tf_op jit(solution)/shard_map/ppermute | solution.py:286
  147.4 4.8 %collective-permute-start.22 = (bf16[32,512]{1,0:T(8,128)(2,1)S(1)}, bf16[32,512]{1,0:T(8,128)(2,1)S(1)}, u32[]{:S(2)}, u32[]{:S(2)}) collective-permute-start(bf16[32,512]{1,0:T(8,128)(2,1)S(1)} %get-tuple-element.58), channel_id=1, source_target_pairs={{0,2},{1,3},{2,0},{3,1},{4,6},{5,7},{6,4},{7,5},{8,10},{9,11},{10,... | collective-permute-start | bytes 98312 | tf_op jit(solution)/shard_map/ppermute | solution.py:38
  147.5 5.5 %collective-permute-start.23 = (bf16[32,512]{1,0:T(8,128)(2,1)S(1)}, bf16[32,512]{1,0:T(8,128)(2,1)S(1)}, u32[]{:S(2)}, u32[]{:S(2)}) collective-permute-start(bf16[32,512]{1,0:T(8,128)(2,1)S(1)} %get-tuple-element.59), channel_id=1, source_target_pairs={{0,4},{1,5},{2,6},{3,7},{4,0},{5,1},{6,2},{7,3},{8,12},{9,13},{10,... | collective-permute-start | bytes 98312 | tf_op jit(solution)/shard_map/ppermute | solution.py:38
  150.1 5.1 %collective-permute-start.24 = (bf16[32,512]{1,0:T(8,128)(2,1)S(1)}, bf16[32,512]{1,0:T(8,128)(2,1)S(1)}, u32[]{:S(2)}, u32[]{:S(2)}) collective-permute-start(bf16[32,512]{1,0:T(8,128)(2,1)S(1)} %get-tuple-element.60), channel_id=1, source_target_pairs={{0,6},{1,7},{2,4},{3,5},{4,2},{5,3},{6,0},{7,1},{8,14},{9,15},{10,... | collective-permute-start | bytes 98312 | tf_op jit(solution)/shard_map/ppermute | solution.py:38
  (9 other events, 182.1 us)

commit v3 on v2

--- a/solution.py
+++ b/solution.py
@@ -27,7 +27,7 @@
 VM = pl.BlockSpec(memory_space=pltpu.VMEM)
 SM = pl.BlockSpec(memory_space=pltpu.SMEM)
 HBM = pl.BlockSpec(memory_space=pltpu.HBM)
-DMA = pltpu.SemaphoreType.DMA
+ANY = pl.BlockSpec(memory_space=pl.ANY)
 
 
 def swap_gx(array, bits):
@@ -38,11 +38,21 @@
     return lax.ppermute(array, "gy", [(i, i ^ bits) for i in range(NY)])
 
 
+def swap_by_core(array, first, second, axis="gx"):
+    pairs = []
+    for i in range(NX):
+        for j in range(NY):
+            bits = second if j & 1 else first
+            pairs.append((i * NY + j, (i ^ bits) * NY + j if axis == "gx" else i * NY + (j ^ bits)))
+    return lax.ppermute(array, ("gx", "gy"), pairs)
+
+
 def gray(place):
     return ((place & 1) ^ (place >> 1)) * 2 + (place >> 1)
 
 
-def call(body, outs, ins, scratch=(), limit=32):
+def call(body, outs, ins, scratch=(), limit=14, cost=0):
+    cost = pl.CostEstimate(flops=0, bytes_accessed=cost, transcendentals=0) if cost else None
     return pl.pallas_call(
         body,
         out_shape=outs,
@@ -50,6 +60,7 @@
         out_specs=jax.tree.map(lambda _: VM, outs),
         scratch_shapes=list(scratch),
         compiler_params=pltpu.CompilerParams(vmem_limit_bytes=limit * MIB),
+        cost_estimate=cost,
     )
 
 
@@ -61,9 +72,30 @@
     return jax.ShapeDtypeStruct(shape, dtype)
 
 
-def qkv_body(where, near, far, gain, weight, out, lhs, rows, held, sem):
-    fetch = pltpu.make_async_copy(weight, held, sem)
-    fetch.start()
+def bring_body(count, *refs):
+    ins, outs, sems = refs[:count], refs[-1 - count : -1], refs[-1]
+    fetches = [pltpu.make_async_copy(a, b, sems.at[i]) for i, (a, b) in enumerate(zip(ins, outs))]
+    for fetch in fetches:
+        fetch.start()
+    for fetch in fetches:
+        fetch.wait()
+
+
+def bring(arrays, after):
+    size = sum(a.size * a.dtype.itemsize for a in arrays)
+    outs = pl.pallas_call(
+        functools.partial(bring_body, len(arrays)),
+        out_shape=tuple(pltpu.VMEM(a.shape, a.dtype) for a in arrays),
+        in_specs=[HBM] * len(arrays) + [ANY] * len(after),
+        out_specs=(VM,) * len(arrays),
+        scratch_shapes=[pltpu.SemaphoreType.DMA((len(arrays),))],
+        compiler_params=pltpu.CompilerParams(vmem_limit_bytes=14 * MIB),
+        cost_estimate=pl.CostEstimate(flops=0, bytes_accessed=2 * size, transcendentals=0),
+    )(*(hbm(a) for a in arrays), *after)
+    return [pltpu.with_memory_space_constraint(a, pltpu.VMEM) for a in outs]
+
+
+def qkv_body(where, near, far, gain, held, out, lhs, rows):
     mine = where[1]
     for flag, source in enumerate((near, far)):
         for k in range(4):
@@ -78,7 +110,6 @@
         high = whole.astype(BF16).astype(F32)
         rows[pl.ds(20 + 2 * t, 128, stride=24), :] = high
         rows[pl.ds(21 + 2 * t, 128, stride=24), :] = whole - high
-    fetch.wait()
     for pair in range(5):
         part = jnp.dot(lhs[...], held[:, pair * 256 : pair * 256 + 256], preferred_element_type=F32)
         for j in (2 * pair, 2 * pair + 1):
@@ -93,23 +124,22 @@
     return call(
         qkv_body,
         shaped((128 * 24, HD), BF16),
-        [SM, VM, VM, VM, HBM],
-        [
-            pltpu.VMEM((256, WIDTH), BF16),
-            pltpu.VMEM((128 * 24, HD), F32),
-            pltpu.VMEM((WIDTH, 1280), BF16),
-            DMA,
-        ],
-    )(where, near, far, gain, hbm(weight))
+        [SM, VM, VM, VM, VM],
+        [pltpu.VMEM((256, WIDTH), BF16), pltpu.VMEM((128 * 24, HD), F32)],
+    )(where, near, far, gain, weight)
 
 
 def turn(vectors, cosine, sine):
     return vectors * cosine + pltpu.roll(vectors, HD // 2, vectors.ndim - 1) * sine
 
 
-def attend_body(angles, received, keys, values, out, fresh, scores, held, sem):
-    fetch = pltpu.make_async_copy(values, held, sem)
-    fetch.start()
+def attend_body(angles, received, keys, values, order, out, fresh, scores, held, sems):
+    fetches = []
+    for i, cache in enumerate((keys, values)):
+        for g in range(0, KVH, 2):
+            fetch = pltpu.make_async_copy(cache.at[0, pl.ds(g, 2)], held.at[i, pl.ds(g, 2)], sems.at[i, g // 2])
+            fetch.start()
+            fetches.append(fetch)
     total = received[0].astype(F32)
     for i in range(1, NX):
         total = total + received[i].astype(F32)
@@ -134,8 +164,10 @@
     both = jnp.concatenate(queries, axis=1)
     both16 = both.astype(BF16)
     for g in range(KVH):
+        if g % 2 == 0:
+            fetches[g // 2].wait()
         scores[g * 16 : g * 16 + 16, :] = lax.dot_general(
-            both16[g], keys[0, g], (((1,), (1,)), ((), ())), preferred_element_type=F32
+            both16[g], held[0, g], (((1,), (1,)), ((), ())), preferred_element_type=F32
         )
     extra = []
     step = lax.broadcasted_iota(jnp.int32, (KVH, 16, 1), 1) // GQ
@@ -151,9 +183,10 @@
     share = 1.0 / (jnp.sum(cached, axis=1, keepdims=True) + extra[0] + extra[1])
     probs = (cached * share).astype(BF16)
     extra = [(value * share).astype(BF16).astype(F32).reshape(KVH, 16, 1) for value in extra]
-    fetch.wait()
     for g in range(KVH):
-        mixed = jnp.dot(probs[g * 16 : g * 16 + 16, :], held[0, g], preferred_element_type=F32)
+        if g % 2 == 0:
+            fetches[4 + g // 2].wait()
+        mixed = jnp.dot(probs[g * 16 : g * 16 + 16, :], held[1, g], preferred_element_type=F32)
         for t in range(2):
             mixed = mixed + extra[t][g] * new_values[t][g : g + 1, :].astype(F32)
         mixed = mixed.astype(BF16)
@@ -161,74 +194,87 @@
             out[i, g] = mixed
 
 
-def attend(angles, received, keys, values):
+def attend(angles, received, keys, values, order):
     return call(
         attend_body,
         (shaped((NX, KVH, 16, HD), BF16), shaped((1, 2, KVH, 2 * HD), BF16)),
-        [VM, VM, VM, HBM],
-        [pltpu.VMEM((KVH * 16, CACHE), F32), pltpu.VMEM((1, KVH, CACHE, HD), BF16), DMA],
-    )(angles, received, keys, hbm(values))
-
-
-def out_body(where, received, weight, keep, send, wide, lhs, held, sem):
-    fetch = pltpu.make_async_copy(weight, held, sem)
-    fetch.start()
-    mine = where[1]
+        [VM, VM, HBM, HBM, ANY],
+        [
+            pltpu.VMEM((KVH * 16, CACHE), F32),
+            pltpu.VMEM((2, KVH, CACHE, HD), BF16),
+            pltpu.SemaphoreType.DMA((2, KVH // 2)),
+        ],
+    )(angles, received, hbm(keys), hbm(values), order)
+
+
+def out_body(where, received, weight, twin, total, send, wide, lhs):
     wide[...] = received[...].astype(F32)
-    for flag in range(2):
-        for k in range(4):
-            block = mine ^ (2 * k + flag)
-            for t in range(2):
-                place = flag * 128 + k * 32 + t * 16
-                for h in range(GQ):
-                    start = block * 256 + t * 8 + h
-                    lhs[place : place + 16, h * HD : h * HD + HD] = wide[
-                        pl.ds(start, 16, stride=16), :
-                    ].astype(BF16)
-    fetch.wait()
-    send[...] = jnp.dot(lhs[128:, :], held[...], preferred_element_type=F32).astype(BF16)
-    keep[...] = jnp.dot(lhs[:128, :], held[...], preferred_element_type=F32)
-
-
-def out_partial(where, received, weight):
+    for other in range(2):
+        core = (where[1] & 1) ^ other
+        for t in range(2):
+            for h in range(GQ):
+                column = (other * GQ + h) * HD
+                lhs[t * 64 : t * 64 + 64, column : column + HD] = wide[
+                    pl.ds(core * 16 + t * 8 + h, 64, stride=32), :
+                ].astype(BF16)
+    half = GQ * HD
+    part = jnp.dot(lhs[:, :half], weight[...], preferred_element_type=F32)
+    part = part + jnp.dot(lhs[:, half:], twin[...], preferred_element_type=F32)
+    total[...] = part
+    send[...] = part.astype(BF16)
+
+
+def out_partial(where, received, mine, twin):
     return call(
         out_body,
         (shaped((128, WIDTH), F32), shaped((128, WIDTH), BF16)),
-        [SM, VM, HBM],
-        [
-            pltpu.VMEM((128 * 16, HD), F32),
-            pltpu.VMEM((256, KVH * HD), BF16),
-            pltpu.VMEM((KVH * HD, WIDTH), BF16),
-            DMA,
-        ],
-    )(where, received, hbm(weight))
-
-
-def add_body(turned, whole, other, total, send):
-    for k in range(4):
-        rows, theirs = slice(k * 32, k * 32 + 32), slice((k ^ turned) * 32, (k ^ turned) * 32 + 32)
-        part = whole[rows, :] + other[theirs, :].astype(F32)
-        total[rows, :] = part
-        send[rows, :] = part.astype(BF16)
-
-
-def residual_body(residual, gain, whole, other, after, normed):
-    for k in range(4):
-        rows, theirs = slice(k * 32, k * 32 + 32), slice((k ^ 3) * 32, (k ^ 3) * 32 + 32)
-        part = residual[rows, :] + whole[rows, :] + other[theirs, :].astype(F32)
-        normed[rows, :] = (part * gain[...]).astype(BF16)
-        if k == 0:
-            after[...] = part
-
-
-def add_attention(residual, gain, keep, send):
-    halves = (shaped((128, WIDTH), F32), shaped((128, WIDTH), BF16))
-    whole, sent = call(functools.partial(add_body, 0), halves, [VM] * 2)(keep, swap_gy(send, 1))
-    whole, sent = call(functools.partial(add_body, 1), halves, [VM] * 2)(whole, swap_gy(sent, 2))
-    after, near = call(
-        residual_body, (shaped((32, WIDTH), F32), shaped((128, WIDTH), BF16)), [VM] * 4
-    )(residual, gain, whole, swap_gy(sent, 6))
-    return after, near, swap_gy(near, 1)
+        [SM, VM, VM, VM],
+        [pltpu.VMEM((64 * 32, HD), F32), pltpu.VMEM((128, 2 * GQ * HD), BF16)],
+    )(where, received, mine, twin)
+
+
+def add_body(whole, one, two, three, mine):
+    total = whole[...] + (one[...].astype(F32) + two[...].astype(F32) + three[...].astype(F32))
+    mine[...] = total.astype(BF16)
+
+
+def sum_over_x(whole, sent):
+    others = [swap_gy(sent, 2 * k) for k in (1, 2, 3)]
+    mine = call(add_body, shaped((128, WIDTH), BF16), [VM] * 4)(whole, *others)
+    return mine, swap_gy(mine, 1)
+
+
+def residual_body(where, residual, far, attn_gain, ffn_gain, mine, twin, after, normed, sums, attention):
+    core = where[1] & 1
+    sums[0] = jnp.where(core == 0, mine[...].astype(F32), twin[...].astype(F32))
+    sums[1] = jnp.where(core == 0, twin[...].astype(F32), mine[...].astype(F32))
+    for flag in range(2):
+        for k in range(4):
+            block = where[1] ^ (2 * k + flag)
+            for t in range(2):
+                start = pl.multiple_of(t * 64 + block * 8, 8)
+                place = flag * 128 + k * 32 + t * 16
+                for odd in range(2):
+                    for q in range(4):
+                        attention[q, pl.ds(place + odd, 8, stride=2), :] = sums[
+                            odd, pl.ds(start, 8), q * 128 : q * 128 + 128
+                        ]
+    for q in range(4):
+        columns = slice(q * 128, q * 128 + 128)
+        first = residual[:, columns] + attention[q, :128, :]
+        after[:, columns] = first[:32]
+        normed[:128, columns] = (first * ffn_gain[:, columns]).astype(BF16)
+        second = far[:, columns].astype(F32) / attn_gain[:, columns] + attention[q, 128:, :]
+        normed[128:, columns] = (second * ffn_gain[:, columns]).astype(BF16)
+
+
+def add_attention(where, residual, far, attn_gain, ffn_gain, sums):
+    return call(
+        residual_body,
+        (shaped((32, WIDTH), F32), shaped((256, WIDTH), BF16)),
+        [SM] + [VM] * 6,
+        [pltpu.VMEM((2, 128, WIDTH), F32), pltpu.VMEM((4, 256, HD), F32)],
+    )(where, residual, far, attn_gain, ffn_gain, *sums)
 
 
 def split_body(keep, other, own, *sends):
@@ -252,19 +298,29 @@
     return call(final_body, shaped((32, WIDTH), F32), [VM] * 5)(after, own, *pieces)
 
 
-def rows_body(own, one, two, three, gain, residual, scaled):
-    for k, piece in enumerate((own, one, two, three)):
-        rows = slice(k * 32, k * 32 + 32)
-        residual[rows, :] = piece[...]
-        scaled[rows, :] = (piece[...] * gain[...]).astype(BF16)
+def rows_body(own, one, two, three, gain, residual, scaled, held, sems):
+    fetches = [
+        pltpu.make_async_copy(gain, held, sems.at[0]),
+        pltpu.make_async_copy(own, residual.at[pl.ds(0, 32)], sems.at[1]),
+    ]
+    for fetch in fetches:
+        fetch.start()
+    for k, piece in enumerate((one, two, three)):
+        residual[k * 32 + 32 : k * 32 + 64, :] = piece[...]
+    for fetch in fetches:
+        fetch.wait()
+    scaled[...] = (residual[...] * held[...]).astype(BF16)
 
 
 def gather_rows(own, gain):
-    pieces = [own] + [swap_gy(own, 2 * k) for k in (1, 2, 3)]
-    residual, near = call(
-        rows_body, (shaped((128, WIDTH), F32), shaped((128, WIDTH), BF16)), [VM] * 5
-    )(*pieces, gain)
-    return residual, near, swap_gy(near, 1)
+    pieces = [swap_gy(own, 2 * k) for k in (1, 2, 3)]
+    residual, near, gain = call(
+        rows_body,
+        (shaped((128, WIDTH), F32), shaped((128, WIDTH), BF16), shaped((1, WIDTH), F32)),
+        [HBM] + [VM] * 3 + [HBM],
+        [pltpu.SemaphoreType.DMA((2,))],
+    )(hbm(own), *pieces, hbm(gain))
+    return residual, near, swap_gy(near, 1), gain
 
 
 def two_parts(squares):
@@ -276,14 +332,6 @@
 def one_part(parts):
     wide = parts.astype(F32)
     return wide + pltpu.roll(wide, HD // 2, 1)
-
-
-def swap_by_core(array, first, second):
-    pairs = []
-    for i in range(NX):
-        for j in range(NY):
-            pairs.append((i * NY + j, (i ^ (second if j & 1 else first)) * NY + j))
-    return lax.ppermute(array, ("gx", "gy"), pairs)
 
 
 def place_of(flow, core, chunk):
@@ -293,17 +341,15 @@
     return turned
 
 
-def gate_body(send, where, near, far, gain, gate, up, *refs):
+def gate_body(send, where, acts, gain, gate, up, *refs):
     outs, lhs = refs[:2], refs[2]
     core = where[1] & 1
     for f in range(2):
-        for flag, source in enumerate((near, far)):
-            for k in range(4):
-                block = where[1] ^ (2 * k + flag)
-                for t in range(2):
-                    place = place_of(f, core, (2 * block + t) ^ where[0])
-                    start = pl.multiple_of(place * 16, 16)
-                    lhs[f, pl.ds(start, 16), :] = source[k * 32 + t * 16 : k * 32 + t * 16 + 16, :]
+        for chunk in range(16):
+            block = where[1] ^ (2 * ((chunk >> 1) & 3) + (chunk >> 3))
+            place = place_of(f, core, (2 * block + (chunk & 1)) ^ where[0])
+            start = pl.multiple_of(place * 16, 16)
+            lhs[f, pl.ds(start, 16), :] = acts[chunk * 16 : chunk * 16 + 16, :]
     rows = slice(128, 256) if send else slice(0, 128)
     plain = lhs[0, rows, :].astype(F32) / gain[...]
     squares = jnp.broadcast_to(jnp.sum(plain * plain, axis=1, keepdims=True), (128, HD))
@@ -318,7 +364,7 @@
     return call(
         functools.partial(gate_body, send),
         tuple(shaped((128, width), BF16 if send else F32) for width in WIDTHS),
-        [SM] + [VM] * 5,
+        [SM] + [VM] * 4,
         [pltpu.VMEM((2, 256, WIDTH), BF16)],
     )(*args)
 
@@ -443,15 +489,26 @@
     angles = rotations(positions)
     attn_gain, ffn_gain = attn_gain.reshape(1, WIDTH), ffn_gain.reshape(1, WIDTH)
 
-    residual, near, far = gather_rows(inputs.reshape(32, WIDTH), attn_gain)
-    partial = qkv_partial(where, near, far, attn_gain, qkv_weight).reshape(128, 24, HD)
+    twin = swap_gy(out_weight, 1)
+    residual, near, far, attn_gain = gather_rows(inputs.reshape(32, WIDTH), attn_gain)
+    (qkv_weight,) = bring((qkv_weight,), (near,))
+    partial = qkv_partial(where, near, far, attn_gain, qkv_weight)
+    out_weight, twin = bring((out_weight, twin), (partial,))
+    partial = partial.reshape(128, 24, HD)
     received = lax.all_to_all(partial, ("gx", "gy"), 0, 0, tiled=True).reshape(NX, NY, 24, HD)
-    attended, new_kv = attend(angles, received, k_cache, v_cache)
-    heads = lax.all_to_all(attended.reshape(128, 16, HD), ("gx", "gy"), 0, 0, tiled=True)
-    keep, send = out_partial(where, heads.reshape(128 * 16, HD), out_weight)
-    after_attn, near, far = add_attention(residual, ffn_gain, keep, send)
-
-    units = hidden_units(where, near, far, ffn_gain, gate_weight, up_weight)
+    attended, new_kv = attend(angles, received, k_cache, v_cache, out_weight)
+    heads = lax.all_to_all(
+        attended.reshape(64, 32, HD),
+        ("gx", "gy"),
+        0,
+        0,
+        axis_index_groups=[[i * NY + 2 * j + core for i in range(NX) for j in range(NY // 2)] for core in range(2)],
+        tiled=True,
+    )
+    even_odd = sum_over_x(*out_partial(where, heads.reshape(64 * 32, HD), out_weight, twin))
+    after_attn, normed = add_attention(where, residual, far, attn_gain, ffn_gain, even_odd)
+
+    units = hidden_units(where, normed, ffn_gain, gate_weight, up_weight)
     outputs = add_ffn(after_attn, *down_partial(where, units, down_weight))
     return outputs.reshape(2, 16, WIDTH), new_kv
 

time: 156 us -> 150 us (0.962)
  waiting for transfers between devices: 81.7 us -> 72.5 us
  Pallas kernels: 16 us -> 18.9 us
  starting transfers between devices: 36.6 us -> 38.6 us
    ppermute x12 -> x13, waiting for transfers between devices: 22.6 us -> 14.2 us  [swap_gy(): return lax.ppermute(array, 'gy', [(i, i ^ bits) for i in range(NY)])]
    pallas_call x5 -> x6, Pallas kernels: 3.51 us -> 6.59 us  [the longest x2 2.89 us: bring(): pl.pallas_call(functools.partial(bring_body, len(arrays)), out_shape=tupl...]
    ppermute x12 -> x13, starting transfers between devices: 10.8 us -> 13.4 us  [swap_gy(): return lax.ppermute(array, 'gy', [(i, i ^ bits) for i in range(NY)])]
    all_to_all x1, waiting for transfers between devices: 15.9 us -> 14.3 us  [per_device(): lax.all_to_all(partial, ('gx', 'gy'), 0, 0, tiled=True)]
  transfers between devices with their start and end apart: 26 -> 27, of which waited for: 21 -> 19; matrix products, arithmetic and copies ran while one was open for 0% -> 0% of each run, Pallas kernels for 1% -> 5%
where the time goes in v3:
time: 150 us
  waiting for transfers between devices  72.5 us (48%)
  starting transfers between devices  38.6 us (26%)
  Pallas kernels  18.9 us (13%)
  blocking collectives  17.7 us (12%)
  between operations  1.51 us (1%)
    ppermute x13, waiting for transfers between devices, swap_by_core(): return lax.ppermute(array, ('gx', 'gy'), pairs)  44 us
    all_to_all x1, blocking collectives, per_device(): lax.all_to_all(attended.reshape(64, 32, HD), ('gx', 'gy'), 0, 0, axis_ind...  17.7 us
    ppermute x13, starting transfers between devices, swap_by_core(): return lax.ppermute(array, ('gx', 'gy'), pairs)  15.1 us
    all_to_all x1, waiting for transfers between devices, per_device(): lax.all_to_all(partial, ('gx', 'gy'), 0, 0, tiled=True)  14.3 us
    ppermute x13, waiting for transfers between devices, swap_gy(): return lax.ppermute(array, 'gy', [(i, i ^ bits) for i in range(NY)])  14.2 us
    ppermute x13, starting transfers between devices, swap_gy(): return lax.ppermute(array, 'gy', [(i, i ^ bits) for i in range(NY)])  13.4 us
    all_to_all x1, starting transfers between devices, per_device(): lax.all_to_all(partial, ('gx', 'gy'), 0, 0, tiled=True)  10.2 us
    pallas_call x1, Pallas kernels, attend(): call(attend_body, (shaped((NX, KVH, 16, HD), BF16), shaped((1, 2, KVH, 2...  3.71 us
  transfers between devices with their start and end apart: 27, of which 19 were waited for; matrix products, arithmetic and copies ran while one was open for 0% of the time, Pallas kernels for 5%

profile of v3, /device:TPU:0, one launch (start us, length us, event | category | flops | bytes accessed | tf_op | source)
XLA Modules:
  0.0 149.9 jit_solution(12095496896468586521)
XLA Ops:
  0.6 2.9 %collective-permute-start.2 = (f32[32,512]{1,0:T(8,128)}, f32[32,512]{1,0:T(8,128)S(1)}, u32[]{:S(2)}, u32[]{:S(2)}) collective-permute-start(f32[32,512]{1,0:T(8,128)} %bitcast.26), channel_id=1, source_target_pairs={{0,6},{1,7},{2,4},{3,5},{4,2},{5,3},{6,0},{7,1},{8,14},{9,15},{10,... | collective-permute-start | bytes 196616 | tf_op jit(solution)/shard_map/ppermute | solution.py:38
  6.4 3.1 %collective-permute-done.1.two = f32[32,512]{1,0:T(8,128)S(1)} collective-permute-done((f32[32,512]{1,0:T(8,128)}, f32[32,512]{1,0:T(8,128)S(1)}, u32[]{:S(2)}, u32[]{:S(2)}) %collective-permute-start.1) | collective-permute-done | bytes 65568 | tf_op jit(solution)/shard_map/ppermute | solution.py:38
  12.0 2.0 %shard_map.124.refs_2_ = bf16[3072,128]{1,0:T(8,128)(2,1)} custom-call(s32[2]{0:T(128)S(1)} %pad_add_fusion.where, bf16[128,512]{1,0:T(8,128)(2,1)S(1)} %get-tuple-element.32.refs_1_.near, bf16[128,512]{1,0:T(8,128)(2,1)S(1)} %collective-permute-done.3.far, f32[1,512]{1,0:T(1,128)S(1)} %get-tuple-element.33.gain.attn_gain, bf16[512,1280]{1,0:T(8,128)(2,1)S(1)} %shard_map.123.held), custom_call_target="tpu_custom_call" | custom-call | tf_op jit(solution)/shard_map/pallas_call | solution.py:124
  14.0 10.2 %all-to-all-start = ((bf16[128,24,128]{2,1,0:T(8,128)(2,1)}), bf16[128,24,128]{2,1,0:T(8,128)(2,1)S(1)}, u32[]{:S(2)}, u32[]{:S(2)}) async-start(bf16[128,24,128]{2,1,0:T(8,128)(2,1)} %bitcast.11), calls=%async_computation | async-start | bytes 1572864 | tf_op jit(solution)/shard_map/all_to_all | solution.py:498
  26.2 14.3 %all-to-all-done = bf16[128,24,128]{2,1,0:T(8,128)(2,1)S(1)} async-done(((bf16[128,24,128]{2,1,0:T(8,128)(2,1)}), bf16[128,24,128]{2,1,0:T(8,128)(2,1)S(1)}, u32[]{:S(2)}, u32[]{:S(2)}) %all-to-all-start) | async-done | bytes 786464 | tf_op jit(solution)/shard_map/all_to_all | solution.py:498
  40.5 3.7 %shard_map.126 = (bf16[16,8,16,128]{3,2,1,0:T(8,128)(2,1)S(1)}, bf16[1,2,8,256]{3,2,1,0:T(8,128)(2,1)}) custom-call(f32[4,128]{1,0:T(4,128)S(1)} %pad_maximum_fusion.angles, bf16[16,8,24,128]{3,2,1,0:T(8,128)(2,1)S(1)} %bitcast.20, bf16[1,8,1024,128]{3,2,1,0:T(8,128)(2,1)} %keys.1, bf16[1,8,1024,128]{3,2,1,0:T(8,128)(2,1)} %values.1, ...), custom_call_target="tpu_custom_call" | custom-call | tf_op jit(solution)/shard_map/pallas_call | solution.py:198
  44.3 17.7 %all_to_all.10 = bf16[64,32,128]{2,1,0:T(8,128)(2,1)S(1)} all-to-all(bf16[64,32,128]{2,1,0:T(8,128)(2,1)S(1)} %bitcast.22), channel_id=1, replica_groups={{0,2,4,6,8,10,12,14,16,18,20,22,24,26,28,30,32,34,36,38,40,42,44,46,48,..., dimensions={0} | all-to-all | bytes 1048576 | tf_op jit(solution)/shard_map/all_to_all | solution.py:500
  67.7 3.5 %collective-permute-done.7.three = bf16[128,512]{1,0:T(8,128)(2,1)S(1)} collective-permute-done((bf16[128,512]{1,0:T(8,128)(2,1)S(1)}, bf16[128,512]{1,0:T(8,128)(2,1)S(1)}, u32[]{:S(2)}, u32[]{:S(2)}) %collective-permute-start.7) | collective-permute-done | bytes 131104 | tf_op jit(solution)/shard_map/ppermute | solution.py:38
  79.0 12.2 %collective-permute-done.10.refs_3_ = bf16[128,3584]{1,0:T(8,128)(2,1)S(1)} collective-permute-done((bf16[128,3584]{1,0:T(8,128)(2,1)S(1)}, bf16[128,3584]{1,0:T(8,128)(2,1)S(1)}, u32[]{:S(2)}, u32[]{:S(2)}) %collective-permute-start.10) | collective-permute-done | bytes 917536 | tf_op jit(solution)/shard_map/ppermute | solution.py:47
  92.5 8.5 %collective-permute-done.12.refs_3_ = bf16[64,3584]{1,0:T(8,128)(2,1)S(1)} collective-permute-done((bf16[64,3584]{1,0:T(8,128)(2,1)S(1)}, bf16[64,3584]{1,0:T(8,128)(2,1)S(1)}, u32[]{:S(2)}, u32[]{:S(2)}) %collective-permute-start.12) | collective-permute-done | bytes 458784 | tf_op jit(solution)/shard_map/ppermute | solution.py:47
  102.2 1.9 %collective-permute-start.14 = (bf16[16,7296]{1,0:T(8,128)(2,1)S(1)}, bf16[16,7296]{1,0:T(8,128)(2,1)S(1)}, u32[]{:S(2)}, u32[]{:S(2)}) collective-permute-start(bf16[16,7296]{1,0:T(8,128)(2,1)S(1)} %get-tuple-element.51), channel_id=1, source_target_pairs={{0,16},{1,65},{2,18},{3,67},{4,20},{5,69},{6,22},{7,71},{8,24},{9,... | collective-permute-start | bytes 700424 | tf_op jit(solution)/shard_map/ppermute | solution.py:47
  104.2 2.6 %collective-permute-start.15 = (bf16[16,7296]{1,0:T(8,128)(2,1)S(1)}, bf16[16,7296]{1,0:T(8,128)(2,1)S(1)}, u32[]{:S(2)}, u32[]{:S(2)}) collective-permute-start(bf16[16,7296]{1,0:T(8,128)(2,1)S(1)} %get-tuple-element.52), channel_id=1, source_target_pairs={{0,24},{1,97},{2,26},{3,99},{4,28},{5,101},{6,30},{7,103},{8,16},{... | collective-permute-start | bytes 700424 | tf_op jit(solution)/shard_map/ppermute | solution.py:47
  108.1 2.7 %collective-permute-done.14.two = bf16[16,7296]{1,0:T(8,128)(2,1)S(1)} collective-permute-done((bf16[16,7296]{1,0:T(8,128)(2,1)S(1)}, bf16[16,7296]{1,0:T(8,128)(2,1)S(1)}, u32[]{:S(2)}, u32[]{:S(2)}) %collective-permute-start.14) | collective-permute-done | bytes 233504 | tf_op jit(solution)/shard_map/ppermute | solution.py:47
  110.8 2.4 %collective-permute-done.15.three = bf16[16,7296]{1,0:T(8,128)(2,1)S(1)} collective-permute-done((bf16[16,7296]{1,0:T(8,128)(2,1)S(1)}, bf16[16,7296]{1,0:T(8,128)(2,1)S(1)}, u32[]{:S(2)}, u32[]{:S(2)}) %collective-permute-start.15) | collective-permute-done | bytes 233504 | tf_op jit(solution)/shard_map/ppermute | solution.py:47
  113.5 2.6 %collective-permute-start.18 = (bf16[16,3584]{1,0:T(8,128)(2,1)S(1)}, bf16[16,3584]{1,0:T(8,128)(2,1)S(1)}, u32[]{:S(2)}, u32[]{:S(2)}) collective-permute-start(bf16[16,3584]{1,0:T(8,128)(2,1)S(1)} %shard_map.134.refs_0_), channel_id=1, source_target_pairs={{0,24},{1,97},{2,26},{3,99},{4,28},{5,101},{6,30},{7,103},{8,16},{... | collective-permute-start | bytes 344072 | tf_op jit(solution)/shard_map/ppermute | solution.py:47
  117.6 1.9 %collective-permute-done.18.refs_3_ = bf16[16,3584]{1,0:T(8,128)(2,1)S(1)} collective-permute-done((bf16[16,3584]{1,0:T(8,128)(2,1)S(1)}, bf16[16,3584]{1,0:T(8,128)(2,1)S(1)}, u32[]{:S(2)}, u32[]{:S(2)}) %collective-permute-start.18) | collective-permute-done | bytes 114720 | tf_op jit(solution)/shard_map/ppermute | solution.py:47
  119.5 2.9 %collective-permute-done.17.refs_2_ = bf16[16,3584]{1,0:T(8,128)(2,1)S(1)} collective-permute-done((bf16[16,3584]{1,0:T(8,128)(2,1)S(1)}, bf16[16,3584]{1,0:T(8,128)(2,1)S(1)}, u32[]{:S(2)}, u32[]{:S(2)}) %collective-permute-start.17) | collective-permute-done | bytes 114720 | tf_op jit(solution)/shard_map/ppermute | solution.py:47
  122.4 1.9 %collective-permute-start.21 = (bf16[64,3584]{1,0:T(8,128)(2,1)S(1)}, bf16[64,3584]{1,0:T(8,128)(2,1)S(1)}, u32[]{:S(2)}, u32[]{:S(2)}) collective-permute-start(bf16[64,3584]{1,0:T(8,128)(2,1)S(1)} %shard_map.135.refs_0_), channel_id=1, source_target_pairs={{0,96},{1,25},{2,98},{3,27},{4,100},{5,29},{6,102},{7,31},{8,104},... | collective-permute-start | bytes 1376264 | tf_op jit(solution)/shard_map/ppermute | solution.py:47
  124.4 2.2 %collective-permute-start.19 = (bf16[64,3584]{1,0:T(8,128)(2,1)S(1)}, bf16[64,3584]{1,0:T(8,128)(2,1)S(1)}, u32[]{:S(2)}, u32[]{:S(2)}) collective-permute-start(bf16[64,3584]{1,0:T(8,128)(2,1)S(1)} %shard_map.135.refs_0_), channel_id=1, source_target_pairs={{0,32},{1,9},{2,34},{3,11},{4,36},{5,13},{6,38},{7,15},{8,40},{9,1... | collective-permute-start | bytes 1376264 | tf_op jit(solution)/shard_map/ppermute | solution.py:47
  126.6 10.5 %collective-permute-done.21.refs_3_ = bf16[64,3584]{1,0:T(8,128)(2,1)S(1)} collective-permute-done((bf16[64,3584]{1,0:T(8,128)(2,1)S(1)}, bf16[64,3584]{1,0:T(8,128)(2,1)S(1)}, u32[]{:S(2)}, u32[]{:S(2)}) %collective-permute-start.21) | collective-permute-done | bytes 458784 | tf_op jit(solution)/shard_map/ppermute | solution.py:47
  138.0 1.8 %shard_map.136 = (f32[128,512]{1,0:T(8,128)S(1)}, bf16[128,512]{1,0:T(8,128)(2,1)S(1)}) custom-call(s32[2]{0:T(128)S(1)} %pad_add_fusion.where, bf16[64,3584]{1,0:T(8,128)(2,1)S(1)} %shard_map.135.refs_0_, bf16[64,3584]{1,0:T(8,128)(2,1)S(1)} %collective-permute-done.19.refs_1_, bf16[64,3584]{1,0:T(8,128)(2,1)S(1)} %collective-permute-done.20.refs_2_, ...), custom_call_target="tpu_custom_call" | custom-call | tf_op jit(solution)/shard_map/pallas_call | solution.py:456
  142.0 2.1 %collective-permute-start.24 = (bf16[32,512]{1,0:T(8,128)(2,1)S(1)}, bf16[32,512]{1,0:T(8,128)(2,1)S(1)}, u32[]{:S(2)}, u32[]{:S(2)}) collective-permute-start(bf16[32,512]{1,0:T(8,128)(2,1)S(1)} %get-tuple-element.57), channel_id=1, source_target_pairs={{0,4},{1,5},{2,6},{3,7},{4,0},{5,1},{6,2},{7,3},{8,12},{9,13},{10,... | collective-permute-start | bytes 98312 | tf_op jit(solution)/shard_map/ppermute | solution.py:38
  144.1 2.0 %collective-permute-start.25 = (bf16[32,512]{1,0:T(8,128)(2,1)S(1)}, bf16[32,512]{1,0:T(8,128)(2,1)S(1)}, u32[]{:S(2)}, u32[]{:S(2)}) collective-permute-start(bf16[32,512]{1,0:T(8,128)(2,1)S(1)} %get-tuple-element.58), channel_id=1, source_target_pairs={{0,6},{1,7},{2,4},{3,5},{4,2},{5,3},{6,0},{7,1},{8,14},{9,15},{10,... | collective-permute-start | bytes 98312 | tf_op jit(solution)/shard_map/ppermute | solution.py:38
  147.4 1.8 %collective-permute-done.25.three = bf16[32,512]{1,0:T(8,128)(2,1)S(1)} collective-permute-done((bf16[32,512]{1,0:T(8,128)(2,1)S(1)}, bf16[32,512]{1,0:T(8,128)(2,1)S(1)}, u32[]{:S(2)}, u32[]{:S(2)}) %collective-permute-start.25) | collective-permute-done | bytes 32800 | tf_op jit(solution)/shard_map/ppermute | solution.py:38
  (66 shorter events, 30.9 us)
Async XLA Ops:
  0.6 5.8 %collective-permute-start.2 = (f32[32,512]{1,0:T(8,128)}, f32[32,512]{1,0:T(8,128)S(1)}, u32[]{:S(2)}, u32[]{:S(2)}) collective-permute-start(f32[32,512]{1,0:T(8,128)} %bitcast.26), channel_id=1, source_target_pairs={{0,6},{1,7},{2,4},{3,5},{4,2},{5,3},{6,0},{7,1},{8,14},{9,15},{10,... | collective-permute-start | bytes 196616 | tf_op jit(solution)/shard_map/ppermute | solution.py:38
  3.6 6.0 %collective-permute-start.1 = (f32[32,512]{1,0:T(8,128)}, f32[32,512]{1,0:T(8,128)S(1)}, u32[]{:S(2)}, u32[]{:S(2)}) collective-permute-start(f32[32,512]{1,0:T(8,128)} %bitcast.27), channel_id=1, source_target_pairs={{0,4},{1,5},{2,6},{3,7},{4,0},{5,1},{6,2},{7,3},{8,12},{9,13},{10,... | collective-permute-start | bytes 196616 | tf_op jit(solution)/shard_map/ppermute | solution.py:38
  4.4 5.2 %collective-permute-start = (f32[32,512]{1,0:T(8,128)}, f32[32,512]{1,0:T(8,128)S(1)}, u32[]{:S(2)}, u32[]{:S(2)}) collective-permute-start(f32[32,512]{1,0:T(8,128)} %bitcast.28), channel_id=1, source_target_pairs={{0,2},{1,3},{2,0},{3,1},{4,6},{5,7},{6,4},{7,5},{8,10},{9,11},{10,... | collective-permute-start | bytes 196616 | tf_op jit(solution)/shard_map/ppermute | solution.py:38
  4.8 19.8 %collective-permute-start.4 = (bf16[1024,512]{1,0:T(8,128)(2,1)}, bf16[1024,512]{1,0:T(8,128)(2,1)}, u32[]{:S(2)}, u32[]{:S(2)}) collective-permute-start(bf16[1024,512]{1,0:T(8,128)(2,1)} %refs_0_.3), channel_id=1, source_target_pairs={{0,1},{1,0},{2,3},{3,2},{4,5},{5,4},{6,7},{7,6},{8,9},{9,8},{10,11... | collective-permute-start | bytes 3145736 | tf_op jit(solution)/shard_map/ppermute | solution.py:38
  14.0 26.5 %all-to-all-start = ((bf16[128,24,128]{2,1,0:T(8,128)(2,1)}), bf16[128,24,128]{2,1,0:T(8,128)(2,1)S(1)}, u32[]{:S(2)}, u32[]{:S(2)}) async-start(bf16[128,24,128]{2,1,0:T(8,128)(2,1)} %bitcast.11), calls=%async_computation | async-start | bytes 1572864 | tf_op jit(solution)/shard_map/all_to_all | solution.py:498
  63.5 7.7 %collective-permute-start.7 = (bf16[128,512]{1,0:T(8,128)(2,1)S(1)}, bf16[128,512]{1,0:T(8,128)(2,1)S(1)}, u32[]{:S(2)}, u32[]{:S(2)}) collective-permute-start(bf16[128,512]{1,0:T(8,128)(2,1)S(1)} %get-tuple-element.38), channel_id=1, source_target_pairs={{0,6},{1,7},{2,4},{3,5},{4,2},{5,3},{6,0},{7,1},{8,14},{9,15},{10,... | collective-permute-start | bytes 393224 | tf_op jit(solution)/shard_map/ppermute | solution.py:38
  64.4 6.8 %collective-permute-start.6 = (bf16[128,512]{1,0:T(8,128)(2,1)S(1)}, bf16[128,512]{1,0:T(8,128)(2,1)S(1)}, u32[]{:S(2)}, u32[]{:S(2)}) collective-permute-start(bf16[128,512]{1,0:T(8,128)(2,1)S(1)} %get-tuple-element.38), channel_id=1, source_target_pairs={{0,4},{1,5},{2,6},{3,7},{4,0},{5,1},{6,2},{7,3},{8,12},{9,13},{10,... | collective-permute-start | bytes 393224 | tf_op jit(solution)/shard_map/ppermute | solution.py:38
  66.1 5.9 %collective-permute-start.5 = (bf16[128,512]{1,0:T(8,128)(2,1)S(1)}, bf16[128,512]{1,0:T(8,128)(2,1)S(1)}, u32[]{:S(2)}, u32[]{:S(2)}) collective-permute-start(bf16[128,512]{1,0:T(8,128)(2,1)S(1)} %get-tuple-element.38), channel_id=1, source_target_pairs={{0,2},{1,3},{2,0},{3,1},{4,6},{5,7},{6,4},{7,5},{8,10},{9,11},{10,... | collective-permute-start | bytes 393224 | tf_op jit(solution)/shard_map/ppermute | solution.py:38
  76.0 15.1 %collective-permute-start.9 = (bf16[128,3712]{1,0:T(8,128)(2,1)S(1)}, bf16[128,3712]{1,0:T(8,128)(2,1)S(1)}, u32[]{:S(2)}, u32[]{:S(2)}) collective-permute-start(bf16[128,3712]{1,0:T(8,128)(2,1)S(1)} %get-tuple-element.42), channel_id=1, source_target_pairs={{0,32},{1,9},{2,34},{3,11},{4,36},{5,13},{6,38},{7,15},{8,40},{9,1... | collective-permute-start | bytes 2850824 | tf_op jit(solution)/shard_map/ppermute | solution.py:47
  76.5 14.6 %collective-permute-start.10 = (bf16[128,3584]{1,0:T(8,128)(2,1)S(1)}, bf16[128,3584]{1,0:T(8,128)(2,1)S(1)}, u32[]{:S(2)}, u32[]{:S(2)}) collective-permute-start(bf16[128,3584]{1,0:T(8,128)(2,1)S(1)} %get-tuple-element.44), channel_id=1, source_target_pairs={{0,96},{1,25},{2,98},{3,27},{4,100},{5,29},{6,102},{7,31},{8,104},... | collective-permute-start | bytes 2752520 | tf_op jit(solution)/shard_map/ppermute | solution.py:47
  91.7 9.9 %collective-permute-start.11 = (bf16[64,3712]{1,0:T(8,128)(2,1)S(1)}, bf16[64,3712]{1,0:T(8,128)(2,1)S(1)}, u32[]{:S(2)}, u32[]{:S(2)}) collective-permute-start(bf16[64,3712]{1,0:T(8,128)(2,1)S(1)} %get-tuple-element.46), channel_id=1, source_target_pairs={{0,96},{1,25},{2,98},{3,27},{4,100},{5,29},{6,102},{7,31},{8,104},... | collective-permute-start | bytes 1425416 | tf_op jit(solution)/shard_map/ppermute | solution.py:47
  92.5 8.5 %collective-permute-start.12 = (bf16[64,3584]{1,0:T(8,128)(2,1)S(1)}, bf16[64,3584]{1,0:T(8,128)(2,1)S(1)}, u32[]{:S(2)}, u32[]{:S(2)}) collective-permute-start(bf16[64,3584]{1,0:T(8,128)(2,1)S(1)} %get-tuple-element.48), channel_id=1, source_target_pairs={{0,32},{1,9},{2,34},{3,11},{4,36},{5,13},{6,38},{7,15},{8,40},{9,1... | collective-permute-start | bytes 1376264 | tf_op jit(solution)/shard_map/ppermute | solution.py:47
  101.9 6.1 %collective-permute-start.13 = (bf16[16,7296]{1,0:T(8,128)(2,1)S(1)}, bf16[16,7296]{1,0:T(8,128)(2,1)S(1)}, u32[]{:S(2)}, u32[]{:S(2)}) collective-permute-start(bf16[16,7296]{1,0:T(8,128)(2,1)S(1)} %get-tuple-element.50), channel_id=1, source_target_pairs={{0,8},{1,33},{2,10},{3,35},{4,12},{5,37},{6,14},{7,39},{8,0},{9,41... | collective-permute-start | bytes 700424 | tf_op jit(solution)/shard_map/ppermute | solution.py:47
  102.2 8.6 %collective-permute-start.14 = (bf16[16,7296]{1,0:T(8,128)(2,1)S(1)}, bf16[16,7296]{1,0:T(8,128)(2,1)S(1)}, u32[]{:S(2)}, u32[]{:S(2)}) collective-permute-start(bf16[16,7296]{1,0:T(8,128)(2,1)S(1)} %get-tuple-element.51), channel_id=1, source_target_pairs={{0,16},{1,65},{2,18},{3,67},{4,20},{5,69},{6,22},{7,71},{8,24},{9,... | collective-permute-start | bytes 700424 | tf_op jit(solution)/shard_map/ppermute | solution.py:47
  104.2 9.0 %collective-permute-start.15 = (bf16[16,7296]{1,0:T(8,128)(2,1)S(1)}, bf16[16,7296]{1,0:T(8,128)(2,1)S(1)}, u32[]{:S(2)}, u32[]{:S(2)}) collective-permute-start(bf16[16,7296]{1,0:T(8,128)(2,1)S(1)} %get-tuple-element.52), channel_id=1, source_target_pairs={{0,24},{1,97},{2,26},{3,99},{4,28},{5,101},{6,30},{7,103},{8,16},{... | collective-permute-start | bytes 700424 | tf_op jit(solution)/shard_map/ppermute | solution.py:47
  113.5 6.1 %collective-permute-start.18 = (bf16[16,3584]{1,0:T(8,128)(2,1)S(1)}, bf16[16,3584]{1,0:T(8,128)(2,1)S(1)}, u32[]{:S(2)}, u32[]{:S(2)}) collective-permute-start(bf16[16,3584]{1,0:T(8,128)(2,1)S(1)} %shard_map.134.refs_0_), channel_id=1, source_target_pairs={{0,24},{1,97},{2,26},{3,99},{4,28},{5,101},{6,30},{7,103},{8,16},{... | collective-permute-start | bytes 344072 | tf_op jit(solution)/shard_map/ppermute | solution.py:47
  116.1 6.3 %collective-permute-start.17 = (bf16[16,3584]{1,0:T(8,128)(2,1)S(1)}, bf16[16,3584]{1,0:T(8,128)(2,1)S(1)}, u32[]{:S(2)}, u32[]{:S(2)}) collective-permute-start(bf16[16,3584]{1,0:T(8,128)(2,1)S(1)} %shard_map.134.refs_0_), channel_id=1, source_target_pairs={{0,16},{1,65},{2,18},{3,67},{4,20},{5,69},{6,22},{7,71},{8,24},{9,... | collective-permute-start | bytes 344072 | tf_op jit(solution)/shard_map/ppermute | solution.py:47
  116.1 6.3 %collective-permute-start.16 = (bf16[16,3584]{1,0:T(8,128)(2,1)S(1)}, bf16[16,3584]{1,0:T(8,128)(2,1)S(1)}, u32[]{:S(2)}, u32[]{:S(2)}) collective-permute-start(bf16[16,3584]{1,0:T(8,128)(2,1)S(1)} %shard_map.134.refs_0_), channel_id=1, source_target_pairs={{0,8},{1,33},{2,10},{3,35},{4,12},{5,37},{6,14},{7,39},{8,0},{9,41... | collective-permute-start | bytes 344072 | tf_op jit(solution)/shard_map/ppermute | solution.py:47
  122.4 14.7 %collective-permute-start.21 = (bf16[64,3584]{1,0:T(8,128)(2,1)S(1)}, bf16[64,3584]{1,0:T(8,128)(2,1)S(1)}, u32[]{:S(2)}, u32[]{:S(2)}) collective-permute-start(bf16[64,3584]{1,0:T(8,128)(2,1)S(1)} %shard_map.135.refs_0_), channel_id=1, source_target_pairs={{0,96},{1,25},{2,98},{3,27},{4,100},{5,29},{6,102},{7,31},{8,104},... | collective-permute-start | bytes 1376264 | tf_op jit(solution)/shard_map/ppermute | solution.py:47
  124.4 12.8 %collective-permute-start.20 = (bf16[64,3584]{1,0:T(8,128)(2,1)S(1)}, bf16[64,3584]{1,0:T(8,128)(2,1)S(1)}, u32[]{:S(2)}, u32[]{:S(2)}) collective-permute-start(bf16[64,3584]{1,0:T(8,128)(2,1)S(1)} %shard_map.135.refs_0_), channel_id=1, source_target_pairs={{0,64},{1,17},{2,66},{3,19},{4,68},{5,21},{6,70},{7,23},{8,72},{9,... | collective-permute-start | bytes 1376264 | tf_op jit(solution)/shard_map/ppermute | solution.py:47
  124.4 13.7 %collective-permute-start.19 = (bf16[64,3584]{1,0:T(8,128)(2,1)S(1)}, bf16[64,3584]{1,0:T(8,128)(2,1)S(1)}, u32[]{:S(2)}, u32[]{:S(2)}) collective-permute-start(bf16[64,3584]{1,0:T(8,128)(2,1)S(1)} %shard_map.135.refs_0_), channel_id=1, source_target_pairs={{0,32},{1,9},{2,34},{3,11},{4,36},{5,13},{6,38},{7,15},{8,40},{9,1... | collective-permute-start | bytes 1376264 | tf_op jit(solution)/shard_map/ppermute | solution.py:47
  141.3 4.8 %collective-permute-start.23 = (bf16[32,512]{1,0:T(8,128)(2,1)S(1)}, bf16[32,512]{1,0:T(8,128)(2,1)S(1)}, u32[]{:S(2)}, u32[]{:S(2)}) collective-permute-start(bf16[32,512]{1,0:T(8,128)(2,1)S(1)} %get-tuple-element.56), channel_id=1, source_target_pairs={{0,2},{1,3},{2,0},{3,1},{4,6},{5,7},{6,4},{7,5},{8,10},{9,11},{10,... | collective-permute-start | bytes 98312 | tf_op jit(solution)/shard_map/ppermute | solution.py:38
  142.0 5.4 %collective-permute-start.24 = (bf16[32,512]{1,0:T(8,128)(2,1)S(1)}, bf16[32,512]{1,0:T(8,128)(2,1)S(1)}, u32[]{:S(2)}, u32[]{:S(2)}) collective-permute-start(bf16[32,512]{1,0:T(8,128)(2,1)S(1)} %get-tuple-element.57), channel_id=1, source_target_pairs={{0,4},{1,5},{2,6},{3,7},{4,0},{5,1},{6,2},{7,3},{8,12},{9,13},{10,... | collective-permute-start | bytes 98312 | tf_op jit(solution)/shard_map/ppermute | solution.py:38
  144.1 5.1 %collective-permute-start.25 = (bf16[32,512]{1,0:T(8,128)(2,1)S(1)}, bf16[32,512]{1,0:T(8,128)(2,1)S(1)}, u32[]{:S(2)}, u32[]{:S(2)}) collective-permute-start(bf16[32,512]{1,0:T(8,128)(2,1)S(1)} %get-tuple-element.58), channel_id=1, source_target_pairs={{0,6},{1,7},{2,4},{3,5},{4,2},{5,3},{6,0},{7,1},{8,14},{9,15},{10,... | collective-permute-start | bytes 98312 | tf_op jit(solution)/shard_map/ppermute | solution.py:38
  (7 other events, 116.1 us)

commit v4 on v3

--- a/solution.py
+++ b/solution.py
@@ -134,12 +134,9 @@
 
 
 def attend_body(angles, received, keys, values, order, out, fresh, scores, held, sems):
-    fetches = []
-    for i, cache in enumerate((keys, values)):
-        for g in range(0, KVH, 2):
-            fetch = pltpu.make_async_copy(cache.at[0, pl.ds(g, 2)], held.at[i, pl.ds(g, 2)], sems.at[i, g // 2])
-            fetch.start()
-            fetches.append(fetch)
+    fetches = [pltpu.make_async_copy(a.at[0], held.at[i], sems.at[i]) for i, a in enumerate((keys, values))]
+    for fetch in fetches:
+        fetch.start()
     total = received[0].astype(F32)
     for i in range(1, NX):
         total = total + received[i].astype(F32)
@@ -163,9 +160,8 @@
         fresh[0, t, :, HD:] = value
     both = jnp.concatenate(queries, axis=1)
     both16 = both.astype(BF16)
+    fetches[0].wait()
     for g in range(KVH):
-        if g % 2 == 0:
-            fetches[g // 2].wait()
         scores[g * 16 : g * 16 + 16, :] = lax.dot_general(
             both16[g], held[0, g], (((1,), (1,)), ((), ())), preferred_element_type=F32
         )
@@ -183,9 +179,8 @@
     share = 1.0 / (jnp.sum(cached, axis=1, keepdims=True) + extra[0] + extra[1])
     probs = (cached * share).astype(BF16)
     extra = [(value * share).astype(BF16).astype(F32).reshape(KVH, 16, 1) for value in extra]
+    fetches[1].wait()
     for g in range(KVH):
-        if g % 2 == 0:
-            fetches[4 + g // 2].wait()
         mixed = jnp.dot(probs[g * 16 : g * 16 + 16, :], held[1, g], preferred_element_type=F32)
         for t in range(2):
             mixed = mixed + extra[t][g] * new_values[t][g : g + 1, :].astype(F32)
@@ -202,7 +197,7 @@
         [
             pltpu.VMEM((KVH * 16, CACHE), F32),
             pltpu.VMEM((2, KVH, CACHE, HD), BF16),
-            pltpu.SemaphoreType.DMA((2, KVH // 2)),
+            pltpu.SemaphoreType.DMA((2,)),
         ],
     )(angles, received, hbm(keys), hbm(values), order)
 
@@ -233,48 +228,15 @@
     )(where, received, mine, twin)
 
 
-def add_body(whole, one, two, three, mine):
+def add_body(whole, three, one, two, mine):
     total = whole[...] + (one[...].astype(F32) + two[...].astype(F32) + three[...].astype(F32))
     mine[...] = total.astype(BF16)
 
 
 def sum_over_x(whole, sent):
-    others = [swap_gy(sent, 2 * k) for k in (1, 2, 3)]
+    others = [swap_gy(sent, 2 * k) for k in (3, 1, 2)]
     mine = call(add_body, shaped((128, WIDTH), BF16), [VM] * 4)(whole, *others)
     return mine, swap_gy(mine, 1)
-
-
-def residual_body(where, residual, far, attn_gain, ffn_gain, mine, twin, after, normed, sums, attention):
-    core = where[1] & 1
-    sums[0] = jnp.where(core == 0, mine[...].astype(F32), twin[...].astype(F32))
-    sums[1] = jnp.where(core == 0, twin[...].astype(F32), mine[...].astype(F32))
-    for flag in range(2):
-        for k in range(4):
-            block = where[1] ^ (2 * k + flag)
-            for t in range(2):
-                start = pl.multiple_of(t * 64 + block * 8, 8)
-                place = flag * 128 + k * 32 + t * 16
-                for odd in range(2):
-                    for q in range(4):
-                        attention[q, pl.ds(place + odd, 8, stride=2), :] = sums[
-                            odd, pl.ds(start, 8), q * 128 : q * 128 + 128
-                        ]
-    for q in range(4):
-        columns = slice(q * 128, q * 128 + 128)
-        first = residual[:, columns] + attention[q, :128, :]
-        after[:, columns] = first[:32]
-        normed[:128, columns] = (first * ffn_gain[:, columns]).astype(BF16)
-        second = far[:, columns].astype(F32) / attn_gain[:, columns] + attention[q, 128:, :]
-        normed[128:, columns] = (second * ffn_gain[:, columns]).astype(BF16)
-
-
-def add_attention(where, residual, far, attn_gain, ffn_gain, sums):
-    return call(
-        residual_body,
-        (shaped((32, WIDTH), F32), shaped((256, WIDTH), BF16)),
-        [SM] + [VM] * 6,
-        [pltpu.VMEM((2, 128, WIDTH), F32), pltpu.VMEM((4, 256, HD), F32)],
-    )(where, residual, far, attn_gain, ffn_gain, *sums)
 
 
 def split_body(keep, other, own, *sends):
@@ -284,42 +246,33 @@
         send[...] = whole[32 * k + 32 : 32 * k + 64].astype(BF16)
 
 
-def final_body(residual, own, one, two, three, out):
+def final_body(residual, own, two, one, three, out):
     out[...] = residual[...] + (own[...] + one[...].astype(F32) + two[...].astype(F32) + three[...].astype(F32))
 
 
-def add_ffn(after, keep, send):
+def add_ffn(after, keep, other):
     own, *sends = call(
         split_body,
         (shaped((32, WIDTH), F32),) + (shaped((32, WIDTH), BF16),) * 3,
         [VM, VM],
-    )(keep, swap_gy(send, 1))
-    pieces = [swap_gy(piece, 2 * (k + 1)) for k, piece in enumerate(sends)]
+    )(keep, other)
+    pieces = [swap_gy(sends[k - 1], 2 * k) for k in (2, 1, 3)]
     return call(final_body, shaped((32, WIDTH), F32), [VM] * 5)(after, own, *pieces)
 
 
-def rows_body(own, one, two, three, gain, residual, scaled, held, sems):
-    fetches = [
-        pltpu.make_async_copy(gain, held, sems.at[0]),
-        pltpu.make_async_copy(own, residual.at[pl.ds(0, 32)], sems.at[1]),
-    ]
-    for fetch in fetches:
-        fetch.start()
-    for k, piece in enumerate((one, two, three)):
-        residual[k * 32 + 32 : k * 32 + 64, :] = piece[...]
-    for fetch in fetches:
-        fetch.wait()
-    scaled[...] = (residual[...] * held[...]).astype(BF16)
+def rows_body(own, one, two, three, gain, residual, scaled):
+    for k, piece in enumerate((own, one, two, three)):
+        rows = slice(k * 32, k * 32 + 32)
+        residual[rows, :] = piece[...]
+        scaled[rows, :] = (piece[...] * gain[...]).astype(BF16)
 
 
 def gather_rows(own, gain):
     pieces = [swap_gy(own, 2 * k) for k in (1, 2, 3)]
-    residual, near, gain = call(
-        rows_body,
-        (shaped((128, WIDTH), F32), shaped((128, WIDTH), BF16), shaped((1, WIDTH), F32)),
-        [HBM] + [VM] * 3 + [HBM],
-        [pltpu.SemaphoreType.DMA((2,))],
-    )(hbm(own), *pieces, hbm(gain))
+    own, gain = bring((own, gain), ())
+    residual, near = call(
+        rows_body, (shaped((128, WIDTH), F32), shaped((128, WIDTH), BF16)), [VM] * 5
+    )(own, *pieces, gain)
     return residual, near, swap_gy(near, 1), gain
 
 
@@ -341,15 +294,7 @@
     return turned
 
 
-def gate_body(send, where, acts, gain, gate, up, *refs):
-    outs, lhs = refs[:2], refs[2]
-    core = where[1] & 1
-    for f in range(2):
-        for chunk in range(16):
-            block = where[1] ^ (2 * ((chunk >> 1) & 3) + (chunk >> 3))
-            place = place_of(f, core, (2 * block + (chunk & 1)) ^ where[0])
-            start = pl.multiple_of(place * 16, 16)
-            lhs[f, pl.ds(start, 16), :] = acts[chunk * 16 : chunk * 16 + 16, :]
+def products(send, lhs, gain, gate, up, outs):
     rows = slice(128, 256) if send else slice(0, 128)
     plain = lhs[0, rows, :].astype(F32) / gain[...]
     squares = jnp.broadcast_to(jnp.sum(plain * plain, axis=1, keepdims=True), (128, HD))
@@ -360,13 +305,47 @@
             outs[f][:, i * HALF : i * HALF + HALF] = part.astype(outs[f].dtype)
 
 
-def gate_partial(send, *args):
+def send_body(where, residual, far, attn_gain, gain, mine, twin, gate, up, after, lhs, first, second, sums, attention):
+    core = where[1] & 1
+    sums[0] = jnp.where(core == 0, mine[...].astype(F32), twin[...].astype(F32))
+    sums[1] = jnp.where(core == 0, twin[...].astype(F32), mine[...].astype(F32))
+    for chunk in range(16):
+        block = where[1] ^ (2 * ((chunk >> 1) & 3) + (chunk >> 3))
+        start = pl.multiple_of((chunk & 1) * 64 + block * 8, 8)
+        for odd in range(2):
+            for q in range(4):
+                attention[q, pl.ds(chunk * 16 + odd, 8, stride=2), :] = sums[
+                    odd, pl.ds(start, 8), q * 128 : q * 128 + 128
+                ]
+    for chunk in range(16):
+        rows = slice(chunk * 16, chunk * 16 + 16)
+        if chunk < 8:
+            whole = residual[rows, :]
+        else:
+            whole = far[chunk * 16 - 128 : chunk * 16 - 112, :].astype(F32) / attn_gain[...]
+        whole = whole + jnp.concatenate([attention[q, rows, :] for q in range(4)], axis=1)
+        if chunk < 2:
+            after[rows, :] = whole
+        normed = (whole * gain[...]).astype(BF16)
+        block = where[1] ^ (2 * ((chunk >> 1) & 3) + (chunk >> 3))
+        for f in range(2):
+            place = place_of(f, core, (2 * block + (chunk & 1)) ^ where[0])
+            lhs[f, pl.ds(pl.multiple_of(place * 16, 16), 16), :] = normed
+    products(True, lhs, gain, gate, up, (first, second))
+
+
+def keep_body(lhs, gain, gate, up, first, second):
+    products(False, lhs, gain, gate, up, (first, second))
+
+
+def send_partial(where, residual, far, attn_gain, gain, sums, gate, up):
     return call(
-        functools.partial(gate_body, send),
-        tuple(shaped((128, width), BF16 if send else F32) for width in WIDTHS),
-        [SM] + [VM] * 4,
-        [pltpu.VMEM((2, 256, WIDTH), BF16)],
-    )(*args)
+        send_body,
+        (shaped((32, WIDTH), F32), shaped((2, 256, WIDTH), BF16))
+        + tuple(shaped((128, width), BF16) for width in WIDTHS),
+        [SM] + [VM] * 8,
+        [pltpu.VMEM((2, 128, WIDTH), F32), pltpu.VMEM((4, 256, HD), F32)],
+    )(where, residual, far, attn_gain, gain, *sums, gate, up)
 
 
 def halve_body(*refs):
@@ -399,7 +378,7 @@
         start += 2 * HALF
 
 
-def hidden_body(own, one, two, three, out):
+def hidden_body(own, one, three, two, out):
     others = (one, two, three)
     squares = own[:, 4 * HALF :] + sum(one_part(other[:, 4 * HALF :]) for other in others)
     scale = lax.rsqrt(squares / D + EPSILON)[:, :1]
@@ -411,10 +390,9 @@
         out[:, f * HALF : f * HALF + HALF] = (gate / (1.0 + jnp.exp(-gate)) * up).astype(BF16)
 
 
-def hidden_units(*args):
-    sends = gate_partial(True, *args)
+def hidden_units(lhs, gain, gate, up, sends):
     moved = [swap_by_core(sends[0], 4, 1), swap_by_core(sends[1], 12, 3)]
-    keeps = gate_partial(False, *args)
+    keeps = call(keep_body, tuple(shaped((128, width), F32) for width in WIDTHS), [VM] * 4)(lhs, gain, gate, up)
     halves = []
     for width in WIDTHS:
         halves += [shaped((64, width), F32), shaped((64, width), BF16)]
@@ -424,7 +402,7 @@
     own, *sends = call(
         quarter_body, (shaped((16, wide), F32),) + (shaped((16, wide), BF16),) * 3, [VM] * 4
     )(parts[0], moved[0], parts[2], moved[1])
-    moved = [swap_by_core(part, k, 4 * k) for k, part in zip((1, 2, 3), sends)]
+    moved = [swap_by_core(sends[k - 1], k, 4 * k) for k in (1, 3, 2)]
     return call(hidden_body, shaped((16, UNITS), BF16), [VM] * 4)(own, *moved)
 
 
@@ -436,7 +414,7 @@
 
 
 def down_body(where, *refs):
-    pieces, (weight, keep, send, lhs) = refs[:4], refs[4:]
+    pieces, (weight, send, lhs) = refs[:4], refs[4:]
     core = where[1] & 1
     for m in range(4):
         for k in range(4):
@@ -446,6 +424,9 @@
             start = (block & 1) * 128 + (block >> 1) * 32 + (place & 1) * 16
             lhs[pl.ds(pl.multiple_of(start, 16), 16), :] = pieces[m][k * 16 : k * 16 + 16, :]
     send[...] = jnp.dot(lhs[128:, :], weight[...], preferred_element_type=F32).astype(BF16)
+
+
+def own_body(lhs, weight, keep):
     keep[...] = jnp.dot(lhs[:128, :], weight[...], preferred_element_type=F32)
 
 
@@ -453,12 +434,11 @@
     pieces = [units] + [swap_by_core(units, k, 4 * k) for k in (1, 2, 3)]
     near = call(stack_body, shaped((64, UNITS), BF16), [VM] * 4)(*pieces)
     pieces = [near] + [swap_by_core(near, 4 * k, k) for k in (1, 2, 3)]
-    return call(
-        down_body,
-        (shaped((128, WIDTH), F32), shaped((128, WIDTH), BF16)),
-        [SM] + [VM] * 5,
-        [pltpu.VMEM((256, UNITS), BF16)],
+    send, lhs = call(
+        down_body, (shaped((128, WIDTH), BF16), shaped((256, UNITS), BF16)), [SM] + [VM] * 5
     )(where, *pieces, weight)
+    other = swap_gy(send, 1)
+    return call(own_body, shaped((128, WIDTH), F32), [VM] * 2)(lhs, weight), other
 
 
 def rotations(positions):
@@ -506,9 +486,10 @@
         tiled=True,
     )
     even_odd = sum_over_x(*out_partial(where, heads.reshape(64 * 32, HD), out_weight, twin))
-    after_attn, normed = add_attention(where, residual, far, attn_gain, ffn_gain, even_odd)
-
-    units = hidden_units(where, normed, ffn_gain, gate_weight, up_weight)
+    after_attn, lhs, *sends = send_partial(
+        where, residual, far, attn_gain, ffn_gain, even_odd, gate_weight, up_weight
+    )
+    units = hidden_units(lhs, ffn_gain, gate_weight, up_weight, sends)
     outputs = add_ffn(after_attn, *down_partial(where, units, down_weight))
     return outputs.reshape(2, 16, WIDTH), new_kv
 

time: 150 us -> 146 us (0.973)
  waiting for transfers between devices: 72.5 us -> 69.5 us
    pallas_call x5, Pallas kernels: 6.86 us -> 4.99 us  [the longest x1 1.88 us: send_partial(): call(send_body, (shaped((32, WIDTH), F32), shaped((2, 256, WIDTH), BF16))...]
    ppermute x13, waiting for transfers between devices: 44 us -> 42.3 us  [swap_by_core(): return lax.ppermute(array, ('gx', 'gy'), pairs)]
    pallas_call x2 -> x3, Pallas kernels: 2.89 us -> 3.75 us  [bring(): pl.pallas_call(functools.partial(bring_body, len(arrays)), out_shape=tupl...]
  transfers between devices with their start and end apart: 27 -> 27, of which waited for: 19 -> 18; matrix products, arithmetic and copies ran while one was open for 0% -> 0% of each run, Pallas kernels for 5% -> 5%
where the time goes in v4:
time: 146 us
  waiting for transfers between devices  69.5 us (48%)
  starting transfers between devices  38.7 us (27%)
  blocking collectives  17.9 us (12%)
  Pallas kernels  17.5 us (12%)
  between operations  1.52 us (1%)
    ppermute x13, waiting for transfers between devices, swap_by_core(): return lax.ppermute(array, ('gx', 'gy'), pairs)  42.3 us
    all_to_all x1, blocking collectives, per_device(): lax.all_to_all(attended.reshape(64, 32, HD), ('gx', 'gy'), 0, 0, axis_ind...  17.9 us
    ppermute x13, starting transfers between devices, swap_by_core(): return lax.ppermute(array, ('gx', 'gy'), pairs)  15.7 us
    all_to_all x1, waiting for transfers between devices, per_device(): lax.all_to_all(partial, ('gx', 'gy'), 0, 0, tiled=True)  14.3 us
    ppermute x13, waiting for transfers between devices, swap_gy(): return lax.ppermute(array, 'gy', [(i, i ^ bits) for i in range(NY)])  12.9 us
    ppermute x13, starting transfers between devices, swap_gy(): return lax.ppermute(array, 'gy', [(i, i ^ bits) for i in range(NY)])  12.8 us
    all_to_all x1, starting transfers between devices, per_device(): lax.all_to_all(partial, ('gx', 'gy'), 0, 0, tiled=True)  10.2 us
    pallas_call x3, Pallas kernels, bring(): pl.pallas_call(functools.partial(bring_body, len(arrays)), out_shape=tupl...  3.75 us
  transfers between devices with their start and end apart: 27, of which 18 were waited for; matrix products, arithmetic and copies ran while one was open for 0% of the time, Pallas kernels for 5%

profile of v4, /device:TPU:0, one launch (start us, length us, event | category | flops | bytes accessed | tf_op | source)
XLA Modules:
  0.0 145.7 jit_solution(16552221283139231043)
XLA Ops:
  0.6 2.9 %collective-permute-start.2 = (f32[32,512]{1,0:T(8,128)}, f32[32,512]{1,0:T(8,128)S(1)}, u32[]{:S(2)}, u32[]{:S(2)}) collective-permute-start(f32[32,512]{1,0:T(8,128)} %bitcast.25), channel_id=1, source_target_pairs={{0,6},{1,7},{2,4},{3,5},{4,2},{5,3},{6,0},{7,1},{8,14},{9,15},{10,... | collective-permute-start | bytes 196616 | tf_op jit(solution)/shard_map/ppermute | solution.py:38
  6.4 3.1 %collective-permute-done.1.two = f32[32,512]{1,0:T(8,128)S(1)} collective-permute-done((f32[32,512]{1,0:T(8,128)}, f32[32,512]{1,0:T(8,128)S(1)}, u32[]{:S(2)}, u32[]{:S(2)}) %collective-permute-start.1) | collective-permute-done | bytes 65568 | tf_op jit(solution)/shard_map/ppermute | solution.py:38
  11.1 2.0 %shard_map.125.refs_2_ = bf16[3072,128]{1,0:T(8,128)(2,1)} custom-call(s32[2]{0:T(128)S(1)} %pad_add_fusion.where, bf16[128,512]{1,0:T(8,128)(2,1)S(1)} %get-tuple-element.35.refs_1_.near, bf16[128,512]{1,0:T(8,128)(2,1)S(1)} %collective-permute-done.3.far, f32[1,512]{1,0:T(1,128)S(1)} %get-tuple-element.33.gain.attn_gain, bf16[512,1280]{1,0:T(8,128)(2,1)S(1)} %shard_map.124.held), custom_call_target="tpu_custom_call" | custom-call | tf_op jit(solution)/shard_map/pallas_call | solution.py:124
  13.2 10.2 %all-to-all-start = ((bf16[128,24,128]{2,1,0:T(8,128)(2,1)}), bf16[128,24,128]{2,1,0:T(8,128)(2,1)S(1)}, u32[]{:S(2)}, u32[]{:S(2)}) async-start(bf16[128,24,128]{2,1,0:T(8,128)(2,1)} %bitcast.11), calls=%async_computation | async-start | bytes 1572864 | tf_op jit(solution)/shard_map/all_to_all | solution.py:478
  25.4 14.3 %all-to-all-done = bf16[128,24,128]{2,1,0:T(8,128)(2,1)S(1)} async-done(((bf16[128,24,128]{2,1,0:T(8,128)(2,1)}), bf16[128,24,128]{2,1,0:T(8,128)(2,1)S(1)}, u32[]{:S(2)}, u32[]{:S(2)}) %all-to-all-start) | async-done | bytes 786464 | tf_op jit(solution)/shard_map/all_to_all | solution.py:478
  39.7 3.3 %shard_map.127 = (bf16[16,8,16,128]{3,2,1,0:T(8,128)(2,1)S(1)}, bf16[1,2,8,256]{3,2,1,0:T(8,128)(2,1)}) custom-call(f32[4,128]{1,0:T(4,128)S(1)} %pad_maximum_fusion.angles, bf16[16,8,24,128]{3,2,1,0:T(8,128)(2,1)S(1)} %bitcast.20, bf16[1,8,1024,128]{3,2,1,0:T(8,128)(2,1)} %keys.1, bf16[1,8,1024,128]{3,2,1,0:T(8,128)(2,1)} %values.1, ...), custom_call_target="tpu_custom_call" | custom-call | tf_op jit(solution)/shard_map/pallas_call | solution.py:193
  43.0 17.9 %all_to_all.10 = bf16[64,32,128]{2,1,0:T(8,128)(2,1)S(1)} all-to-all(bf16[64,32,128]{2,1,0:T(8,128)(2,1)S(1)} %bitcast.22), channel_id=1, replica_groups={{0,2,4,6,8,10,12,14,16,18,20,22,24,26,28,30,32,34,36,38,40,42,44,46,48,..., dimensions={0} | all-to-all | bytes 1048576 | tf_op jit(solution)/shard_map/all_to_all | solution.py:480
  64.2 2.4 %collective-permute-start.5 = (bf16[128,512]{1,0:T(8,128)(2,1)S(1)}, bf16[128,512]{1,0:T(8,128)(2,1)S(1)}, u32[]{:S(2)}, u32[]{:S(2)}) collective-permute-start(bf16[128,512]{1,0:T(8,128)(2,1)S(1)} %get-tuple-element.40), channel_id=1, source_target_pairs={{0,6},{1,7},{2,4},{3,5},{4,2},{5,3},{6,0},{7,1},{8,14},{9,15},{10,... | collective-permute-start | bytes 393224 | tf_op jit(solution)/shard_map/ppermute | solution.py:38
  66.6 2.4 %collective-permute-done.7.two = bf16[128,512]{1,0:T(8,128)(2,1)S(1)} collective-permute-done((bf16[128,512]{1,0:T(8,128)(2,1)S(1)}, bf16[128,512]{1,0:T(8,128)(2,1)S(1)}, u32[]{:S(2)}, u32[]{:S(2)}) %collective-permute-start.7) | collective-permute-done | bytes 131104 | tf_op jit(solution)/shard_map/ppermute | solution.py:38
  71.9 1.9 %shard_map.130 = (f32[32,512]{1,0:T(8,128)S(1)}, bf16[2,256,512]{2,1,0:T(8,128)(2,1)S(1)}, bf16[128,3712]{1,0:T(8,128)(2,1)S(1)}, bf16[128,3584]{1,0:T(8,128)(2,1)S(1)}) custom-call(s32[2]{0:T(128)S(1)} %pad_add_fusion.where, f32[128,512]{1,0:T(8,128)S(1)} %get-tuple-element.34.residual, bf16[128,512]{1,0:T(8,128)(2,1)S(1)} %collective-permute-done.3.far, ...), custom_call_target="tpu_custom_call" | custom-call | tf_op jit(solution)/shard_map/pallas_call | solution.py:342
  76.8 12.1 %collective-permute-done.10.refs_3_ = bf16[128,3584]{1,0:T(8,128)(2,1)S(1)} collective-permute-done((bf16[128,3584]{1,0:T(8,128)(2,1)S(1)}, bf16[128,3584]{1,0:T(8,128)(2,1)S(1)}, u32[]{:S(2)}, u32[]{:S(2)}) %collective-permute-start.10) | collective-permute-done | bytes 917536 | tf_op jit(solution)/shard_map/ppermute | solution.py:47
  90.9 8.5 %collective-permute-done.12.refs_3_ = bf16[64,3584]{1,0:T(8,128)(2,1)S(1)} collective-permute-done((bf16[64,3584]{1,0:T(8,128)(2,1)S(1)}, bf16[64,3584]{1,0:T(8,128)(2,1)S(1)}, u32[]{:S(2)}, u32[]{:S(2)}) %collective-permute-start.12) | collective-permute-done | bytes 458784 | tf_op jit(solution)/shard_map/ppermute | solution.py:47
  101.9 2.0 %collective-permute-start.15 = (bf16[16,7296]{1,0:T(8,128)(2,1)S(1)}, bf16[16,7296]{1,0:T(8,128)(2,1)S(1)}, u32[]{:S(2)}, u32[]{:S(2)}) collective-permute-start(bf16[16,7296]{1,0:T(8,128)(2,1)S(1)} %get-tuple-element.54), channel_id=1, source_target_pairs={{0,16},{1,65},{2,18},{3,67},{4,20},{5,69},{6,22},{7,71},{8,24},{9,... | collective-permute-start | bytes 700424 | tf_op jit(solution)/shard_map/ppermute | solution.py:47
  103.9 2.0 %collective-permute-done.13.one = bf16[16,7296]{1,0:T(8,128)(2,1)S(1)} collective-permute-done((bf16[16,7296]{1,0:T(8,128)(2,1)S(1)}, bf16[16,7296]{1,0:T(8,128)(2,1)S(1)}, u32[]{:S(2)}, u32[]{:S(2)}) %collective-permute-start.13) | collective-permute-done | bytes 233504 | tf_op jit(solution)/shard_map/ppermute | solution.py:47
  105.9 4.2 %collective-permute-done.14.three = bf16[16,7296]{1,0:T(8,128)(2,1)S(1)} collective-permute-done((bf16[16,7296]{1,0:T(8,128)(2,1)S(1)}, bf16[16,7296]{1,0:T(8,128)(2,1)S(1)}, u32[]{:S(2)}, u32[]{:S(2)}) %collective-permute-start.14) | collective-permute-done | bytes 233504 | tf_op jit(solution)/shard_map/ppermute | solution.py:47
  110.4 1.6 %collective-permute-start.18 = (bf16[16,3584]{1,0:T(8,128)(2,1)S(1)}, bf16[16,3584]{1,0:T(8,128)(2,1)S(1)}, u32[]{:S(2)}, u32[]{:S(2)}) collective-permute-start(bf16[16,3584]{1,0:T(8,128)(2,1)S(1)} %shard_map.134.refs_0_), channel_id=1, source_target_pairs={{0,24},{1,97},{2,26},{3,99},{4,28},{5,101},{6,30},{7,103},{8,16},{... | collective-permute-start | bytes 344072 | tf_op jit(solution)/shard_map/ppermute | solution.py:47
  112.8 1.7 %collective-permute-start.16 = (bf16[16,3584]{1,0:T(8,128)(2,1)S(1)}, bf16[16,3584]{1,0:T(8,128)(2,1)S(1)}, u32[]{:S(2)}, u32[]{:S(2)}) collective-permute-start(bf16[16,3584]{1,0:T(8,128)(2,1)S(1)} %shard_map.134.refs_0_), channel_id=1, source_target_pairs={{0,8},{1,33},{2,10},{3,35},{4,12},{5,37},{6,14},{7,39},{8,0},{9,41... | collective-permute-start | bytes 344072 | tf_op jit(solution)/shard_map/ppermute | solution.py:47
  114.5 1.9 %collective-permute-done.18.refs_3_ = bf16[16,3584]{1,0:T(8,128)(2,1)S(1)} collective-permute-done((bf16[16,3584]{1,0:T(8,128)(2,1)S(1)}, bf16[16,3584]{1,0:T(8,128)(2,1)S(1)}, u32[]{:S(2)}, u32[]{:S(2)}) %collective-permute-start.18) | collective-permute-done | bytes 114720 | tf_op jit(solution)/shard_map/ppermute | solution.py:47
  116.4 1.9 %collective-permute-done.17.refs_2_ = bf16[16,3584]{1,0:T(8,128)(2,1)S(1)} collective-permute-done((bf16[16,3584]{1,0:T(8,128)(2,1)S(1)}, bf16[16,3584]{1,0:T(8,128)(2,1)S(1)}, u32[]{:S(2)}, u32[]{:S(2)}) %collective-permute-start.17) | collective-permute-done | bytes 114720 | tf_op jit(solution)/shard_map/ppermute | solution.py:47
  118.6 1.8 %collective-permute-start.21 = (bf16[64,3584]{1,0:T(8,128)(2,1)S(1)}, bf16[64,3584]{1,0:T(8,128)(2,1)S(1)}, u32[]{:S(2)}, u32[]{:S(2)}) collective-permute-start(bf16[64,3584]{1,0:T(8,128)(2,1)S(1)} %shard_map.135.refs_0_), channel_id=1, source_target_pairs={{0,96},{1,25},{2,98},{3,27},{4,100},{5,29},{6,102},{7,31},{8,104},... | collective-permute-start | bytes 1376264 | tf_op jit(solution)/shard_map/ppermute | solution.py:47
  120.7 2.0 %collective-permute-start.19 = (bf16[64,3584]{1,0:T(8,128)(2,1)S(1)}, bf16[64,3584]{1,0:T(8,128)(2,1)S(1)}, u32[]{:S(2)}, u32[]{:S(2)}) collective-permute-start(bf16[64,3584]{1,0:T(8,128)(2,1)S(1)} %shard_map.135.refs_0_), channel_id=1, source_target_pairs={{0,32},{1,9},{2,34},{3,11},{4,36},{5,13},{6,38},{7,15},{8,40},{9,1... | collective-permute-start | bytes 1376264 | tf_op jit(solution)/shard_map/ppermute | solution.py:47
  122.7 10.5 %collective-permute-done.21.refs_3_ = bf16[64,3584]{1,0:T(8,128)(2,1)S(1)} collective-permute-done((bf16[64,3584]{1,0:T(8,128)(2,1)S(1)}, bf16[64,3584]{1,0:T(8,128)(2,1)S(1)}, u32[]{:S(2)}, u32[]{:S(2)}) %collective-permute-start.21) | collective-permute-done | bytes 458784 | tf_op jit(solution)/shard_map/ppermute | solution.py:47
  136.9 1.9 %collective-permute-start.23 = (bf16[32,512]{1,0:T(8,128)(2,1)S(1)}, bf16[32,512]{1,0:T(8,128)(2,1)S(1)}, u32[]{:S(2)}, u32[]{:S(2)}) collective-permute-start(bf16[32,512]{1,0:T(8,128)(2,1)S(1)} %get-tuple-element.58), channel_id=1, source_target_pairs={{0,4},{1,5},{2,6},{3,7},{4,0},{5,1},{6,2},{7,3},{8,12},{9,13},{10,... | collective-permute-start | bytes 98312 | tf_op jit(solution)/shard_map/ppermute | solution.py:38
  142.7 2.3 %collective-permute-done.25.three = bf16[32,512]{1,0:T(8,128)(2,1)S(1)} collective-permute-done((bf16[32,512]{1,0:T(8,128)(2,1)S(1)}, bf16[32,512]{1,0:T(8,128)(2,1)S(1)}, u32[]{:S(2)}, u32[]{:S(2)}) %collective-permute-start.25) | collective-permute-done | bytes 32800 | tf_op jit(solution)/shard_map/ppermute | solution.py:38
  (67 shorter events, 29.1 us)
Async XLA Ops:
  0.6 5.8 %collective-permute-start.2 = (f32[32,512]{1,0:T(8,128)}, f32[32,512]{1,0:T(8,128)S(1)}, u32[]{:S(2)}, u32[]{:S(2)}) collective-permute-start(f32[32,512]{1,0:T(8,128)} %bitcast.25), channel_id=1, source_target_pairs={{0,6},{1,7},{2,4},{3,5},{4,2},{5,3},{6,0},{7,1},{8,14},{9,15},{10,... | collective-permute-start | bytes 196616 | tf_op jit(solution)/shard_map/ppermute | solution.py:38
  3.6 6.0 %collective-permute-start.1 = (f32[32,512]{1,0:T(8,128)}, f32[32,512]{1,0:T(8,128)S(1)}, u32[]{:S(2)}, u32[]{:S(2)}) collective-permute-start(f32[32,512]{1,0:T(8,128)} %bitcast.26), channel_id=1, source_target_pairs={{0,4},{1,5},{2,6},{3,7},{4,0},{5,1},{6,2},{7,3},{8,12},{9,13},{10,... | collective-permute-start | bytes 196616 | tf_op jit(solution)/shard_map/ppermute | solution.py:38
  4.4 5.2 %collective-permute-start = (f32[32,512]{1,0:T(8,128)}, f32[32,512]{1,0:T(8,128)S(1)}, u32[]{:S(2)}, u32[]{:S(2)}) collective-permute-start(f32[32,512]{1,0:T(8,128)} %bitcast.27), channel_id=1, source_target_pairs={{0,2},{1,3},{2,0},{3,1},{4,6},{5,7},{6,4},{7,5},{8,10},{9,11},{10,... | collective-permute-start | bytes 196616 | tf_op jit(solution)/shard_map/ppermute | solution.py:38
  4.8 19.0 %collective-permute-start.4 = (bf16[1024,512]{1,0:T(8,128)(2,1)}, bf16[1024,512]{1,0:T(8,128)(2,1)}, u32[]{:S(2)}, u32[]{:S(2)}) collective-permute-start(bf16[1024,512]{1,0:T(8,128)(2,1)} %refs_0_.3), channel_id=1, source_target_pairs={{0,1},{1,0},{2,3},{3,2},{4,5},{5,4},{6,7},{7,6},{8,9},{9,8},{10,11... | collective-permute-start | bytes 3145736 | tf_op jit(solution)/shard_map/ppermute | solution.py:38
  13.2 26.5 %all-to-all-start = ((bf16[128,24,128]{2,1,0:T(8,128)(2,1)}), bf16[128,24,128]{2,1,0:T(8,128)(2,1)S(1)}, u32[]{:S(2)}, u32[]{:S(2)}) async-start(bf16[128,24,128]{2,1,0:T(8,128)(2,1)} %bitcast.11), calls=%async_computation | async-start | bytes 1572864 | tf_op jit(solution)/shard_map/all_to_all | solution.py:478
  62.5 6.5 %collective-permute-start.7 = (bf16[128,512]{1,0:T(8,128)(2,1)S(1)}, bf16[128,512]{1,0:T(8,128)(2,1)S(1)}, u32[]{:S(2)}, u32[]{:S(2)}) collective-permute-start(bf16[128,512]{1,0:T(8,128)(2,1)S(1)} %get-tuple-element.40), channel_id=1, source_target_pairs={{0,4},{1,5},{2,6},{3,7},{4,0},{5,1},{6,2},{7,3},{8,12},{9,13},{10,... | collective-permute-start | bytes 393224 | tf_op jit(solution)/shard_map/ppermute | solution.py:38
  63.6 5.4 %collective-permute-start.6 = (bf16[128,512]{1,0:T(8,128)(2,1)S(1)}, bf16[128,512]{1,0:T(8,128)(2,1)S(1)}, u32[]{:S(2)}, u32[]{:S(2)}) collective-permute-start(bf16[128,512]{1,0:T(8,128)(2,1)S(1)} %get-tuple-element.40), channel_id=1, source_target_pairs={{0,2},{1,3},{2,0},{3,1},{4,6},{5,7},{6,4},{7,5},{8,10},{9,11},{10,... | collective-permute-start | bytes 393224 | tf_op jit(solution)/shard_map/ppermute | solution.py:38
  64.2 6.2 %collective-permute-start.5 = (bf16[128,512]{1,0:T(8,128)(2,1)S(1)}, bf16[128,512]{1,0:T(8,128)(2,1)S(1)}, u32[]{:S(2)}, u32[]{:S(2)}) collective-permute-start(bf16[128,512]{1,0:T(8,128)(2,1)S(1)} %get-tuple-element.40), channel_id=1, source_target_pairs={{0,6},{1,7},{2,4},{3,5},{4,2},{5,3},{6,0},{7,1},{8,14},{9,15},{10,... | collective-permute-start | bytes 393224 | tf_op jit(solution)/shard_map/ppermute | solution.py:38
  73.8 15.1 %collective-permute-start.9 = (bf16[128,3712]{1,0:T(8,128)(2,1)S(1)}, bf16[128,3712]{1,0:T(8,128)(2,1)S(1)}, u32[]{:S(2)}, u32[]{:S(2)}) collective-permute-start(bf16[128,3712]{1,0:T(8,128)(2,1)S(1)} %get-tuple-element.44), channel_id=1, source_target_pairs={{0,32},{1,9},{2,34},{3,11},{4,36},{5,13},{6,38},{7,15},{8,40},{9,1... | collective-permute-start | bytes 2850824 | tf_op jit(solution)/shard_map/ppermute | solution.py:47
  74.3 14.6 %collective-permute-start.10 = (bf16[128,3584]{1,0:T(8,128)(2,1)S(1)}, bf16[128,3584]{1,0:T(8,128)(2,1)S(1)}, u32[]{:S(2)}, u32[]{:S(2)}) collective-permute-start(bf16[128,3584]{1,0:T(8,128)(2,1)S(1)} %get-tuple-element.46), channel_id=1, source_target_pairs={{0,96},{1,25},{2,98},{3,27},{4,100},{5,29},{6,102},{7,31},{8,104},... | collective-permute-start | bytes 2752520 | tf_op jit(solution)/shard_map/ppermute | solution.py:47
  89.5 9.9 %collective-permute-start.11 = (bf16[64,3712]{1,0:T(8,128)(2,1)S(1)}, bf16[64,3712]{1,0:T(8,128)(2,1)S(1)}, u32[]{:S(2)}, u32[]{:S(2)}) collective-permute-start(bf16[64,3712]{1,0:T(8,128)(2,1)S(1)} %get-tuple-element.48), channel_id=1, source_target_pairs={{0,96},{1,25},{2,98},{3,27},{4,100},{5,29},{6,102},{7,31},{8,104},... | collective-permute-start | bytes 1425416 | tf_op jit(solution)/shard_map/ppermute | solution.py:47
  90.9 8.5 %collective-permute-start.12 = (bf16[64,3584]{1,0:T(8,128)(2,1)S(1)}, bf16[64,3584]{1,0:T(8,128)(2,1)S(1)}, u32[]{:S(2)}, u32[]{:S(2)}) collective-permute-start(bf16[64,3584]{1,0:T(8,128)(2,1)S(1)} %get-tuple-element.50), channel_id=1, source_target_pairs={{0,32},{1,9},{2,34},{3,11},{4,36},{5,13},{6,38},{7,15},{8,40},{9,1... | collective-permute-start | bytes 1376264 | tf_op jit(solution)/shard_map/ppermute | solution.py:47
  99.7 6.1 %collective-permute-start.13 = (bf16[16,7296]{1,0:T(8,128)(2,1)S(1)}, bf16[16,7296]{1,0:T(8,128)(2,1)S(1)}, u32[]{:S(2)}, u32[]{:S(2)}) collective-permute-start(bf16[16,7296]{1,0:T(8,128)(2,1)S(1)} %get-tuple-element.52), channel_id=1, source_target_pairs={{0,8},{1,33},{2,10},{3,35},{4,12},{5,37},{6,14},{7,39},{8,0},{9,41... | collective-permute-start | bytes 700424 | tf_op jit(solution)/shard_map/ppermute | solution.py:47
  100.3 9.8 %collective-permute-start.14 = (bf16[16,7296]{1,0:T(8,128)(2,1)S(1)}, bf16[16,7296]{1,0:T(8,128)(2,1)S(1)}, u32[]{:S(2)}, u32[]{:S(2)}) collective-permute-start(bf16[16,7296]{1,0:T(8,128)(2,1)S(1)} %get-tuple-element.53), channel_id=1, source_target_pairs={{0,24},{1,97},{2,26},{3,99},{4,28},{5,101},{6,30},{7,103},{8,16},{... | collective-permute-start | bytes 700424 | tf_op jit(solution)/shard_map/ppermute | solution.py:47
  101.9 8.2 %collective-permute-start.15 = (bf16[16,7296]{1,0:T(8,128)(2,1)S(1)}, bf16[16,7296]{1,0:T(8,128)(2,1)S(1)}, u32[]{:S(2)}, u32[]{:S(2)}) collective-permute-start(bf16[16,7296]{1,0:T(8,128)(2,1)S(1)} %get-tuple-element.54), channel_id=1, source_target_pairs={{0,16},{1,65},{2,18},{3,67},{4,20},{5,69},{6,22},{7,71},{8,24},{9,... | collective-permute-start | bytes 700424 | tf_op jit(solution)/shard_map/ppermute | solution.py:47
  110.4 6.1 %collective-permute-start.18 = (bf16[16,3584]{1,0:T(8,128)(2,1)S(1)}, bf16[16,3584]{1,0:T(8,128)(2,1)S(1)}, u32[]{:S(2)}, u32[]{:S(2)}) collective-permute-start(bf16[16,3584]{1,0:T(8,128)(2,1)S(1)} %shard_map.134.refs_0_), channel_id=1, source_target_pairs={{0,24},{1,97},{2,26},{3,99},{4,28},{5,101},{6,30},{7,103},{8,16},{... | collective-permute-start | bytes 344072 | tf_op jit(solution)/shard_map/ppermute | solution.py:47
  112.0 6.3 %collective-permute-start.17 = (bf16[16,3584]{1,0:T(8,128)(2,1)S(1)}, bf16[16,3584]{1,0:T(8,128)(2,1)S(1)}, u32[]{:S(2)}, u32[]{:S(2)}) collective-permute-start(bf16[16,3584]{1,0:T(8,128)(2,1)S(1)} %shard_map.134.refs_0_), channel_id=1, source_target_pairs={{0,16},{1,65},{2,18},{3,67},{4,20},{5,69},{6,22},{7,71},{8,24},{9,... | collective-permute-start | bytes 344072 | tf_op jit(solution)/shard_map/ppermute | solution.py:47
  112.8 5.7 %collective-permute-start.16 = (bf16[16,3584]{1,0:T(8,128)(2,1)S(1)}, bf16[16,3584]{1,0:T(8,128)(2,1)S(1)}, u32[]{:S(2)}, u32[]{:S(2)}) collective-permute-start(bf16[16,3584]{1,0:T(8,128)(2,1)S(1)} %shard_map.134.refs_0_), channel_id=1, source_target_pairs={{0,8},{1,33},{2,10},{3,35},{4,12},{5,37},{6,14},{7,39},{8,0},{9,41... | collective-permute-start | bytes 344072 | tf_op jit(solution)/shard_map/ppermute | solution.py:47
  118.6 14.7 %collective-permute-start.21 = (bf16[64,3584]{1,0:T(8,128)(2,1)S(1)}, bf16[64,3584]{1,0:T(8,128)(2,1)S(1)}, u32[]{:S(2)}, u32[]{:S(2)}) collective-permute-start(bf16[64,3584]{1,0:T(8,128)(2,1)S(1)} %shard_map.135.refs_0_), channel_id=1, source_target_pairs={{0,96},{1,25},{2,98},{3,27},{4,100},{5,29},{6,102},{7,31},{8,104},... | collective-permute-start | bytes 1376264 | tf_op jit(solution)/shard_map/ppermute | solution.py:47
  120.4 12.8 %collective-permute-start.20 = (bf16[64,3584]{1,0:T(8,128)(2,1)S(1)}, bf16[64,3584]{1,0:T(8,128)(2,1)S(1)}, u32[]{:S(2)}, u32[]{:S(2)}) collective-permute-start(bf16[64,3584]{1,0:T(8,128)(2,1)S(1)} %shard_map.135.refs_0_), channel_id=1, source_target_pairs={{0,64},{1,17},{2,66},{3,19},{4,68},{5,21},{6,70},{7,23},{8,72},{9,... | collective-permute-start | bytes 1376264 | tf_op jit(solution)/shard_map/ppermute | solution.py:47
  120.7 13.4 %collective-permute-start.19 = (bf16[64,3584]{1,0:T(8,128)(2,1)S(1)}, bf16[64,3584]{1,0:T(8,128)(2,1)S(1)}, u32[]{:S(2)}, u32[]{:S(2)}) collective-permute-start(bf16[64,3584]{1,0:T(8,128)(2,1)S(1)} %shard_map.135.refs_0_), channel_id=1, source_target_pairs={{0,32},{1,9},{2,34},{3,11},{4,36},{5,13},{6,38},{7,15},{8,40},{9,1... | collective-permute-start | bytes 1376264 | tf_op jit(solution)/shard_map/ppermute | solution.py:47
  136.9 5.8 %collective-permute-start.23 = (bf16[32,512]{1,0:T(8,128)(2,1)S(1)}, bf16[32,512]{1,0:T(8,128)(2,1)S(1)}, u32[]{:S(2)}, u32[]{:S(2)}) collective-permute-start(bf16[32,512]{1,0:T(8,128)(2,1)S(1)} %get-tuple-element.58), channel_id=1, source_target_pairs={{0,4},{1,5},{2,6},{3,7},{4,0},{5,1},{6,2},{7,3},{8,12},{9,13},{10,... | collective-permute-start | bytes 98312 | tf_op jit(solution)/shard_map/ppermute | solution.py:38
  138.8 3.9 %collective-permute-start.24 = (bf16[32,512]{1,0:T(8,128)(2,1)S(1)}, bf16[32,512]{1,0:T(8,128)(2,1)S(1)}, u32[]{:S(2)}, u32[]{:S(2)}) collective-permute-start(bf16[32,512]{1,0:T(8,128)(2,1)S(1)} %get-tuple-element.59), channel_id=1, source_target_pairs={{0,2},{1,3},{2,0},{3,1},{4,6},{5,7},{6,4},{7,5},{8,10},{9,11},{10,... | collective-permute-start | bytes 98312 | tf_op jit(solution)/shard_map/ppermute | solution.py:38
  139.9 5.1 %collective-permute-start.25 = (bf16[32,512]{1,0:T(8,128)(2,1)S(1)}, bf16[32,512]{1,0:T(8,128)(2,1)S(1)}, u32[]{:S(2)}, u32[]{:S(2)}) collective-permute-start(bf16[32,512]{1,0:T(8,128)(2,1)S(1)} %get-tuple-element.60), channel_id=1, source_target_pairs={{0,6},{1,7},{2,4},{3,5},{4,2},{5,3},{6,0},{7,1},{8,14},{9,15},{10,... | collective-permute-start | bytes 98312 | tf_op jit(solution)/shard_map/ppermute | solution.py:38
  (7 other events, 129.3 us)

commit v5 on v4

--- a/solution.py
+++ b/solution.py
@@ -73,7 +73,7 @@
 
 
 def bring_body(count, *refs):
-    ins, outs, sems = refs[:count], refs[-1 - count : -1], refs[-1]
+    ins, outs, sems = refs[:count], refs[count:-1], refs[-1]
     fetches = [pltpu.make_async_copy(a, b, sems.at[i]) for i, (a, b) in enumerate(zip(ins, outs))]
     for fetch in fetches:
         fetch.start()
@@ -81,21 +81,21 @@
         fetch.wait()
 
 
-def bring(arrays, after):
+def bring(arrays):
     size = sum(a.size * a.dtype.itemsize for a in arrays)
     outs = pl.pallas_call(
         functools.partial(bring_body, len(arrays)),
         out_shape=tuple(pltpu.VMEM(a.shape, a.dtype) for a in arrays),
-        in_specs=[HBM] * len(arrays) + [ANY] * len(after),
+        in_specs=[HBM] * len(arrays),
         out_specs=(VM,) * len(arrays),
         scratch_shapes=[pltpu.SemaphoreType.DMA((len(arrays),))],
         compiler_params=pltpu.CompilerParams(vmem_limit_bytes=14 * MIB),
         cost_estimate=pl.CostEstimate(flops=0, bytes_accessed=2 * size, transcendentals=0),
-    )(*(hbm(a) for a in arrays), *after)
+    )(*(hbm(a) for a in arrays))
     return [pltpu.with_memory_space_constraint(a, pltpu.VMEM) for a in outs]
 
 
-def qkv_body(where, near, far, gain, held, out, lhs, rows):
+def qkv_body(where, near, far, gain, held, angles, twin, out, lhs, rows):
     mine = where[1]
     for flag, source in enumerate((near, far)):
         for k in range(4):
@@ -120,23 +120,20 @@
     out[...] = rows[...].astype(BF16)
 
 
-def qkv_partial(where, near, far, gain, weight):
+def qkv_partial(where, near, far, gain, weight, *order):
     return call(
         qkv_body,
         shaped((128 * 24, HD), BF16),
-        [SM, VM, VM, VM, VM],
+        [SM, VM, VM, VM, VM, ANY, ANY],
         [pltpu.VMEM((256, WIDTH), BF16), pltpu.VMEM((128 * 24, HD), F32)],
-    )(where, near, far, gain, weight)
+    )(where, near, far, gain, weight, *order)
 
 
 def turn(vectors, cosine, sine):
     return vectors * cosine + pltpu.roll(vectors, HD // 2, vectors.ndim - 1) * sine
 
 
-def attend_body(angles, received, keys, values, order, out, fresh, scores, held, sems):
-    fetches = [pltpu.make_async_copy(a.at[0], held.at[i], sems.at[i]) for i, a in enumerate((keys, values))]
-    for fetch in fetches:
-        fetch.start()
+def attend_body(angles, received, keys, values, out, fresh, scores):
     total = received[0].astype(F32)
     for i in range(1, NX):
         total = total + received[i].astype(F32)
@@ -160,10 +157,9 @@
         fresh[0, t, :, HD:] = value
     both = jnp.concatenate(queries, axis=1)
     both16 = both.astype(BF16)
-    fetches[0].wait()
     for g in range(KVH):
         scores[g * 16 : g * 16 + 16, :] = lax.dot_general(
-            both16[g], held[0, g], (((1,), (1,)), ((), ())), preferred_element_type=F32
+            both16[g], keys[0, g], (((1,), (1,)), ((), ())), preferred_element_type=F32
         )
     extra = []
     step = lax.broadcasted_iota(jnp.int32, (KVH, 16, 1), 1) // GQ
@@ -179,9 +175,8 @@
     share = 1.0 / (jnp.sum(cached, axis=1, keepdims=True) + extra[0] + extra[1])
     probs = (cached * share).astype(BF16)
     extra = [(value * share).astype(BF16).astype(F32).reshape(KVH, 16, 1) for value in extra]
-    fetches[1].wait()
     for g in range(KVH):
-        mixed = jnp.dot(probs[g * 16 : g * 16 + 16, :], held[1, g], preferred_element_type=F32)
+        mixed = jnp.dot(probs[g * 16 : g * 16 + 16, :], values[0, g], preferred_element_type=F32)
         for t in range(2):
             mixed = mixed + extra[t][g] * new_values[t][g : g + 1, :].astype(F32)
         mixed = mixed.astype(BF16)
@@ -189,17 +184,13 @@
             out[i, g] = mixed
 
 
-def attend(angles, received, keys, values, order):
+def attend(angles, received, keys, values):
     return call(
         attend_body,
         (shaped((NX, KVH, 16, HD), BF16), shaped((1, 2, KVH, 2 * HD), BF16)),
-        [VM, VM, HBM, HBM, ANY],
-        [
-            pltpu.VMEM((KVH * 16, CACHE), F32),
-            pltpu.VMEM((2, KVH, CACHE, HD), BF16),
-            pltpu.SemaphoreType.DMA((2,)),
-        ],
-    )(angles, received, hbm(keys), hbm(values), order)
+        [VM, VM, VM, VM],
+        [pltpu.VMEM((KVH * 16, CACHE), F32)],
+    )(angles, received, keys, values)
 
 
 def out_body(where, received, weight, twin, total, send, wide, lhs):
@@ -267,13 +258,13 @@
         scaled[rows, :] = (piece[...] * gain[...]).astype(BF16)
 
 
-def gather_rows(own, gain):
+def gather_rows(own, gain, *weights):
     pieces = [swap_gy(own, 2 * k) for k in (1, 2, 3)]
-    own, gain = bring((own, gain), ())
+    own, gain, *weights = bring((own, gain, *weights))
     residual, near = call(
         rows_body, (shaped((128, WIDTH), F32), shaped((128, WIDTH), BF16)), [VM] * 5
     )(own, *pieces, gain)
-    return residual, near, swap_gy(near, 1), gain
+    return residual, near, swap_gy(near, 1), gain, *weights
 
 
 def two_parts(squares):
@@ -348,34 +339,29 @@
     )(where, residual, far, attn_gain, gain, *sums, gate, up)
 
 
-def halve_body(*refs):
+def halve_body(send, *refs):
     ins, outs = refs[:4], refs[4:]
+    rows = slice(64, 128) if send else slice(0, 64)
     for f in range(2):
         keep, other = ins[2 * f], ins[2 * f + 1]
-        whole = keep[:, : 2 * HALF] + other[:, : 2 * HALF].astype(F32)
-        outs[2 * f][:, : 2 * HALF] = whole[:64]
-        outs[2 * f + 1][:, : 2 * HALF] = whole[64:].astype(BF16)
+        whole = keep[rows, : 2 * HALF] + other[rows, : 2 * HALF].astype(F32)
+        outs[f][:, : 2 * HALF] = whole.astype(outs[f].dtype)
         if f == 0:
-            squares = keep[:, 2 * HALF :] + one_part(other[:, 2 * HALF :])
-            outs[0][:, 2 * HALF :] = squares[:64]
-            outs[1][:, 2 * HALF :] = two_parts(squares[64:])
-
-
-def quarter_body(*refs):
+            squares = keep[rows, 2 * HALF :] + one_part(other[rows, 2 * HALF :])
+            outs[0][:, 2 * HALF :] = two_parts(squares) if send else squares
+
+
+def quarter_body(places, *refs):
     ins, outs = refs[:4], refs[4:]
-    start = 0
-    for f in range(2):
-        keep, other = ins[2 * f], ins[2 * f + 1]
-        whole = keep[:, : 2 * HALF] + other[:, : 2 * HALF].astype(F32)
-        for k, out in enumerate(outs):
-            rows = slice(gray(k) * 16, gray(k) * 16 + 16)
-            out[:, start : start + 2 * HALF] = whole[rows].astype(out.dtype)
-        if f == 0:
-            squares = keep[:, 2 * HALF :] + one_part(other[:, 2 * HALF :])
-            for k, out in enumerate(outs):
-                part = squares[gray(k) * 16 : gray(k) * 16 + 16]
-                out[:, 4 * HALF :] = part if k == 0 else two_parts(part)
-        start += 2 * HALF
+    for k, out in zip(places, outs):
+        rows = slice(gray(k) * 16, gray(k) * 16 + 16)
+        for f in range(2):
+            keep, other = ins[2 * f], ins[2 * f + 1]
+            start = f * 2 * HALF
+            whole = keep[rows, : 2 * HALF] + other[rows, : 2 * HALF].astype(F32)
+            out[:, start : start + 2 * HALF] = whole.astype(out.dtype)
+        squares = ins[0][rows, 2 * HALF :] + one_part(ins[1][rows, 2 * HALF :])
+        out[:, 4 * HALF :] = squares if k == 0 else two_parts(squares)
 
 
 def hidden_body(own, one, three, two, out):
@@ -393,15 +379,18 @@
 def hidden_units(lhs, gain, gate, up, sends):
     moved = [swap_by_core(sends[0], 4, 1), swap_by_core(sends[1], 12, 3)]
     keeps = call(keep_body, tuple(shaped((128, width), F32) for width in WIDTHS), [VM] * 4)(lhs, gain, gate, up)
-    halves = []
-    for width in WIDTHS:
-        halves += [shaped((64, width), F32), shaped((64, width), BF16)]
-    parts = call(halve_body, tuple(halves), [VM] * 4)(keeps[0], moved[0], keeps[1], moved[1])
-    moved = [swap_by_core(parts[1], 12, 3), swap_by_core(parts[3], 4, 1)]
+    parts = [keeps[0], moved[0], keeps[1], moved[1]]
+    sends = call(
+        functools.partial(halve_body, True), tuple(shaped((64, width), BF16) for width in WIDTHS), [VM] * 4
+    )(*parts)
+    moved = [swap_by_core(sends[0], 12, 3), swap_by_core(sends[1], 4, 1)]
+    keeps = call(
+        functools.partial(halve_body, False), tuple(shaped((64, width), F32) for width in WIDTHS), [VM] * 4
+    )(*parts)
+    parts = [keeps[0], moved[0], keeps[1], moved[1]]
     wide = 4 * HALF + HD
-    own, *sends = call(
-        quarter_body, (shaped((16, wide), F32),) + (shaped((16, wide), BF16),) * 3, [VM] * 4
-    )(parts[0], moved[0], parts[2], moved[1])
+    sends = call(functools.partial(quarter_body, (1, 2, 3)), (shaped((16, wide), BF16),) * 3, [VM] * 4)(*parts)
+    own = call(functools.partial(quarter_body, (0,)), shaped((16, wide), F32), [VM] * 4)(*parts)
     moved = [swap_by_core(sends[k - 1], k, 4 * k) for k in (1, 3, 2)]
     return call(hidden_body, shaped((16, UNITS), BF16), [VM] * 4)(own, *moved)
 
@@ -470,13 +459,13 @@
     attn_gain, ffn_gain = attn_gain.reshape(1, WIDTH), ffn_gain.reshape(1, WIDTH)
 
     twin = swap_gy(out_weight, 1)
-    residual, near, far, attn_gain = gather_rows(inputs.reshape(32, WIDTH), attn_gain)
-    (qkv_weight,) = bring((qkv_weight,), (near,))
-    partial = qkv_partial(where, near, far, attn_gain, qkv_weight)
-    out_weight, twin = bring((out_weight, twin), (partial,))
+    residual, near, far, attn_gain, qkv_weight, out_weight = gather_rows(
+        inputs.reshape(32, WIDTH), attn_gain, qkv_weight, out_weight
+    )
+    partial = qkv_partial(where, near, far, attn_gain, qkv_weight, angles, twin)
     partial = partial.reshape(128, 24, HD)
     received = lax.all_to_all(partial, ("gx", "gy"), 0, 0, tiled=True).reshape(NX, NY, 24, HD)
-    attended, new_kv = attend(angles, received, k_cache, v_cache, out_weight)
+    attended, new_kv = attend(angles, received, k_cache, v_cache)
     heads = lax.all_to_all(
         attended.reshape(64, 32, HD),
         ("gx", "gy"),

time: 146 us -> 143 us (0.979)
  blocking collectives: 17.9 us -> 44.1 us
  waiting for transfers between devices: 69.5 us -> 55.1 us
  starting transfers between devices: 38.7 us -> 28.5 us
  Pallas kernels: 17.5 us -> 12.8 us
    all_to_all x0 -> x1, blocking collectives: none -> 26.2 us  [per_device(): lax.all_to_all(partial, ('gx', 'gy'), 0, 0, tiled=True)]
    all_to_all x1 -> x0, waiting for transfers between devices: 14.3 us -> none  [per_device(): lax.all_to_all(partial, ('gx', 'gy'), 0, 0, tiled=True)]
    all_to_all x1 -> x0, starting transfers between devices: 10.2 us -> none  [per_device(): lax.all_to_all(partial, ('gx', 'gy'), 0, 0, tiled=True)]
    pallas_call x3 -> x1, Pallas kernels: 3.75 us -> 1.71 us  [bring(): pl.pallas_call(functools.partial(bring_body, len(arrays)), out_shape=tupl...]
    pallas_call x1, Pallas kernels: 3.26 us -> 1.62 us  [attend(): call(attend_body, (shaped((NX, KVH, 16, HD), BF16), shaped((1, 2, KVH, 2...]
  transfers between devices with their start and end apart: 27 -> 26, of which waited for: 18 -> 19; matrix products, arithmetic and copies ran while one was open for 0% -> 0% of each run, Pallas kernels for 5% -> 3%
where the time goes in v5:
time: 143 us
  waiting for transfers between devices  55.1 us (39%)
  blocking collectives  44.1 us (31%)
  starting transfers between devices  28.5 us (20%)
  Pallas kernels  12.8 us (9%)
  between operations  1.46 us (1%)
    ppermute x13, waiting for transfers between devices, swap_by_core(): return lax.ppermute(array, ('gx', 'gy'), pairs)  42 us
    all_to_all x1, blocking collectives, per_device(): lax.all_to_all(partial, ('gx', 'gy'), 0, 0, tiled=True)  26.2 us
    all_to_all x1, blocking collectives, per_device(): lax.all_to_all(attended.reshape(64, 32, HD), ('gx', 'gy'), 0, 0, axis_ind...  17.9 us
    ppermute x13, starting transfers between devices, swap_by_core(): return lax.ppermute(array, ('gx', 'gy'), pairs)  15.7 us
    ppermute x13, waiting for transfers between devices, swap_gy(): return lax.ppermute(array, 'gy', [(i, i ^ bits) for i in range(NY)])  13.1 us
    ppermute x13, starting transfers between devices, swap_gy(): return lax.ppermute(array, 'gy', [(i, i ^ bits) for i in range(NY)])  12.8 us
  transfers between devices with their start and end apart: 26, of which 19 were waited for; matrix products, arithmetic and copies ran while one was open for 0% of the time, Pallas kernels for 3%

profile of v5, /device:TPU:0, one launch (start us, length us, event | category | flops | bytes accessed | tf_op | source)
XLA Modules:
  0.0 142.6 jit_solution(1721513091155915130)
XLA Ops:
  0.6 2.9 %collective-permute-start.2 = (f32[32,512]{1,0:T(8,128)}, f32[32,512]{1,0:T(8,128)S(1)}, u32[]{:S(2)}, u32[]{:S(2)}) collective-permute-start(f32[32,512]{1,0:T(8,128)} %bitcast.26), channel_id=1, source_target_pairs={{0,6},{1,7},{2,4},{3,5},{4,2},{5,3},{6,0},{7,1},{8,14},{9,15},{10,... | collective-permute-start | bytes 196616 | tf_op jit(solution)/shard_map/ppermute | solution.py:38
  5.5 1.7 %shard_map.122 = (f32[32,512]{1,0:T(8,128)S(1)}, f32[1,512]{1,0:T(1,128)S(1)}, bf16[512,1280]{1,0:T(8,128)(2,1)S(1)}, bf16[1024,512]{1,0:T(8,128)(2,1)S(1)}) custom-call(f32[32,512]{1,0:T(8,128)} %bitcast.29, f32[1,512]{1,0:T(1,128)} %bitcast.31, bf16[512,1280]{1,0:T(8,128)(2,1)} %refs_2_.1, bf16[1024,512]{1,0:T(8,128)(2,1)} %refs_3_.1), custom_call_target="tpu_custom_call" | custom-call | bytes 4853760 | tf_op jit(solution)/shard_map/pallas_call | solution.py:86
  7.7 1.8 %collective-permute-done.1.two = f32[32,512]{1,0:T(8,128)S(1)} collective-permute-done((f32[32,512]{1,0:T(8,128)}, f32[32,512]{1,0:T(8,128)S(1)}, u32[]{:S(2)}, u32[]{:S(2)}) %collective-permute-start.1) | collective-permute-done | bytes 65568 | tf_op jit(solution)/shard_map/ppermute | solution.py:38
  12.2 26.2 %all_to_all.10 = bf16[128,24,128]{2,1,0:T(8,128)(2,1)S(1)} all-to-all(bf16[128,24,128]{2,1,0:T(8,128)(2,1)S(1)} %bitcast.21), channel_id=1, replica_groups=mesh['gx'=16,'gy'=8] {'gx','gy'}, dimensions={0} | all-to-all | bytes 1572864 | tf_op jit(solution)/shard_map/all_to_all | solution.py:467
  38.4 1.6 %shard_map.125 = (bf16[16,8,16,128]{3,2,1,0:T(8,128)(2,1)S(1)}, bf16[1,2,8,256]{3,2,1,0:T(8,128)(2,1)}) custom-call(f32[4,128]{1,0:T(4,128)S(1)} %pad_maximum_fusion.angles, bf16[16,8,24,128]{3,2,1,0:T(8,128)(2,1)S(1)} %bitcast.20, bf16[1,8,1024,128]{3,2,1,0:T(8,128)(2,1)S(1)} %copy-done.3, bf16[1,8,1024,128]{3,2,1,0:T(8,128)(2,1)S(1)} %copy-done.4), custom_call_target="tpu_custom_call" | custom-call | tf_op jit(solution)/shard_map/pallas_call | solution.py:188
  40.0 17.9 %all_to_all.11 = bf16[64,32,128]{2,1,0:T(8,128)(2,1)S(1)} all-to-all(bf16[64,32,128]{2,1,0:T(8,128)(2,1)S(1)} %bitcast.23), channel_id=1, replica_groups={{0,2,4,6,8,10,12,14,16,18,20,22,24,26,28,30,32,34,36,38,40,42,44,46,48,..., dimensions={0} | all-to-all | bytes 1048576 | tf_op jit(solution)/shard_map/all_to_all | solution.py:469
  57.9 1.6 %shard_map.126 = (f32[128,512]{1,0:T(8,128)S(1)}, bf16[128,512]{1,0:T(8,128)(2,1)S(1)}) custom-call(s32[2]{0:T(128)S(1)} %pad_add_fusion.where, bf16[2048,128]{1,0:T(8,128)(2,1)S(1)} %bitcast.22, bf16[1024,512]{1,0:T(8,128)(2,1)S(1)} %get-tuple-element.37.weight, bf16[1024,512]{1,0:T(8,128)(2,1)S(1)} %collective-permute-done.4.twin), custom_call_target="tpu_custom_call" | custom-call | tf_op jit(solution)/shard_map/pallas_call | solution.py:214
  61.3 2.4 %collective-permute-start.5 = (bf16[128,512]{1,0:T(8,128)(2,1)S(1)}, bf16[128,512]{1,0:T(8,128)(2,1)S(1)}, u32[]{:S(2)}, u32[]{:S(2)}) collective-permute-start(bf16[128,512]{1,0:T(8,128)(2,1)S(1)} %get-tuple-element.39), channel_id=1, source_target_pairs={{0,6},{1,7},{2,4},{3,5},{4,2},{5,3},{6,0},{7,1},{8,14},{9,15},{10,... | collective-permute-start | bytes 393224 | tf_op jit(solution)/shard_map/ppermute | solution.py:38
  63.7 2.4 %collective-permute-done.7.two = bf16[128,512]{1,0:T(8,128)(2,1)S(1)} collective-permute-done((bf16[128,512]{1,0:T(8,128)(2,1)S(1)}, bf16[128,512]{1,0:T(8,128)(2,1)S(1)}, u32[]{:S(2)}, u32[]{:S(2)}) %collective-permute-start.7) | collective-permute-done | bytes 131104 | tf_op jit(solution)/shard_map/ppermute | solution.py:38
  69.0 1.8 %shard_map.128 = (f32[32,512]{1,0:T(8,128)S(1)}, bf16[2,256,512]{2,1,0:T(8,128)(2,1)S(1)}, bf16[128,3712]{1,0:T(8,128)(2,1)S(1)}, bf16[128,3584]{1,0:T(8,128)(2,1)S(1)}) custom-call(s32[2]{0:T(128)S(1)} %pad_add_fusion.where, f32[128,512]{1,0:T(8,128)S(1)} %get-tuple-element.33.residual, bf16[128,512]{1,0:T(8,128)(2,1)S(1)} %collective-permute-done.3.far, ...), custom_call_target="tpu_custom_call" | custom-call | tf_op jit(solution)/shard_map/pallas_call | solution.py:333
  73.8 12.2 %collective-permute-done.10.refs_3_ = bf16[128,3584]{1,0:T(8,128)(2,1)S(1)} collective-permute-done((bf16[128,3584]{1,0:T(8,128)(2,1)S(1)}, bf16[128,3584]{1,0:T(8,128)(2,1)S(1)}, u32[]{:S(2)}, u32[]{:S(2)}) %collective-permute-start.10) | collective-permute-done | bytes 917536 | tf_op jit(solution)/shard_map/ppermute | solution.py:47
  87.9 8.3 %collective-permute-done.12.refs_3_ = bf16[64,3584]{1,0:T(8,128)(2,1)S(1)} collective-permute-done((bf16[64,3584]{1,0:T(8,128)(2,1)S(1)}, bf16[64,3584]{1,0:T(8,128)(2,1)S(1)}, u32[]{:S(2)}, u32[]{:S(2)}) %collective-permute-start.12) | collective-permute-done | bytes 458784 | tf_op jit(solution)/shard_map/ppermute | solution.py:47
  98.6 2.0 %collective-permute-start.15 = (bf16[16,7296]{1,0:T(8,128)(2,1)S(1)}, bf16[16,7296]{1,0:T(8,128)(2,1)S(1)}, u32[]{:S(2)}, u32[]{:S(2)}) collective-permute-start(bf16[16,7296]{1,0:T(8,128)(2,1)S(1)} %get-tuple-element.52), channel_id=1, source_target_pairs={{0,16},{1,65},{2,18},{3,67},{4,20},{5,69},{6,22},{7,71},{8,24},{9,... | collective-permute-start | bytes 700424 | tf_op jit(solution)/shard_map/ppermute | solution.py:47
  100.7 1.9 %collective-permute-done.13.one = bf16[16,7296]{1,0:T(8,128)(2,1)S(1)} collective-permute-done((bf16[16,7296]{1,0:T(8,128)(2,1)S(1)}, bf16[16,7296]{1,0:T(8,128)(2,1)S(1)}, u32[]{:S(2)}, u32[]{:S(2)}) %collective-permute-start.13) | collective-permute-done | bytes 233504 | tf_op jit(solution)/shard_map/ppermute | solution.py:47
  102.6 4.2 %collective-permute-done.14.three = bf16[16,7296]{1,0:T(8,128)(2,1)S(1)} collective-permute-done((bf16[16,7296]{1,0:T(8,128)(2,1)S(1)}, bf16[16,7296]{1,0:T(8,128)(2,1)S(1)}, u32[]{:S(2)}, u32[]{:S(2)}) %collective-permute-start.14) | collective-permute-done | bytes 233504 | tf_op jit(solution)/shard_map/ppermute | solution.py:47
  107.1 1.6 %collective-permute-start.18 = (bf16[16,3584]{1,0:T(8,128)(2,1)S(1)}, bf16[16,3584]{1,0:T(8,128)(2,1)S(1)}, u32[]{:S(2)}, u32[]{:S(2)}) collective-permute-start(bf16[16,3584]{1,0:T(8,128)(2,1)S(1)} %shard_map.134.refs_0_), channel_id=1, source_target_pairs={{0,24},{1,97},{2,26},{3,99},{4,28},{5,101},{6,30},{7,103},{8,16},{... | collective-permute-start | bytes 344072 | tf_op jit(solution)/shard_map/ppermute | solution.py:47
  109.5 1.7 %collective-permute-start.16 = (bf16[16,3584]{1,0:T(8,128)(2,1)S(1)}, bf16[16,3584]{1,0:T(8,128)(2,1)S(1)}, u32[]{:S(2)}, u32[]{:S(2)}) collective-permute-start(bf16[16,3584]{1,0:T(8,128)(2,1)S(1)} %shard_map.134.refs_0_), channel_id=1, source_target_pairs={{0,8},{1,33},{2,10},{3,35},{4,12},{5,37},{6,14},{7,39},{8,0},{9,41... | collective-permute-start | bytes 344072 | tf_op jit(solution)/shard_map/ppermute | solution.py:47
  111.2 1.9 %collective-permute-done.18.refs_3_ = bf16[16,3584]{1,0:T(8,128)(2,1)S(1)} collective-permute-done((bf16[16,3584]{1,0:T(8,128)(2,1)S(1)}, bf16[16,3584]{1,0:T(8,128)(2,1)S(1)}, u32[]{:S(2)}, u32[]{:S(2)}) %collective-permute-start.18) | collective-permute-done | bytes 114720 | tf_op jit(solution)/shard_map/ppermute | solution.py:47
  113.1 1.9 %collective-permute-done.17.refs_2_ = bf16[16,3584]{1,0:T(8,128)(2,1)S(1)} collective-permute-done((bf16[16,3584]{1,0:T(8,128)(2,1)S(1)}, bf16[16,3584]{1,0:T(8,128)(2,1)S(1)}, u32[]{:S(2)}, u32[]{:S(2)}) %collective-permute-start.17) | collective-permute-done | bytes 114720 | tf_op jit(solution)/shard_map/ppermute | solution.py:47
  115.3 2.0 %collective-permute-start.21 = (bf16[64,3584]{1,0:T(8,128)(2,1)S(1)}, bf16[64,3584]{1,0:T(8,128)(2,1)S(1)}, u32[]{:S(2)}, u32[]{:S(2)}) collective-permute-start(bf16[64,3584]{1,0:T(8,128)(2,1)S(1)} %shard_map.135.refs_0_), channel_id=1, source_target_pairs={{0,96},{1,25},{2,98},{3,27},{4,100},{5,29},{6,102},{7,31},{8,104},... | collective-permute-start | bytes 1376264 | tf_op jit(solution)/shard_map/ppermute | solution.py:47
  117.4 2.0 %collective-permute-start.19 = (bf16[64,3584]{1,0:T(8,128)(2,1)S(1)}, bf16[64,3584]{1,0:T(8,128)(2,1)S(1)}, u32[]{:S(2)}, u32[]{:S(2)}) collective-permute-start(bf16[64,3584]{1,0:T(8,128)(2,1)S(1)} %shard_map.135.refs_0_), channel_id=1, source_target_pairs={{0,32},{1,9},{2,34},{3,11},{4,36},{5,13},{6,38},{7,15},{8,40},{9,1... | collective-permute-start | bytes 1376264 | tf_op jit(solution)/shard_map/ppermute | solution.py:47
  119.4 10.5 %collective-permute-done.21.refs_3_ = bf16[64,3584]{1,0:T(8,128)(2,1)S(1)} collective-permute-done((bf16[64,3584]{1,0:T(8,128)(2,1)S(1)}, bf16[64,3584]{1,0:T(8,128)(2,1)S(1)}, u32[]{:S(2)}, u32[]{:S(2)}) %collective-permute-start.21) | collective-permute-done | bytes 458784 | tf_op jit(solution)/shard_map/ppermute | solution.py:47
  133.6 2.1 %collective-permute-start.23 = (bf16[32,512]{1,0:T(8,128)(2,1)S(1)}, bf16[32,512]{1,0:T(8,128)(2,1)S(1)}, u32[]{:S(2)}, u32[]{:S(2)}) collective-permute-start(bf16[32,512]{1,0:T(8,128)(2,1)S(1)} %get-tuple-element.56), channel_id=1, source_target_pairs={{0,4},{1,5},{2,6},{3,7},{4,0},{5,1},{6,2},{7,3},{8,12},{9,13},{10,... | collective-permute-start | bytes 98312 | tf_op jit(solution)/shard_map/ppermute | solution.py:38
  139.6 2.4 %collective-permute-done.25.three = bf16[32,512]{1,0:T(8,128)(2,1)S(1)} collective-permute-done((bf16[32,512]{1,0:T(8,128)(2,1)S(1)}, bf16[32,512]{1,0:T(8,128)(2,1)S(1)}, u32[]{:S(2)}, u32[]{:S(2)}) %collective-permute-start.25) | collective-permute-done | bytes 32800 | tf_op jit(solution)/shard_map/ppermute | solution.py:38
  (70 shorter events, 26.0 us)
Async XLA Ops:
  0.6 7.1 %collective-permute-start.2 = (f32[32,512]{1,0:T(8,128)}, f32[32,512]{1,0:T(8,128)S(1)}, u32[]{:S(2)}, u32[]{:S(2)}) collective-permute-start(f32[32,512]{1,0:T(8,128)} %bitcast.26), channel_id=1, source_target_pairs={{0,6},{1,7},{2,4},{3,5},{4,2},{5,3},{6,0},{7,1},{8,14},{9,15},{10,... | collective-permute-start | bytes 196616 | tf_op jit(solution)/shard_map/ppermute | solution.py:38
  3.6 6.0 %collective-permute-start.1 = (f32[32,512]{1,0:T(8,128)}, f32[32,512]{1,0:T(8,128)S(1)}, u32[]{:S(2)}, u32[]{:S(2)}) collective-permute-start(f32[32,512]{1,0:T(8,128)} %bitcast.27), channel_id=1, source_target_pairs={{0,4},{1,5},{2,6},{3,7},{4,0},{5,1},{6,2},{7,3},{8,12},{9,13},{10,... | collective-permute-start | bytes 196616 | tf_op jit(solution)/shard_map/ppermute | solution.py:38
  4.4 5.2 %collective-permute-start = (f32[32,512]{1,0:T(8,128)}, f32[32,512]{1,0:T(8,128)S(1)}, u32[]{:S(2)}, u32[]{:S(2)}) collective-permute-start(f32[32,512]{1,0:T(8,128)} %bitcast.28), channel_id=1, source_target_pairs={{0,2},{1,3},{2,0},{3,1},{4,6},{5,7},{6,4},{7,5},{8,10},{9,11},{10,... | collective-permute-start | bytes 196616 | tf_op jit(solution)/shard_map/ppermute | solution.py:38
  4.8 6.2 %collective-permute-start.4 = (bf16[1024,512]{1,0:T(8,128)(2,1)}, bf16[1024,512]{1,0:T(8,128)(2,1)S(1)}, u32[]{:S(2)}, u32[]{:S(2)}) collective-permute-start(bf16[1024,512]{1,0:T(8,128)(2,1)} %refs_3_.1), channel_id=1, source_target_pairs={{0,1},{1,0},{2,3},{3,2},{4,5},{5,4},{6,7},{7,6},{8,9},{9,8},{10,11... | collective-permute-start | bytes 3145736 | tf_op jit(solution)/shard_map/ppermute | solution.py:38
  9.6 1.4 %collective-permute-start.3 = (bf16[128,512]{1,0:T(8,128)(2,1)S(1)}, bf16[128,512]{1,0:T(8,128)(2,1)S(1)}, u32[]{:S(2)}, u32[]{:S(2)}) collective-permute-start(bf16[128,512]{1,0:T(8,128)(2,1)S(1)} %get-tuple-element.34.near), channel_id=1, source_target_pairs={{0,1},{1,0},{2,3},{3,2},{4,5},{5,4},{6,7},{7,6},{8,9},{9,8},{10,11... | collective-permute-start | bytes 393224 | tf_op jit(solution)/shard_map/ppermute | solution.py:38
  59.5 6.5 %collective-permute-start.7 = (bf16[128,512]{1,0:T(8,128)(2,1)S(1)}, bf16[128,512]{1,0:T(8,128)(2,1)S(1)}, u32[]{:S(2)}, u32[]{:S(2)}) collective-permute-start(bf16[128,512]{1,0:T(8,128)(2,1)S(1)} %get-tuple-element.39), channel_id=1, source_target_pairs={{0,4},{1,5},{2,6},{3,7},{4,0},{5,1},{6,2},{7,3},{8,12},{9,13},{10,... | collective-permute-start | bytes 393224 | tf_op jit(solution)/shard_map/ppermute | solution.py:38
  60.7 5.4 %collective-permute-start.6 = (bf16[128,512]{1,0:T(8,128)(2,1)S(1)}, bf16[128,512]{1,0:T(8,128)(2,1)S(1)}, u32[]{:S(2)}, u32[]{:S(2)}) collective-permute-start(bf16[128,512]{1,0:T(8,128)(2,1)S(1)} %get-tuple-element.39), channel_id=1, source_target_pairs={{0,2},{1,3},{2,0},{3,1},{4,6},{5,7},{6,4},{7,5},{8,10},{9,11},{10,... | collective-permute-start | bytes 393224 | tf_op jit(solution)/shard_map/ppermute | solution.py:38
  61.3 6.2 %collective-permute-start.5 = (bf16[128,512]{1,0:T(8,128)(2,1)S(1)}, bf16[128,512]{1,0:T(8,128)(2,1)S(1)}, u32[]{:S(2)}, u32[]{:S(2)}) collective-permute-start(bf16[128,512]{1,0:T(8,128)(2,1)S(1)} %get-tuple-element.39), channel_id=1, source_target_pairs={{0,6},{1,7},{2,4},{3,5},{4,2},{5,3},{6,0},{7,1},{8,14},{9,15},{10,... | collective-permute-start | bytes 393224 | tf_op jit(solution)/shard_map/ppermute | solution.py:38
  70.8 15.1 %collective-permute-start.9 = (bf16[128,3712]{1,0:T(8,128)(2,1)S(1)}, bf16[128,3712]{1,0:T(8,128)(2,1)S(1)}, u32[]{:S(2)}, u32[]{:S(2)}) collective-permute-start(bf16[128,3712]{1,0:T(8,128)(2,1)S(1)} %get-tuple-element.43), channel_id=1, source_target_pairs={{0,32},{1,9},{2,34},{3,11},{4,36},{5,13},{6,38},{7,15},{8,40},{9,1... | collective-permute-start | bytes 2850824 | tf_op jit(solution)/shard_map/ppermute | solution.py:47
  71.3 14.6 %collective-permute-start.10 = (bf16[128,3584]{1,0:T(8,128)(2,1)S(1)}, bf16[128,3584]{1,0:T(8,128)(2,1)S(1)}, u32[]{:S(2)}, u32[]{:S(2)}) collective-permute-start(bf16[128,3584]{1,0:T(8,128)(2,1)S(1)} %get-tuple-element.45), channel_id=1, source_target_pairs={{0,96},{1,25},{2,98},{3,27},{4,100},{5,29},{6,102},{7,31},{8,104},... | collective-permute-start | bytes 2752520 | tf_op jit(solution)/shard_map/ppermute | solution.py:47
  86.3 9.9 %collective-permute-start.11 = (bf16[64,3712]{1,0:T(8,128)(2,1)S(1)}, bf16[64,3712]{1,0:T(8,128)(2,1)S(1)}, u32[]{:S(2)}, u32[]{:S(2)}) collective-permute-start(bf16[64,3712]{1,0:T(8,128)(2,1)S(1)} %get-tuple-element.47), channel_id=1, source_target_pairs={{0,96},{1,25},{2,98},{3,27},{4,100},{5,29},{6,102},{7,31},{8,104},... | collective-permute-start | bytes 1425416 | tf_op jit(solution)/shard_map/ppermute | solution.py:47
  87.7 8.5 %collective-permute-start.12 = (bf16[64,3584]{1,0:T(8,128)(2,1)S(1)}, bf16[64,3584]{1,0:T(8,128)(2,1)S(1)}, u32[]{:S(2)}, u32[]{:S(2)}) collective-permute-start(bf16[64,3584]{1,0:T(8,128)(2,1)S(1)} %get-tuple-element.49), channel_id=1, source_target_pairs={{0,32},{1,9},{2,34},{3,11},{4,36},{5,13},{6,38},{7,15},{8,40},{9,1... | collective-permute-start | bytes 1376264 | tf_op jit(solution)/shard_map/ppermute | solution.py:47
  96.4 6.1 %collective-permute-start.13 = (bf16[16,7296]{1,0:T(8,128)(2,1)S(1)}, bf16[16,7296]{1,0:T(8,128)(2,1)S(1)}, u32[]{:S(2)}, u32[]{:S(2)}) collective-permute-start(bf16[16,7296]{1,0:T(8,128)(2,1)S(1)} %get-tuple-element.50), channel_id=1, source_target_pairs={{0,8},{1,33},{2,10},{3,35},{4,12},{5,37},{6,14},{7,39},{8,0},{9,41... | collective-permute-start | bytes 700424 | tf_op jit(solution)/shard_map/ppermute | solution.py:47
  97.0 9.8 %collective-permute-start.14 = (bf16[16,7296]{1,0:T(8,128)(2,1)S(1)}, bf16[16,7296]{1,0:T(8,128)(2,1)S(1)}, u32[]{:S(2)}, u32[]{:S(2)}) collective-permute-start(bf16[16,7296]{1,0:T(8,128)(2,1)S(1)} %get-tuple-element.51), channel_id=1, source_target_pairs={{0,24},{1,97},{2,26},{3,99},{4,28},{5,101},{6,30},{7,103},{8,16},{... | collective-permute-start | bytes 700424 | tf_op jit(solution)/shard_map/ppermute | solution.py:47
  98.6 8.2 %collective-permute-start.15 = (bf16[16,7296]{1,0:T(8,128)(2,1)S(1)}, bf16[16,7296]{1,0:T(8,128)(2,1)S(1)}, u32[]{:S(2)}, u32[]{:S(2)}) collective-permute-start(bf16[16,7296]{1,0:T(8,128)(2,1)S(1)} %get-tuple-element.52), channel_id=1, source_target_pairs={{0,16},{1,65},{2,18},{3,67},{4,20},{5,69},{6,22},{7,71},{8,24},{9,... | collective-permute-start | bytes 700424 | tf_op jit(solution)/shard_map/ppermute | solution.py:47
  107.1 6.1 %collective-permute-start.18 = (bf16[16,3584]{1,0:T(8,128)(2,1)S(1)}, bf16[16,3584]{1,0:T(8,128)(2,1)S(1)}, u32[]{:S(2)}, u32[]{:S(2)}) collective-permute-start(bf16[16,3584]{1,0:T(8,128)(2,1)S(1)} %shard_map.134.refs_0_), channel_id=1, source_target_pairs={{0,24},{1,97},{2,26},{3,99},{4,28},{5,101},{6,30},{7,103},{8,16},{... | collective-permute-start | bytes 344072 | tf_op jit(solution)/shard_map/ppermute | solution.py:47
  108.7 6.3 %collective-permute-start.17 = (bf16[16,3584]{1,0:T(8,128)(2,1)S(1)}, bf16[16,3584]{1,0:T(8,128)(2,1)S(1)}, u32[]{:S(2)}, u32[]{:S(2)}) collective-permute-start(bf16[16,3584]{1,0:T(8,128)(2,1)S(1)} %shard_map.134.refs_0_), channel_id=1, source_target_pairs={{0,16},{1,65},{2,18},{3,67},{4,20},{5,69},{6,22},{7,71},{8,24},{9,... | collective-permute-start | bytes 344072 | tf_op jit(solution)/shard_map/ppermute | solution.py:47
  109.5 5.7 %collective-permute-start.16 = (bf16[16,3584]{1,0:T(8,128)(2,1)S(1)}, bf16[16,3584]{1,0:T(8,128)(2,1)S(1)}, u32[]{:S(2)}, u32[]{:S(2)}) collective-permute-start(bf16[16,3584]{1,0:T(8,128)(2,1)S(1)} %shard_map.134.refs_0_), channel_id=1, source_target_pairs={{0,8},{1,33},{2,10},{3,35},{4,12},{5,37},{6,14},{7,39},{8,0},{9,41... | collective-permute-start | bytes 344072 | tf_op jit(solution)/shard_map/ppermute | solution.py:47
  115.3 14.7 %collective-permute-start.21 = (bf16[64,3584]{1,0:T(8,128)(2,1)S(1)}, bf16[64,3584]{1,0:T(8,128)(2,1)S(1)}, u32[]{:S(2)}, u32[]{:S(2)}) collective-permute-start(bf16[64,3584]{1,0:T(8,128)(2,1)S(1)} %shard_map.135.refs_0_), channel_id=1, source_target_pairs={{0,96},{1,25},{2,98},{3,27},{4,100},{5,29},{6,102},{7,31},{8,104},... | collective-permute-start | bytes 1376264 | tf_op jit(solution)/shard_map/ppermute | solution.py:47
  117.2 12.7 %collective-permute-start.20 = (bf16[64,3584]{1,0:T(8,128)(2,1)S(1)}, bf16[64,3584]{1,0:T(8,128)(2,1)S(1)}, u32[]{:S(2)}, u32[]{:S(2)}) collective-permute-start(bf16[64,3584]{1,0:T(8,128)(2,1)S(1)} %shard_map.135.refs_0_), channel_id=1, source_target_pairs={{0,64},{1,17},{2,66},{3,19},{4,68},{5,21},{6,70},{7,23},{8,72},{9,... | collective-permute-start | bytes 1376264 | tf_op jit(solution)/shard_map/ppermute | solution.py:47
  117.4 13.4 %collective-permute-start.19 = (bf16[64,3584]{1,0:T(8,128)(2,1)S(1)}, bf16[64,3584]{1,0:T(8,128)(2,1)S(1)}, u32[]{:S(2)}, u32[]{:S(2)}) collective-permute-start(bf16[64,3584]{1,0:T(8,128)(2,1)S(1)} %shard_map.135.refs_0_), channel_id=1, source_target_pairs={{0,32},{1,9},{2,34},{3,11},{4,36},{5,13},{6,38},{7,15},{8,40},{9,1... | collective-permute-start | bytes 1376264 | tf_op jit(solution)/shard_map/ppermute | solution.py:47
  133.6 5.6 %collective-permute-start.23 = (bf16[32,512]{1,0:T(8,128)(2,1)S(1)}, bf16[32,512]{1,0:T(8,128)(2,1)S(1)}, u32[]{:S(2)}, u32[]{:S(2)}) collective-permute-start(bf16[32,512]{1,0:T(8,128)(2,1)S(1)} %get-tuple-element.56), channel_id=1, source_target_pairs={{0,4},{1,5},{2,6},{3,7},{4,0},{5,1},{6,2},{7,3},{8,12},{9,13},{10,... | collective-permute-start | bytes 98312 | tf_op jit(solution)/shard_map/ppermute | solution.py:38
  135.7 3.9 %collective-permute-start.24 = (bf16[32,512]{1,0:T(8,128)(2,1)S(1)}, bf16[32,512]{1,0:T(8,128)(2,1)S(1)}, u32[]{:S(2)}, u32[]{:S(2)}) collective-permute-start(bf16[32,512]{1,0:T(8,128)(2,1)S(1)} %get-tuple-element.57), channel_id=1, source_target_pairs={{0,2},{1,3},{2,0},{3,1},{4,6},{5,7},{6,4},{7,5},{8,10},{9,11},{10,... | collective-permute-start | bytes 98312 | tf_op jit(solution)/shard_map/ppermute | solution.py:38
  136.9 5.1 %collective-permute-start.25 = (bf16[32,512]{1,0:T(8,128)(2,1)S(1)}, bf16[32,512]{1,0:T(8,128)(2,1)S(1)}, u32[]{:S(2)}, u32[]{:S(2)}) collective-permute-start(bf16[32,512]{1,0:T(8,128)(2,1)S(1)} %get-tuple-element.58), channel_id=1, source_target_pairs={{0,6},{1,7},{2,4},{3,5},{4,2},{5,3},{6,0},{7,1},{8,14},{9,15},{10,... | collective-permute-start | bytes 98312 | tf_op jit(solution)/shard_map/ppermute | solution.py:38
  (8 other events, 178.4 us)

commit v6 on v5

--- a/solution.py
+++ b/solution.py
@@ -95,38 +95,44 @@
     return [pltpu.with_memory_space_constraint(a, pltpu.VMEM) for a in outs]
 
 
-def qkv_body(where, near, far, gain, held, angles, twin, out, lhs, rows):
-    mine = where[1]
-    for flag, source in enumerate((near, far)):
-        for k in range(4):
-            block = mine ^ (2 * k + flag)
-            for t in range(2):
-                start = pl.multiple_of(t * 128 + block * 16, 16)
-                lhs[pl.ds(start, 16), :] = source[k * 32 + t * 16 : k * 32 + t * 16 + 16, :]
-    plain = lhs[...].astype(F32) / gain[...]
-    squares = jnp.sum(plain * plain, axis=1, keepdims=True)
-    for t in range(2):
-        whole = jnp.broadcast_to(squares[t * 128 : t * 128 + 128], (128, HD))
-        high = whole.astype(BF16).astype(F32)
-        rows[pl.ds(20 + 2 * t, 128, stride=24), :] = high
-        rows[pl.ds(21 + 2 * t, 128, stride=24), :] = whole - high
+def qkv_rows(source, gain, weight, rows):
+    plain = source[...].astype(F32) / gain[...]
+    squares = jnp.broadcast_to(jnp.sum(plain * plain, axis=1, keepdims=True), (128, HD))
+    high = squares.astype(BF16).astype(F32)
+    places = [(k, t, k * 32 + t * 16) for k in range(4) for t in range(2)]
+    for k, t, start in places:
+        rows[pl.ds(k * 384 + 20 + 2 * t, 16, stride=24), :] = high[start : start + 16]
+        rows[pl.ds(k * 384 + 21 + 2 * t, 16, stride=24), :] = squares[start : start + 16] - high[start : start + 16]
     for pair in range(5):
-        part = jnp.dot(lhs[...], held[:, pair * 256 : pair * 256 + 256], preferred_element_type=F32)
+        part = jnp.dot(source[...], weight[:, pair * 256 : pair * 256 + 256], preferred_element_type=F32)
         for j in (2 * pair, 2 * pair + 1):
-            for t in range(2):
+            column = (j - 2 * pair) * HD
+            for k, t, start in places:
                 place = t * 8 + j if j < GQ else 16 + (j - GQ) * 2 + t
-                column = (j - 2 * pair) * HD
-                rows[pl.ds(place, 128, stride=24), :] = part[t * 128 : t * 128 + 128, column : column + HD]
+                rows[pl.ds(k * 384 + place, 16, stride=24), :] = part[start : start + 16, column : column + HD]
+
+
+def near_body(near, gain, weight, out, rows):
+    qkv_rows(near, gain, weight, rows)
     out[...] = rows[...].astype(BF16)
 
 
+def qkv_body(where, earlier, far, gain, weight, angles, twin, out, rows):
+    qkv_rows(far, gain, weight, rows)
+    for k in range(4):
+        part = slice(k * 384, k * 384 + 384)
+        start = pl.multiple_of((where[1] ^ (2 * k)) * 384, 16)
+        out[pl.ds(start, 384), :] = earlier[part, :]
+        start = pl.multiple_of((where[1] ^ (2 * k + 1)) * 384, 16)
+        out[pl.ds(start, 384), :] = rows[part, :].astype(BF16)
+
+
 def qkv_partial(where, near, far, gain, weight, *order):
+    scratch = [pltpu.VMEM((64 * 24, HD), F32)]
+    earlier = call(near_body, shaped((64 * 24, HD), BF16), [VM] * 3, scratch)(near, gain, weight)
     return call(
-        qkv_body,
-        shaped((128 * 24, HD), BF16),
-        [SM, VM, VM, VM, VM, ANY, ANY],
-        [pltpu.VMEM((256, WIDTH), BF16), pltpu.VMEM((128 * 24, HD), F32)],
-    )(where, near, far, gain, weight, *order)
+        qkv_body, shaped((128 * 24, HD), BF16), [SM] + [VM] * 4 + [ANY] * 2, scratch
+    )(where, earlier, far, gain, weight, *order)
 
 
 def turn(vectors, cosine, sine):
@@ -364,7 +370,7 @@
         out[:, 4 * HALF :] = squares if k == 0 else two_parts(squares)
 
 
-def hidden_body(own, one, three, two, out):
+def hidden_body(own, two, one, three, out):
     others = (one, two, three)
     squares = own[:, 4 * HALF :] + sum(one_part(other[:, 4 * HALF :]) for other in others)
     scale = lax.rsqrt(squares / D + EPSILON)[:, :1]
@@ -391,7 +397,7 @@
     wide = 4 * HALF + HD
     sends = call(functools.partial(quarter_body, (1, 2, 3)), (shaped((16, wide), BF16),) * 3, [VM] * 4)(*parts)
     own = call(functools.partial(quarter_body, (0,)), shaped((16, wide), F32), [VM] * 4)(*parts)
-    moved = [swap_by_core(sends[k - 1], k, 4 * k) for k in (1, 3, 2)]
+    moved = [swap_by_core(sends[k - 1], k, 4 * k) for k in (2, 1, 3)]
     return call(hidden_body, shaped((16, UNITS), BF16), [VM] * 4)(own, *moved)
 
 
@@ -402,8 +408,8 @@
         out[k * rows : k * rows + rows, :] = piece[...]
 
 
-def down_body(where, *refs):
-    pieces, (weight, send, lhs) = refs[:4], refs[4:]
+def down_body(where, own, three, one, two, weight, send, lhs):
+    pieces = (own, one, two, three)
     core = where[1] & 1
     for m in range(4):
         for k in range(4):
@@ -422,7 +428,7 @@
 def down_partial(where, units, weight):
     pieces = [units] + [swap_by_core(units, k, 4 * k) for k in (1, 2, 3)]
     near = call(stack_body, shaped((64, UNITS), BF16), [VM] * 4)(*pieces)
-    pieces = [near] + [swap_by_core(near, 4 * k, k) for k in (1, 2, 3)]
+    pieces = [near] + [swap_by_core(near, 4 * k, k) for k in (3, 1, 2)]
     send, lhs = call(
         down_body, (shaped((128, WIDTH), BF16), shaped((256, UNITS), BF16)), [SM] + [VM] * 5
     )(where, *pieces, weight)

time: 143 us -> 143 us (level)
  transfers between devices with their start and end apart: 26 -> 26, of which waited for: 19 -> 20; matrix products, arithmetic and copies ran while one was open for 0% -> 0% of each run, Pallas kernels for 3% -> 3%
where the time goes in v6:
time: 143 us
  waiting for transfers between devices  54.8 us (38%)
  blocking collectives  44.1 us (31%)
  starting transfers between devices  28.5 us (20%)
  Pallas kernels  13 us (9%)
  between operations  1.48 us (1%)
    ppermute x13, waiting for transfers between devices, swap_by_core(): return lax.ppermute(array, ('gx', 'gy'), pairs)  42 us
    all_to_all x1, blocking collectives, per_device(): lax.all_to_all(partial, ('gx', 'gy'), 0, 0, tiled=True)  26.2 us
    all_to_all x1, blocking collectives, per_device(): lax.all_to_all(attended.reshape(64, 32, HD), ('gx', 'gy'), 0, 0, axis_ind...  17.9 us
    ppermute x13, starting transfers between devices, swap_by_core(): return lax.ppermute(array, ('gx', 'gy'), pairs)  15.7 us
    ppermute x13, starting transfers between devices, swap_gy(): return lax.ppermute(array, 'gy', [(i, i ^ bits) for i in range(NY)])  12.8 us
    ppermute x13, waiting for transfers between devices, swap_gy(): return lax.ppermute(array, 'gy', [(i, i ^ bits) for i in range(NY)])  12.7 us
  transfers between devices with their start and end apart: 26, of which 20 were waited for; matrix products, arithmetic and copies ran while one was open for 0% of the time, Pallas kernels for 3%

profile of v6, /device:TPU:0, one launch (start us, length us, event | category | flops | bytes accessed | tf_op | source)
XLA Modules:
  0.0 142.5 jit_solution(16680314667661141598)
XLA Ops:
  0.6 2.9 %collective-permute-start.2 = (f32[32,512]{1,0:T(8,128)}, f32[32,512]{1,0:T(8,128)S(1)}, u32[]{:S(2)}, u32[]{:S(2)}) collective-permute-start(f32[32,512]{1,0:T(8,128)} %bitcast.26), channel_id=1, source_target_pairs={{0,6},{1,7},{2,4},{3,5},{4,2},{5,3},{6,0},{7,1},{8,14},{9,15},{10,... | collective-permute-start | bytes 196616 | tf_op jit(solution)/shard_map/ppermute | solution.py:38
  5.5 1.7 %shard_map.122 = (f32[32,512]{1,0:T(8,128)S(1)}, f32[1,512]{1,0:T(1,128)S(1)}, bf16[512,1280]{1,0:T(8,128)(2,1)S(1)}, bf16[1024,512]{1,0:T(8,128)(2,1)S(1)}) custom-call(f32[32,512]{1,0:T(8,128)} %bitcast.29, f32[1,512]{1,0:T(1,128)} %bitcast.31, bf16[512,1280]{1,0:T(8,128)(2,1)} %refs_2_.1, bf16[1024,512]{1,0:T(8,128)(2,1)} %refs_3_.1), custom_call_target="tpu_custom_call" | custom-call | bytes 4853760 | tf_op jit(solution)/shard_map/pallas_call | solution.py:86
  7.7 1.8 %collective-permute-done.1.two = f32[32,512]{1,0:T(8,128)S(1)} collective-permute-done((f32[32,512]{1,0:T(8,128)}, f32[32,512]{1,0:T(8,128)S(1)}, u32[]{:S(2)}, u32[]{:S(2)}) %collective-permute-start.1) | collective-permute-done | bytes 65568 | tf_op jit(solution)/shard_map/ppermute | solution.py:38
  12.0 26.2 %all_to_all.10 = bf16[128,24,128]{2,1,0:T(8,128)(2,1)S(1)} all-to-all(bf16[128,24,128]{2,1,0:T(8,128)(2,1)S(1)} %bitcast.21), channel_id=1, replica_groups=mesh['gx'=16,'gy'=8] {'gx','gy'}, dimensions={0} | all-to-all | bytes 1572864 | tf_op jit(solution)/shard_map/all_to_all | solution.py:473
  38.2 1.6 %shard_map.126 = (bf16[16,8,16,128]{3,2,1,0:T(8,128)(2,1)S(1)}, bf16[1,2,8,256]{3,2,1,0:T(8,128)(2,1)}) custom-call(f32[4,128]{1,0:T(4,128)S(1)} %pad_maximum_fusion.angles, bf16[16,8,24,128]{3,2,1,0:T(8,128)(2,1)S(1)} %bitcast.20, bf16[1,8,1024,128]{3,2,1,0:T(8,128)(2,1)S(1)} %copy-done.3, bf16[1,8,1024,128]{3,2,1,0:T(8,128)(2,1)S(1)} %copy-done.4), custom_call_target="tpu_custom_call" | custom-call | tf_op jit(solution)/shard_map/pallas_call | solution.py:194
  39.8 17.9 %all_to_all.11 = bf16[64,32,128]{2,1,0:T(8,128)(2,1)S(1)} all-to-all(bf16[64,32,128]{2,1,0:T(8,128)(2,1)S(1)} %bitcast.23), channel_id=1, replica_groups={{0,2,4,6,8,10,12,14,16,18,20,22,24,26,28,30,32,34,36,38,40,42,44,46,48,..., dimensions={0} | all-to-all | bytes 1048576 | tf_op jit(solution)/shard_map/all_to_all | solution.py:475
  57.7 1.6 %shard_map.127 = (f32[128,512]{1,0:T(8,128)S(1)}, bf16[128,512]{1,0:T(8,128)(2,1)S(1)}) custom-call(s32[2]{0:T(128)S(1)} %pad_add_fusion.where, bf16[2048,128]{1,0:T(8,128)(2,1)S(1)} %bitcast.22, bf16[1024,512]{1,0:T(8,128)(2,1)S(1)} %get-tuple-element.37.weight, bf16[1024,512]{1,0:T(8,128)(2,1)S(1)} %collective-permute-done.4.twin), custom_call_target="tpu_custom_call" | custom-call | tf_op jit(solution)/shard_map/pallas_call | solution.py:220
  61.1 2.4 %collective-permute-start.5 = (bf16[128,512]{1,0:T(8,128)(2,1)S(1)}, bf16[128,512]{1,0:T(8,128)(2,1)S(1)}, u32[]{:S(2)}, u32[]{:S(2)}) collective-permute-start(bf16[128,512]{1,0:T(8,128)(2,1)S(1)} %get-tuple-element.39), channel_id=1, source_target_pairs={{0,6},{1,7},{2,4},{3,5},{4,2},{5,3},{6,0},{7,1},{8,14},{9,15},{10,... | collective-permute-start | bytes 393224 | tf_op jit(solution)/shard_map/ppermute | solution.py:38
  63.5 2.4 %collective-permute-done.7.two = bf16[128,512]{1,0:T(8,128)(2,1)S(1)} collective-permute-done((bf16[128,512]{1,0:T(8,128)(2,1)S(1)}, bf16[128,512]{1,0:T(8,128)(2,1)S(1)}, u32[]{:S(2)}, u32[]{:S(2)}) %collective-permute-start.7) | collective-permute-done | bytes 131104 | tf_op jit(solution)/shard_map/ppermute | solution.py:38
  68.8 1.8 %shard_map.129 = (f32[32,512]{1,0:T(8,128)S(1)}, bf16[2,256,512]{2,1,0:T(8,128)(2,1)S(1)}, bf16[128,3712]{1,0:T(8,128)(2,1)S(1)}, bf16[128,3584]{1,0:T(8,128)(2,1)S(1)}) custom-call(s32[2]{0:T(128)S(1)} %pad_add_fusion.where, f32[128,512]{1,0:T(8,128)S(1)} %get-tuple-element.33.residual, bf16[128,512]{1,0:T(8,128)(2,1)S(1)} %collective-permute-done.3.far, ...), custom_call_target="tpu_custom_call" | custom-call | tf_op jit(solution)/shard_map/pallas_call | solution.py:339
  73.6 12.2 %collective-permute-done.10.refs_3_ = bf16[128,3584]{1,0:T(8,128)(2,1)S(1)} collective-permute-done((bf16[128,3584]{1,0:T(8,128)(2,1)S(1)}, bf16[128,3584]{1,0:T(8,128)(2,1)S(1)}, u32[]{:S(2)}, u32[]{:S(2)}) %collective-permute-start.10) | collective-permute-done | bytes 917536 | tf_op jit(solution)/shard_map/ppermute | solution.py:47
  87.7 8.3 %collective-permute-done.12.refs_3_ = bf16[64,3584]{1,0:T(8,128)(2,1)S(1)} collective-permute-done((bf16[64,3584]{1,0:T(8,128)(2,1)S(1)}, bf16[64,3584]{1,0:T(8,128)(2,1)S(1)}, u32[]{:S(2)}, u32[]{:S(2)}) %collective-permute-start.12) | collective-permute-done | bytes 458784 | tf_op jit(solution)/shard_map/ppermute | solution.py:47
  96.2 1.6 %collective-permute-start.13 = (bf16[16,7296]{1,0:T(8,128)(2,1)S(1)}, bf16[16,7296]{1,0:T(8,128)(2,1)S(1)}, u32[]{:S(2)}, u32[]{:S(2)}) collective-permute-start(bf16[16,7296]{1,0:T(8,128)(2,1)S(1)} %get-tuple-element.50), channel_id=1, source_target_pairs={{0,16},{1,65},{2,18},{3,67},{4,20},{5,69},{6,22},{7,71},{8,24},{9,... | collective-permute-start | bytes 700424 | tf_op jit(solution)/shard_map/ppermute | solution.py:47
  98.5 1.9 %collective-permute-start.15 = (bf16[16,7296]{1,0:T(8,128)(2,1)S(1)}, bf16[16,7296]{1,0:T(8,128)(2,1)S(1)}, u32[]{:S(2)}, u32[]{:S(2)}) collective-permute-start(bf16[16,7296]{1,0:T(8,128)(2,1)S(1)} %get-tuple-element.52), channel_id=1, source_target_pairs={{0,24},{1,97},{2,26},{3,99},{4,28},{5,101},{6,30},{7,103},{8,16},{... | collective-permute-start | bytes 700424 | tf_op jit(solution)/shard_map/ppermute | solution.py:47
  100.5 3.5 %collective-permute-done.13.two = bf16[16,7296]{1,0:T(8,128)(2,1)S(1)} collective-permute-done((bf16[16,7296]{1,0:T(8,128)(2,1)S(1)}, bf16[16,7296]{1,0:T(8,128)(2,1)S(1)}, u32[]{:S(2)}, u32[]{:S(2)}) %collective-permute-start.13) | collective-permute-done | bytes 233504 | tf_op jit(solution)/shard_map/ppermute | solution.py:47
  109.3 1.5 %collective-permute-start.16 = (bf16[16,3584]{1,0:T(8,128)(2,1)S(1)}, bf16[16,3584]{1,0:T(8,128)(2,1)S(1)}, u32[]{:S(2)}, u32[]{:S(2)}) collective-permute-start(bf16[16,3584]{1,0:T(8,128)(2,1)S(1)} %shard_map.135.refs_0_), channel_id=1, source_target_pairs={{0,8},{1,33},{2,10},{3,35},{4,12},{5,37},{6,14},{7,39},{8,0},{9,41... | collective-permute-start | bytes 344072 | tf_op jit(solution)/shard_map/ppermute | solution.py:47
  110.8 1.9 %collective-permute-done.18.refs_3_ = bf16[16,3584]{1,0:T(8,128)(2,1)S(1)} collective-permute-done((bf16[16,3584]{1,0:T(8,128)(2,1)S(1)}, bf16[16,3584]{1,0:T(8,128)(2,1)S(1)}, u32[]{:S(2)}, u32[]{:S(2)}) %collective-permute-start.18) | collective-permute-done | bytes 114720 | tf_op jit(solution)/shard_map/ppermute | solution.py:47
  112.7 1.6 %collective-permute-done.17.refs_2_ = bf16[16,3584]{1,0:T(8,128)(2,1)S(1)} collective-permute-done((bf16[16,3584]{1,0:T(8,128)(2,1)S(1)}, bf16[16,3584]{1,0:T(8,128)(2,1)S(1)}, u32[]{:S(2)}, u32[]{:S(2)}) %collective-permute-start.17) | collective-permute-done | bytes 114720 | tf_op jit(solution)/shard_map/ppermute | solution.py:47
  115.7 1.8 %collective-permute-start.21 = (bf16[64,3584]{1,0:T(8,128)(2,1)S(1)}, bf16[64,3584]{1,0:T(8,128)(2,1)S(1)}, u32[]{:S(2)}, u32[]{:S(2)}) collective-permute-start(bf16[64,3584]{1,0:T(8,128)(2,1)S(1)} %shard_map.136.own), channel_id=1, source_target_pairs={{0,64},{1,17},{2,66},{3,19},{4,68},{5,21},{6,70},{7,23},{8,72},{9,... | collective-permute-start | bytes 1376264 | tf_op jit(solution)/shard_map/ppermute | solution.py:47
  119.9 6.0 %collective-permute-done.21.two = bf16[64,3584]{1,0:T(8,128)(2,1)S(1)} collective-permute-done((bf16[64,3584]{1,0:T(8,128)(2,1)S(1)}, bf16[64,3584]{1,0:T(8,128)(2,1)S(1)}, u32[]{:S(2)}, u32[]{:S(2)}) %collective-permute-start.21) | collective-permute-done | bytes 458784 | tf_op jit(solution)/shard_map/ppermute | solution.py:47
  125.9 4.5 %collective-permute-done.20.one = bf16[64,3584]{1,0:T(8,128)(2,1)S(1)} collective-permute-done((bf16[64,3584]{1,0:T(8,128)(2,1)S(1)}, bf16[64,3584]{1,0:T(8,128)(2,1)S(1)}, u32[]{:S(2)}, u32[]{:S(2)}) %collective-permute-start.20) | collective-permute-done | bytes 458784 | tf_op jit(solution)/shard_map/ppermute | solution.py:47
  133.4 1.6 %collective-permute-start.23 = (bf16[32,512]{1,0:T(8,128)(2,1)S(1)}, bf16[32,512]{1,0:T(8,128)(2,1)S(1)}, u32[]{:S(2)}, u32[]{:S(2)}) collective-permute-start(bf16[32,512]{1,0:T(8,128)(2,1)S(1)} %get-tuple-element.56), channel_id=1, source_target_pairs={{0,4},{1,5},{2,6},{3,7},{4,0},{5,1},{6,2},{7,3},{8,12},{9,13},{10,... | collective-permute-start | bytes 98312 | tf_op jit(solution)/shard_map/ppermute | solution.py:38
  135.0 1.7 %collective-permute-start.24 = (bf16[32,512]{1,0:T(8,128)(2,1)S(1)}, bf16[32,512]{1,0:T(8,128)(2,1)S(1)}, u32[]{:S(2)}, u32[]{:S(2)}) collective-permute-start(bf16[32,512]{1,0:T(8,128)(2,1)S(1)} %get-tuple-element.57), channel_id=1, source_target_pairs={{0,2},{1,3},{2,0},{3,1},{4,6},{5,7},{6,4},{7,5},{8,10},{9,11},{10,... | collective-permute-start | bytes 98312 | tf_op jit(solution)/shard_map/ppermute | solution.py:38
  139.1 2.8 %collective-permute-done.25.three = bf16[32,512]{1,0:T(8,128)(2,1)S(1)} collective-permute-done((bf16[32,512]{1,0:T(8,128)(2,1)S(1)}, bf16[32,512]{1,0:T(8,128)(2,1)S(1)}, u32[]{:S(2)}, u32[]{:S(2)}) %collective-permute-start.25) | collective-permute-done | bytes 32800 | tf_op jit(solution)/shard_map/ppermute | solution.py:38
  (71 shorter events, 29.8 us)
Async XLA Ops:
  0.6 7.1 %collective-permute-start.2 = (f32[32,512]{1,0:T(8,128)}, f32[32,512]{1,0:T(8,128)S(1)}, u32[]{:S(2)}, u32[]{:S(2)}) collective-permute-start(f32[32,512]{1,0:T(8,128)} %bitcast.26), channel_id=1, source_target_pairs={{0,6},{1,7},{2,4},{3,5},{4,2},{5,3},{6,0},{7,1},{8,14},{9,15},{10,... | collective-permute-start | bytes 196616 | tf_op jit(solution)/shard_map/ppermute | solution.py:38
  3.6 6.0 %collective-permute-start.1 = (f32[32,512]{1,0:T(8,128)}, f32[32,512]{1,0:T(8,128)S(1)}, u32[]{:S(2)}, u32[]{:S(2)}) collective-permute-start(f32[32,512]{1,0:T(8,128)} %bitcast.27), channel_id=1, source_target_pairs={{0,4},{1,5},{2,6},{3,7},{4,0},{5,1},{6,2},{7,3},{8,12},{9,13},{10,... | collective-permute-start | bytes 196616 | tf_op jit(solution)/shard_map/ppermute | solution.py:38
  4.4 5.2 %collective-permute-start = (f32[32,512]{1,0:T(8,128)}, f32[32,512]{1,0:T(8,128)S(1)}, u32[]{:S(2)}, u32[]{:S(2)}) collective-permute-start(f32[32,512]{1,0:T(8,128)} %bitcast.28), channel_id=1, source_target_pairs={{0,2},{1,3},{2,0},{3,1},{4,6},{5,7},{6,4},{7,5},{8,10},{9,11},{10,... | collective-permute-start | bytes 196616 | tf_op jit(solution)/shard_map/ppermute | solution.py:38
  4.8 6.2 %collective-permute-start.4 = (bf16[1024,512]{1,0:T(8,128)(2,1)}, bf16[1024,512]{1,0:T(8,128)(2,1)S(1)}, u32[]{:S(2)}, u32[]{:S(2)}) collective-permute-start(bf16[1024,512]{1,0:T(8,128)(2,1)} %refs_3_.1), channel_id=1, source_target_pairs={{0,1},{1,0},{2,3},{3,2},{4,5},{5,4},{6,7},{7,6},{8,9},{9,8},{10,11... | collective-permute-start | bytes 3145736 | tf_op jit(solution)/shard_map/ppermute | solution.py:38
  59.3 6.5 %collective-permute-start.7 = (bf16[128,512]{1,0:T(8,128)(2,1)S(1)}, bf16[128,512]{1,0:T(8,128)(2,1)S(1)}, u32[]{:S(2)}, u32[]{:S(2)}) collective-permute-start(bf16[128,512]{1,0:T(8,128)(2,1)S(1)} %get-tuple-element.39), channel_id=1, source_target_pairs={{0,4},{1,5},{2,6},{3,7},{4,0},{5,1},{6,2},{7,3},{8,12},{9,13},{10,... | collective-permute-start | bytes 393224 | tf_op jit(solution)/shard_map/ppermute | solution.py:38
  60.5 5.4 %collective-permute-start.6 = (bf16[128,512]{1,0:T(8,128)(2,1)S(1)}, bf16[128,512]{1,0:T(8,128)(2,1)S(1)}, u32[]{:S(2)}, u32[]{:S(2)}) collective-permute-start(bf16[128,512]{1,0:T(8,128)(2,1)S(1)} %get-tuple-element.39), channel_id=1, source_target_pairs={{0,2},{1,3},{2,0},{3,1},{4,6},{5,7},{6,4},{7,5},{8,10},{9,11},{10,... | collective-permute-start | bytes 393224 | tf_op jit(solution)/shard_map/ppermute | solution.py:38
  61.1 6.2 %collective-permute-start.5 = (bf16[128,512]{1,0:T(8,128)(2,1)S(1)}, bf16[128,512]{1,0:T(8,128)(2,1)S(1)}, u32[]{:S(2)}, u32[]{:S(2)}) collective-permute-start(bf16[128,512]{1,0:T(8,128)(2,1)S(1)} %get-tuple-element.39), channel_id=1, source_target_pairs={{0,6},{1,7},{2,4},{3,5},{4,2},{5,3},{6,0},{7,1},{8,14},{9,15},{10,... | collective-permute-start | bytes 393224 | tf_op jit(solution)/shard_map/ppermute | solution.py:38
  67.3 1.4 %collective-permute-start.8 = (bf16[128,512]{1,0:T(8,128)(2,1)S(1)}, bf16[128,512]{1,0:T(8,128)(2,1)S(1)}, u32[]{:S(2)}, u32[]{:S(2)}) collective-permute-start(bf16[128,512]{1,0:T(8,128)(2,1)S(1)} %shard_map.128.mine), channel_id=1, source_target_pairs={{0,1},{1,0},{2,3},{3,2},{4,5},{5,4},{6,7},{7,6},{8,9},{9,8},{10,11... | collective-permute-start | bytes 393224 | tf_op jit(solution)/shard_map/ppermute | solution.py:38
  70.6 15.1 %collective-permute-start.9 = (bf16[128,3712]{1,0:T(8,128)(2,1)S(1)}, bf16[128,3712]{1,0:T(8,128)(2,1)S(1)}, u32[]{:S(2)}, u32[]{:S(2)}) collective-permute-start(bf16[128,3712]{1,0:T(8,128)(2,1)S(1)} %get-tuple-element.43), channel_id=1, source_target_pairs={{0,32},{1,9},{2,34},{3,11},{4,36},{5,13},{6,38},{7,15},{8,40},{9,1... | collective-permute-start | bytes 2850824 | tf_op jit(solution)/shard_map/ppermute | solution.py:47
  71.1 14.6 %collective-permute-start.10 = (bf16[128,3584]{1,0:T(8,128)(2,1)S(1)}, bf16[128,3584]{1,0:T(8,128)(2,1)S(1)}, u32[]{:S(2)}, u32[]{:S(2)}) collective-permute-start(bf16[128,3584]{1,0:T(8,128)(2,1)S(1)} %get-tuple-element.45), channel_id=1, source_target_pairs={{0,96},{1,25},{2,98},{3,27},{4,100},{5,29},{6,102},{7,31},{8,104},... | collective-permute-start | bytes 2752520 | tf_op jit(solution)/shard_map/ppermute | solution.py:47
  86.1 9.9 %collective-permute-start.11 = (bf16[64,3712]{1,0:T(8,128)(2,1)S(1)}, bf16[64,3712]{1,0:T(8,128)(2,1)S(1)}, u32[]{:S(2)}, u32[]{:S(2)}) collective-permute-start(bf16[64,3712]{1,0:T(8,128)(2,1)S(1)} %get-tuple-element.47), channel_id=1, source_target_pairs={{0,96},{1,25},{2,98},{3,27},{4,100},{5,29},{6,102},{7,31},{8,104},... | collective-permute-start | bytes 1425416 | tf_op jit(solution)/shard_map/ppermute | solution.py:47
  87.5 8.5 %collective-permute-start.12 = (bf16[64,3584]{1,0:T(8,128)(2,1)S(1)}, bf16[64,3584]{1,0:T(8,128)(2,1)S(1)}, u32[]{:S(2)}, u32[]{:S(2)}) collective-permute-start(bf16[64,3584]{1,0:T(8,128)(2,1)S(1)} %get-tuple-element.49), channel_id=1, source_target_pairs={{0,32},{1,9},{2,34},{3,11},{4,36},{5,13},{6,38},{7,15},{8,40},{9,1... | collective-permute-start | bytes 1376264 | tf_op jit(solution)/shard_map/ppermute | solution.py:47
  96.2 7.7 %collective-permute-start.13 = (bf16[16,7296]{1,0:T(8,128)(2,1)S(1)}, bf16[16,7296]{1,0:T(8,128)(2,1)S(1)}, u32[]{:S(2)}, u32[]{:S(2)}) collective-permute-start(bf16[16,7296]{1,0:T(8,128)(2,1)S(1)} %get-tuple-element.50), channel_id=1, source_target_pairs={{0,16},{1,65},{2,18},{3,67},{4,20},{5,69},{6,22},{7,71},{8,24},{9,... | collective-permute-start | bytes 700424 | tf_op jit(solution)/shard_map/ppermute | solution.py:47
  97.8 7.2 %collective-permute-start.14 = (bf16[16,7296]{1,0:T(8,128)(2,1)S(1)}, bf16[16,7296]{1,0:T(8,128)(2,1)S(1)}, u32[]{:S(2)}, u32[]{:S(2)}) collective-permute-start(bf16[16,7296]{1,0:T(8,128)(2,1)S(1)} %get-tuple-element.51), channel_id=1, source_target_pairs={{0,8},{1,33},{2,10},{3,35},{4,12},{5,37},{6,14},{7,39},{8,0},{9,41... | collective-permute-start | bytes 700424 | tf_op jit(solution)/shard_map/ppermute | solution.py:47
  98.5 7.9 %collective-permute-start.15 = (bf16[16,7296]{1,0:T(8,128)(2,1)S(1)}, bf16[16,7296]{1,0:T(8,128)(2,1)S(1)}, u32[]{:S(2)}, u32[]{:S(2)}) collective-permute-start(bf16[16,7296]{1,0:T(8,128)(2,1)S(1)} %get-tuple-element.52), channel_id=1, source_target_pairs={{0,24},{1,97},{2,26},{3,99},{4,28},{5,101},{6,30},{7,103},{8,16},{... | collective-permute-start | bytes 700424 | tf_op jit(solution)/shard_map/ppermute | solution.py:47
  106.6 6.1 %collective-permute-start.18 = (bf16[16,3584]{1,0:T(8,128)(2,1)S(1)}, bf16[16,3584]{1,0:T(8,128)(2,1)S(1)}, u32[]{:S(2)}, u32[]{:S(2)}) collective-permute-start(bf16[16,3584]{1,0:T(8,128)(2,1)S(1)} %shard_map.135.refs_0_), channel_id=1, source_target_pairs={{0,24},{1,97},{2,26},{3,99},{4,28},{5,101},{6,30},{7,103},{8,16},{... | collective-permute-start | bytes 344072 | tf_op jit(solution)/shard_map/ppermute | solution.py:47
  108.1 6.3 %collective-permute-start.17 = (bf16[16,3584]{1,0:T(8,128)(2,1)S(1)}, bf16[16,3584]{1,0:T(8,128)(2,1)S(1)}, u32[]{:S(2)}, u32[]{:S(2)}) collective-permute-start(bf16[16,3584]{1,0:T(8,128)(2,1)S(1)} %shard_map.135.refs_0_), channel_id=1, source_target_pairs={{0,16},{1,65},{2,18},{3,67},{4,20},{5,69},{6,22},{7,71},{8,24},{9,... | collective-permute-start | bytes 344072 | tf_op jit(solution)/shard_map/ppermute | solution.py:47
  109.3 6.4 %collective-permute-start.16 = (bf16[16,3584]{1,0:T(8,128)(2,1)S(1)}, bf16[16,3584]{1,0:T(8,128)(2,1)S(1)}, u32[]{:S(2)}, u32[]{:S(2)}) collective-permute-start(bf16[16,3584]{1,0:T(8,128)(2,1)S(1)} %shard_map.135.refs_0_), channel_id=1, source_target_pairs={{0,8},{1,33},{2,10},{3,35},{4,12},{5,37},{6,14},{7,39},{8,0},{9,41... | collective-permute-start | bytes 344072 | tf_op jit(solution)/shard_map/ppermute | solution.py:47
  115.7 10.2 %collective-permute-start.21 = (bf16[64,3584]{1,0:T(8,128)(2,1)S(1)}, bf16[64,3584]{1,0:T(8,128)(2,1)S(1)}, u32[]{:S(2)}, u32[]{:S(2)}) collective-permute-start(bf16[64,3584]{1,0:T(8,128)(2,1)S(1)} %shard_map.136.own), channel_id=1, source_target_pairs={{0,64},{1,17},{2,66},{3,19},{4,68},{5,21},{6,70},{7,23},{8,72},{9,... | collective-permute-start | bytes 1376264 | tf_op jit(solution)/shard_map/ppermute | solution.py:47
  117.4 12.9 %collective-permute-start.20 = (bf16[64,3584]{1,0:T(8,128)(2,1)S(1)}, bf16[64,3584]{1,0:T(8,128)(2,1)S(1)}, u32[]{:S(2)}, u32[]{:S(2)}) collective-permute-start(bf16[64,3584]{1,0:T(8,128)(2,1)S(1)} %shard_map.136.own), channel_id=1, source_target_pairs={{0,32},{1,9},{2,34},{3,11},{4,36},{5,13},{6,38},{7,15},{8,40},{9,1... | collective-permute-start | bytes 1376264 | tf_op jit(solution)/shard_map/ppermute | solution.py:47
  118.9 11.7 %collective-permute-start.19 = (bf16[64,3584]{1,0:T(8,128)(2,1)S(1)}, bf16[64,3584]{1,0:T(8,128)(2,1)S(1)}, u32[]{:S(2)}, u32[]{:S(2)}) collective-permute-start(bf16[64,3584]{1,0:T(8,128)(2,1)S(1)} %shard_map.136.own), channel_id=1, source_target_pairs={{0,96},{1,25},{2,98},{3,27},{4,100},{5,29},{6,102},{7,31},{8,104},... | collective-permute-start | bytes 1376264 | tf_op jit(solution)/shard_map/ppermute | solution.py:47
  133.4 5.7 %collective-permute-start.23 = (bf16[32,512]{1,0:T(8,128)(2,1)S(1)}, bf16[32,512]{1,0:T(8,128)(2,1)S(1)}, u32[]{:S(2)}, u32[]{:S(2)}) collective-permute-start(bf16[32,512]{1,0:T(8,128)(2,1)S(1)} %get-tuple-element.56), channel_id=1, source_target_pairs={{0,4},{1,5},{2,6},{3,7},{4,0},{5,1},{6,2},{7,3},{8,12},{9,13},{10,... | collective-permute-start | bytes 98312 | tf_op jit(solution)/shard_map/ppermute | solution.py:38
  135.0 4.0 %collective-permute-start.24 = (bf16[32,512]{1,0:T(8,128)(2,1)S(1)}, bf16[32,512]{1,0:T(8,128)(2,1)S(1)}, u32[]{:S(2)}, u32[]{:S(2)}) collective-permute-start(bf16[32,512]{1,0:T(8,128)(2,1)S(1)} %get-tuple-element.57), channel_id=1, source_target_pairs={{0,2},{1,3},{2,0},{3,1},{4,6},{5,7},{6,4},{7,5},{8,10},{9,11},{10,... | collective-permute-start | bytes 98312 | tf_op jit(solution)/shard_map/ppermute | solution.py:38
  136.8 5.1 %collective-permute-start.25 = (bf16[32,512]{1,0:T(8,128)(2,1)S(1)}, bf16[32,512]{1,0:T(8,128)(2,1)S(1)}, u32[]{:S(2)}, u32[]{:S(2)}) collective-permute-start(bf16[32,512]{1,0:T(8,128)(2,1)S(1)} %get-tuple-element.58), channel_id=1, source_target_pairs={{0,6},{1,7},{2,4},{3,5},{4,2},{5,3},{6,0},{7,1},{8,14},{9,15},{10,... | collective-permute-start | bytes 98312 | tf_op jit(solution)/shard_map/ppermute | solution.py:38
  (8 other events, 179.6 us)

commit v7 on v6

--- a/solution.py
+++ b/solution.py
@@ -257,20 +257,17 @@
     return call(final_body, shaped((32, WIDTH), F32), [VM] * 5)(after, own, *pieces)
 
 
-def rows_body(own, one, two, three, gain, residual, scaled):
+def rows_body(own, one, two, three, gain, scaled):
     for k, piece in enumerate((own, one, two, three)):
         rows = slice(k * 32, k * 32 + 32)
-        residual[rows, :] = piece[...]
         scaled[rows, :] = (piece[...] * gain[...]).astype(BF16)
 
 
 def gather_rows(own, gain, *weights):
     pieces = [swap_gy(own, 2 * k) for k in (1, 2, 3)]
     own, gain, *weights = bring((own, gain, *weights))
-    residual, near = call(
-        rows_body, (shaped((128, WIDTH), F32), shaped((128, WIDTH), BF16)), [VM] * 5
-    )(own, *pieces, gain)
-    return residual, near, swap_gy(near, 1), gain, *weights
+    near = call(rows_body, shaped((128, WIDTH), BF16), [VM] * 5)(own, *pieces, gain)
+    return (own, *pieces), near, swap_gy(near, 1), gain, *weights
 
 
 def two_parts(squares):
@@ -302,7 +299,9 @@
             outs[f][:, i * HALF : i * HALF + HALF] = part.astype(outs[f].dtype)
 
 
-def send_body(where, residual, far, attn_gain, gain, mine, twin, gate, up, after, lhs, first, second, sums, attention):
+def send_body(where, *refs):
+    residual, refs = refs[:4], refs[4:]
+    far, attn_gain, gain, mine, twin, gate, up, after, lhs, first, second, sums, attention = refs
     core = where[1] & 1
     sums[0] = jnp.where(core == 0, mine[...].astype(F32), twin[...].astype(F32))
     sums[1] = jnp.where(core == 0, twin[...].astype(F32), mine[...].astype(F32))
@@ -317,7 +316,7 @@
     for chunk in range(16):
         rows = slice(chunk * 16, chunk * 16 + 16)
         if chunk < 8:
-            whole = residual[rows, :]
+            whole = residual[chunk // 2][chunk % 2 * 16 : chunk % 2 * 16 + 16, :]
         else:
             whole = far[chunk * 16 - 128 : chunk * 16 - 112, :].astype(F32) / attn_gain[...]
         whole = whole + jnp.concatenate([attention[q, rows, :] for q in range(4)], axis=1)
@@ -340,9 +339,9 @@
         send_body,
         (shaped((32, WIDTH), F32), shaped((2, 256, WIDTH), BF16))
         + tuple(shaped((128, width), BF16) for width in WIDTHS),
-        [SM] + [VM] * 8,
+        [SM] + [VM] * 11,
         [pltpu.VMEM((2, 128, WIDTH), F32), pltpu.VMEM((4, 256, HD), F32)],
-    )(where, residual, far, attn_gain, gain, *sums, gate, up)
+    )(where, *residual, far, attn_gain, gain, *sums, gate, up)
 
 
 def halve_body(send, *refs):

time: 143 us -> 143 us (level)
  no operation moved by 1% of the time
where the time goes in v7:
time: 143 us
  waiting for transfers between devices  54.7 us (38%)
  blocking collectives  44.1 us (31%)
  starting transfers between devices  28.5 us (20%)
  Pallas kernels  13 us (9%)
  between operations  1.48 us (1%)
    ppermute x13, waiting for transfers between devices, swap_by_core(): return lax.ppermute(array, ('gx', 'gy'), pairs)  42 us
    all_to_all x1, blocking collectives, per_device(): lax.all_to_all(partial, ('gx', 'gy'), 0, 0, tiled=True)  26.2 us
    all_to_all x1, blocking collectives, per_device(): lax.all_to_all(attended.reshape(64, 32, HD), ('gx', 'gy'), 0, 0, axis_ind...  17.9 us
    ppermute x13, starting transfers between devices, swap_by_core(): return lax.ppermute(array, ('gx', 'gy'), pairs)  15.7 us
    ppermute x13, starting transfers between devices, swap_gy(): return lax.ppermute(array, 'gy', [(i, i ^ bits) for i in range(NY)])  12.8 us
    ppermute x13, waiting for transfers between devices, swap_gy(): return lax.ppermute(array, 'gy', [(i, i ^ bits) for i in range(NY)])  12.7 us
  transfers between devices with their start and end apart: 26, of which 20 were waited for; matrix products, arithmetic and copies ran while one was open for 0% of the time, Pallas kernels for 3%

profile of v7, /device:TPU:0, one launch (start us, length us, event | category | flops | bytes accessed | tf_op | source)
XLA Modules:
  0.0 142.5 jit_solution(475062981343882386)
XLA Ops:
  0.6 2.9 %collective-permute-start.2 = (f32[32,512]{1,0:T(8,128)}, f32[32,512]{1,0:T(8,128)S(1)}, u32[]{:S(2)}, u32[]{:S(2)}) collective-permute-start(f32[32,512]{1,0:T(8,128)} %bitcast.26), channel_id=1, source_target_pairs={{0,6},{1,7},{2,4},{3,5},{4,2},{5,3},{6,0},{7,1},{8,14},{9,15},{10,... | collective-permute-start | bytes 196616 | tf_op jit(solution)/shard_map/ppermute | solution.py:38
  5.5 1.7 %shard_map.122 = (f32[32,512]{1,0:T(8,128)S(1)}, f32[1,512]{1,0:T(1,128)S(1)}, bf16[512,1280]{1,0:T(8,128)(2,1)S(1)}, bf16[1024,512]{1,0:T(8,128)(2,1)S(1)}) custom-call(f32[32,512]{1,0:T(8,128)} %bitcast.29, f32[1,512]{1,0:T(1,128)} %bitcast.31, bf16[512,1280]{1,0:T(8,128)(2,1)} %refs_2_.1, bf16[1024,512]{1,0:T(8,128)(2,1)} %refs_3_.1), custom_call_target="tpu_custom_call" | custom-call | bytes 4853760 | tf_op jit(solution)/shard_map/pallas_call | solution.py:86
  7.7 1.8 %collective-permute-done.1.two.refs_2_ = f32[32,512]{1,0:T(8,128)S(1)} collective-permute-done((f32[32,512]{1,0:T(8,128)}, f32[32,512]{1,0:T(8,128)S(1)}, u32[]{:S(2)}, u32[]{:S(2)}) %collective-permute-start.1) | collective-permute-done | bytes 65568 | tf_op jit(solution)/shard_map/ppermute | solution.py:38
  12.0 26.2 %all_to_all.10 = bf16[128,24,128]{2,1,0:T(8,128)(2,1)S(1)} all-to-all(bf16[128,24,128]{2,1,0:T(8,128)(2,1)S(1)} %bitcast.21), channel_id=1, replica_groups=mesh['gx'=16,'gy'=8] {'gx','gy'}, dimensions={0} | all-to-all | bytes 1572864 | tf_op jit(solution)/shard_map/all_to_all | solution.py:472
  38.2 1.6 %shard_map.126 = (bf16[16,8,16,128]{3,2,1,0:T(8,128)(2,1)S(1)}, bf16[1,2,8,256]{3,2,1,0:T(8,128)(2,1)}) custom-call(f32[4,128]{1,0:T(4,128)S(1)} %pad_maximum_fusion.angles, bf16[16,8,24,128]{3,2,1,0:T(8,128)(2,1)S(1)} %bitcast.20, bf16[1,8,1024,128]{3,2,1,0:T(8,128)(2,1)S(1)} %copy-done.3, bf16[1,8,1024,128]{3,2,1,0:T(8,128)(2,1)S(1)} %copy-done.4), custom_call_target="tpu_custom_call" | custom-call | tf_op jit(solution)/shard_map/pallas_call | solution.py:194
  39.8 17.9 %all_to_all.11 = bf16[64,32,128]{2,1,0:T(8,128)(2,1)S(1)} all-to-all(bf16[64,32,128]{2,1,0:T(8,128)(2,1)S(1)} %bitcast.23), channel_id=1, replica_groups={{0,2,4,6,8,10,12,14,16,18,20,22,24,26,28,30,32,34,36,38,40,42,44,46,48,..., dimensions={0} | all-to-all | bytes 1048576 | tf_op jit(solution)/shard_map/all_to_all | solution.py:474
  57.7 1.6 %shard_map.127 = (f32[128,512]{1,0:T(8,128)S(1)}, bf16[128,512]{1,0:T(8,128)(2,1)S(1)}) custom-call(s32[2]{0:T(128)S(1)} %pad_add_fusion.where, bf16[2048,128]{1,0:T(8,128)(2,1)S(1)} %bitcast.22, bf16[1024,512]{1,0:T(8,128)(2,1)S(1)} %get-tuple-element.33.weight, bf16[1024,512]{1,0:T(8,128)(2,1)S(1)} %collective-permute-done.4.twin), custom_call_target="tpu_custom_call" | custom-call | tf_op jit(solution)/shard_map/pallas_call | solution.py:220
  61.0 2.4 %collective-permute-start.5 = (bf16[128,512]{1,0:T(8,128)(2,1)S(1)}, bf16[128,512]{1,0:T(8,128)(2,1)S(1)}, u32[]{:S(2)}, u32[]{:S(2)}) collective-permute-start(bf16[128,512]{1,0:T(8,128)(2,1)S(1)} %get-tuple-element.35), channel_id=1, source_target_pairs={{0,6},{1,7},{2,4},{3,5},{4,2},{5,3},{6,0},{7,1},{8,14},{9,15},{10,... | collective-permute-start | bytes 393224 | tf_op jit(solution)/shard_map/ppermute | solution.py:38
  63.5 2.4 %collective-permute-done.7.two = bf16[128,512]{1,0:T(8,128)(2,1)S(1)} collective-permute-done((bf16[128,512]{1,0:T(8,128)(2,1)S(1)}, bf16[128,512]{1,0:T(8,128)(2,1)S(1)}, u32[]{:S(2)}, u32[]{:S(2)}) %collective-permute-start.7) | collective-permute-done | bytes 131104 | tf_op jit(solution)/shard_map/ppermute | solution.py:38
  68.8 1.8 %shard_map.129 = (f32[32,512]{1,0:T(8,128)S(1)}, bf16[2,256,512]{2,1,0:T(8,128)(2,1)S(1)}, bf16[128,3712]{1,0:T(8,128)(2,1)S(1)}, bf16[128,3584]{1,0:T(8,128)(2,1)S(1)}) custom-call(s32[2]{0:T(128)S(1)} %pad_add_fusion.where, f32[32,512]{1,0:T(8,128)S(1)} %get-tuple-element.29.own.refs_0_, f32[32,512]{1,0:T(8,128)S(1)} %collective-permute-done.one.refs_1_, ...), custom_call_target="tpu_custom_call" | custom-call | tf_op jit(solution)/shard_map/pallas_call | solution.py:338
  73.5 12.2 %collective-permute-done.10.refs_3_ = bf16[128,3584]{1,0:T(8,128)(2,1)S(1)} collective-permute-done((bf16[128,3584]{1,0:T(8,128)(2,1)S(1)}, bf16[128,3584]{1,0:T(8,128)(2,1)S(1)}, u32[]{:S(2)}, u32[]{:S(2)}) %collective-permute-start.10) | collective-permute-done | bytes 917536 | tf_op jit(solution)/shard_map/ppermute | solution.py:47
  87.7 8.3 %collective-permute-done.12.refs_3_ = bf16[64,3584]{1,0:T(8,128)(2,1)S(1)} collective-permute-done((bf16[64,3584]{1,0:T(8,128)(2,1)S(1)}, bf16[64,3584]{1,0:T(8,128)(2,1)S(1)}, u32[]{:S(2)}, u32[]{:S(2)}) %collective-permute-start.12) | collective-permute-done | bytes 458784 | tf_op jit(solution)/shard_map/ppermute | solution.py:47
  96.2 1.6 %collective-permute-start.13 = (bf16[16,7296]{1,0:T(8,128)(2,1)S(1)}, bf16[16,7296]{1,0:T(8,128)(2,1)S(1)}, u32[]{:S(2)}, u32[]{:S(2)}) collective-permute-start(bf16[16,7296]{1,0:T(8,128)(2,1)S(1)} %get-tuple-element.46), channel_id=1, source_target_pairs={{0,16},{1,65},{2,18},{3,67},{4,20},{5,69},{6,22},{7,71},{8,24},{9,... | collective-permute-start | bytes 700424 | tf_op jit(solution)/shard_map/ppermute | solution.py:47
  98.5 1.9 %collective-permute-start.15 = (bf16[16,7296]{1,0:T(8,128)(2,1)S(1)}, bf16[16,7296]{1,0:T(8,128)(2,1)S(1)}, u32[]{:S(2)}, u32[]{:S(2)}) collective-permute-start(bf16[16,7296]{1,0:T(8,128)(2,1)S(1)} %get-tuple-element.48), channel_id=1, source_target_pairs={{0,24},{1,97},{2,26},{3,99},{4,28},{5,101},{6,30},{7,103},{8,16},{... | collective-permute-start | bytes 700424 | tf_op jit(solution)/shard_map/ppermute | solution.py:47
  100.4 3.5 %collective-permute-done.13.two = bf16[16,7296]{1,0:T(8,128)(2,1)S(1)} collective-permute-done((bf16[16,7296]{1,0:T(8,128)(2,1)S(1)}, bf16[16,7296]{1,0:T(8,128)(2,1)S(1)}, u32[]{:S(2)}, u32[]{:S(2)}) %collective-permute-start.13) | collective-permute-done | bytes 233504 | tf_op jit(solution)/shard_map/ppermute | solution.py:47
  109.3 1.5 %collective-permute-start.16 = (bf16[16,3584]{1,0:T(8,128)(2,1)S(1)}, bf16[16,3584]{1,0:T(8,128)(2,1)S(1)}, u32[]{:S(2)}, u32[]{:S(2)}) collective-permute-start(bf16[16,3584]{1,0:T(8,128)(2,1)S(1)} %shard_map.135.refs_0_), channel_id=1, source_target_pairs={{0,8},{1,33},{2,10},{3,35},{4,12},{5,37},{6,14},{7,39},{8,0},{9,41... | collective-permute-start | bytes 344072 | tf_op jit(solution)/shard_map/ppermute | solution.py:47
  110.8 1.9 %collective-permute-done.18.refs_3_ = bf16[16,3584]{1,0:T(8,128)(2,1)S(1)} collective-permute-done((bf16[16,3584]{1,0:T(8,128)(2,1)S(1)}, bf16[16,3584]{1,0:T(8,128)(2,1)S(1)}, u32[]{:S(2)}, u32[]{:S(2)}) %collective-permute-start.18) | collective-permute-done | bytes 114720 | tf_op jit(solution)/shard_map/ppermute | solution.py:47
  112.7 1.7 %collective-permute-done.17.refs_2_ = bf16[16,3584]{1,0:T(8,128)(2,1)S(1)} collective-permute-done((bf16[16,3584]{1,0:T(8,128)(2,1)S(1)}, bf16[16,3584]{1,0:T(8,128)(2,1)S(1)}, u32[]{:S(2)}, u32[]{:S(2)}) %collective-permute-start.17) | collective-permute-done | bytes 114720 | tf_op jit(solution)/shard_map/ppermute | solution.py:47
  115.7 1.8 %collective-permute-start.21 = (bf16[64,3584]{1,0:T(8,128)(2,1)S(1)}, bf16[64,3584]{1,0:T(8,128)(2,1)S(1)}, u32[]{:S(2)}, u32[]{:S(2)}) collective-permute-start(bf16[64,3584]{1,0:T(8,128)(2,1)S(1)} %shard_map.136.own), channel_id=1, source_target_pairs={{0,64},{1,17},{2,66},{3,19},{4,68},{5,21},{6,70},{7,23},{8,72},{9,... | collective-permute-start | bytes 1376264 | tf_op jit(solution)/shard_map/ppermute | solution.py:47
  119.9 6.0 %collective-permute-done.21.two = bf16[64,3584]{1,0:T(8,128)(2,1)S(1)} collective-permute-done((bf16[64,3584]{1,0:T(8,128)(2,1)S(1)}, bf16[64,3584]{1,0:T(8,128)(2,1)S(1)}, u32[]{:S(2)}, u32[]{:S(2)}) %collective-permute-start.21) | collective-permute-done | bytes 458784 | tf_op jit(solution)/shard_map/ppermute | solution.py:47
  125.8 4.5 %collective-permute-done.20.one = bf16[64,3584]{1,0:T(8,128)(2,1)S(1)} collective-permute-done((bf16[64,3584]{1,0:T(8,128)(2,1)S(1)}, bf16[64,3584]{1,0:T(8,128)(2,1)S(1)}, u32[]{:S(2)}, u32[]{:S(2)}) %collective-permute-start.20) | collective-permute-done | bytes 458784 | tf_op jit(solution)/shard_map/ppermute | solution.py:47
  133.4 1.6 %collective-permute-start.23 = (bf16[32,512]{1,0:T(8,128)(2,1)S(1)}, bf16[32,512]{1,0:T(8,128)(2,1)S(1)}, u32[]{:S(2)}, u32[]{:S(2)}) collective-permute-start(bf16[32,512]{1,0:T(8,128)(2,1)S(1)} %get-tuple-element.52), channel_id=1, source_target_pairs={{0,4},{1,5},{2,6},{3,7},{4,0},{5,1},{6,2},{7,3},{8,12},{9,13},{10,... | collective-permute-start | bytes 98312 | tf_op jit(solution)/shard_map/ppermute | solution.py:38
  135.0 1.7 %collective-permute-start.24 = (bf16[32,512]{1,0:T(8,128)(2,1)S(1)}, bf16[32,512]{1,0:T(8,128)(2,1)S(1)}, u32[]{:S(2)}, u32[]{:S(2)}) collective-permute-start(bf16[32,512]{1,0:T(8,128)(2,1)S(1)} %get-tuple-element.53), channel_id=1, source_target_pairs={{0,2},{1,3},{2,0},{3,1},{4,6},{5,7},{6,4},{7,5},{8,10},{9,11},{10,... | collective-permute-start | bytes 98312 | tf_op jit(solution)/shard_map/ppermute | solution.py:38
  139.1 2.8 %collective-permute-done.25.three = bf16[32,512]{1,0:T(8,128)(2,1)S(1)} collective-permute-done((bf16[32,512]{1,0:T(8,128)(2,1)S(1)}, bf16[32,512]{1,0:T(8,128)(2,1)S(1)}, u32[]{:S(2)}, u32[]{:S(2)}) %collective-permute-start.25) | collective-permute-done | bytes 32800 | tf_op jit(solution)/shard_map/ppermute | solution.py:38
  (71 shorter events, 29.9 us)
Async XLA Ops:
  0.6 7.1 %collective-permute-start.2 = (f32[32,512]{1,0:T(8,128)}, f32[32,512]{1,0:T(8,128)S(1)}, u32[]{:S(2)}, u32[]{:S(2)}) collective-permute-start(f32[32,512]{1,0:T(8,128)} %bitcast.26), channel_id=1, source_target_pairs={{0,6},{1,7},{2,4},{3,5},{4,2},{5,3},{6,0},{7,1},{8,14},{9,15},{10,... | collective-permute-start | bytes 196616 | tf_op jit(solution)/shard_map/ppermute | solution.py:38
  3.6 6.0 %collective-permute-start.1 = (f32[32,512]{1,0:T(8,128)}, f32[32,512]{1,0:T(8,128)S(1)}, u32[]{:S(2)}, u32[]{:S(2)}) collective-permute-start(f32[32,512]{1,0:T(8,128)} %bitcast.27), channel_id=1, source_target_pairs={{0,4},{1,5},{2,6},{3,7},{4,0},{5,1},{6,2},{7,3},{8,12},{9,13},{10,... | collective-permute-start | bytes 196616 | tf_op jit(solution)/shard_map/ppermute | solution.py:38
  4.4 5.2 %collective-permute-start = (f32[32,512]{1,0:T(8,128)}, f32[32,512]{1,0:T(8,128)S(1)}, u32[]{:S(2)}, u32[]{:S(2)}) collective-permute-start(f32[32,512]{1,0:T(8,128)} %bitcast.28), channel_id=1, source_target_pairs={{0,2},{1,3},{2,0},{3,1},{4,6},{5,7},{6,4},{7,5},{8,10},{9,11},{10,... | collective-permute-start | bytes 196616 | tf_op jit(solution)/shard_map/ppermute | solution.py:38
  4.8 6.2 %collective-permute-start.4 = (bf16[1024,512]{1,0:T(8,128)(2,1)}, bf16[1024,512]{1,0:T(8,128)(2,1)S(1)}, u32[]{:S(2)}, u32[]{:S(2)}) collective-permute-start(bf16[1024,512]{1,0:T(8,128)(2,1)} %refs_3_.1), channel_id=1, source_target_pairs={{0,1},{1,0},{2,3},{3,2},{4,5},{5,4},{6,7},{7,6},{8,9},{9,8},{10,11... | collective-permute-start | bytes 3145736 | tf_op jit(solution)/shard_map/ppermute | solution.py:38
  59.3 6.5 %collective-permute-start.7 = (bf16[128,512]{1,0:T(8,128)(2,1)S(1)}, bf16[128,512]{1,0:T(8,128)(2,1)S(1)}, u32[]{:S(2)}, u32[]{:S(2)}) collective-permute-start(bf16[128,512]{1,0:T(8,128)(2,1)S(1)} %get-tuple-element.35), channel_id=1, source_target_pairs={{0,4},{1,5},{2,6},{3,7},{4,0},{5,1},{6,2},{7,3},{8,12},{9,13},{10,... | collective-permute-start | bytes 393224 | tf_op jit(solution)/shard_map/ppermute | solution.py:38
  60.5 5.4 %collective-permute-start.6 = (bf16[128,512]{1,0:T(8,128)(2,1)S(1)}, bf16[128,512]{1,0:T(8,128)(2,1)S(1)}, u32[]{:S(2)}, u32[]{:S(2)}) collective-permute-start(bf16[128,512]{1,0:T(8,128)(2,1)S(1)} %get-tuple-element.35), channel_id=1, source_target_pairs={{0,2},{1,3},{2,0},{3,1},{4,6},{5,7},{6,4},{7,5},{8,10},{9,11},{10,... | collective-permute-start | bytes 393224 | tf_op jit(solution)/shard_map/ppermute | solution.py:38
  61.0 6.2 %collective-permute-start.5 = (bf16[128,512]{1,0:T(8,128)(2,1)S(1)}, bf16[128,512]{1,0:T(8,128)(2,1)S(1)}, u32[]{:S(2)}, u32[]{:S(2)}) collective-permute-start(bf16[128,512]{1,0:T(8,128)(2,1)S(1)} %get-tuple-element.35), channel_id=1, source_target_pairs={{0,6},{1,7},{2,4},{3,5},{4,2},{5,3},{6,0},{7,1},{8,14},{9,15},{10,... | collective-permute-start | bytes 393224 | tf_op jit(solution)/shard_map/ppermute | solution.py:38
  67.3 1.4 %collective-permute-start.8 = (bf16[128,512]{1,0:T(8,128)(2,1)S(1)}, bf16[128,512]{1,0:T(8,128)(2,1)S(1)}, u32[]{:S(2)}, u32[]{:S(2)}) collective-permute-start(bf16[128,512]{1,0:T(8,128)(2,1)S(1)} %shard_map.128.refs_7_), channel_id=1, source_target_pairs={{0,1},{1,0},{2,3},{3,2},{4,5},{5,4},{6,7},{7,6},{8,9},{9,8},{10,11... | collective-permute-start | bytes 393224 | tf_op jit(solution)/shard_map/ppermute | solution.py:38
  70.6 15.1 %collective-permute-start.9 = (bf16[128,3712]{1,0:T(8,128)(2,1)S(1)}, bf16[128,3712]{1,0:T(8,128)(2,1)S(1)}, u32[]{:S(2)}, u32[]{:S(2)}) collective-permute-start(bf16[128,3712]{1,0:T(8,128)(2,1)S(1)} %get-tuple-element.39), channel_id=1, source_target_pairs={{0,32},{1,9},{2,34},{3,11},{4,36},{5,13},{6,38},{7,15},{8,40},{9,1... | collective-permute-start | bytes 2850824 | tf_op jit(solution)/shard_map/ppermute | solution.py:47
  71.1 14.6 %collective-permute-start.10 = (bf16[128,3584]{1,0:T(8,128)(2,1)S(1)}, bf16[128,3584]{1,0:T(8,128)(2,1)S(1)}, u32[]{:S(2)}, u32[]{:S(2)}) collective-permute-start(bf16[128,3584]{1,0:T(8,128)(2,1)S(1)} %get-tuple-element.41), channel_id=1, source_target_pairs={{0,96},{1,25},{2,98},{3,27},{4,100},{5,29},{6,102},{7,31},{8,104},... | collective-permute-start | bytes 2752520 | tf_op jit(solution)/shard_map/ppermute | solution.py:47
  86.1 9.9 %collective-permute-start.11 = (bf16[64,3712]{1,0:T(8,128)(2,1)S(1)}, bf16[64,3712]{1,0:T(8,128)(2,1)S(1)}, u32[]{:S(2)}, u32[]{:S(2)}) collective-permute-start(bf16[64,3712]{1,0:T(8,128)(2,1)S(1)} %get-tuple-element.43), channel_id=1, source_target_pairs={{0,96},{1,25},{2,98},{3,27},{4,100},{5,29},{6,102},{7,31},{8,104},... | collective-permute-start | bytes 1425416 | tf_op jit(solution)/shard_map/ppermute | solution.py:47
  87.5 8.5 %collective-permute-start.12 = (bf16[64,3584]{1,0:T(8,128)(2,1)S(1)}, bf16[64,3584]{1,0:T(8,128)(2,1)S(1)}, u32[]{:S(2)}, u32[]{:S(2)}) collective-permute-start(bf16[64,3584]{1,0:T(8,128)(2,1)S(1)} %get-tuple-element.45), channel_id=1, source_target_pairs={{0,32},{1,9},{2,34},{3,11},{4,36},{5,13},{6,38},{7,15},{8,40},{9,1... | collective-permute-start | bytes 1376264 | tf_op jit(solution)/shard_map/ppermute | solution.py:47
  96.2 7.7 %collective-permute-start.13 = (bf16[16,7296]{1,0:T(8,128)(2,1)S(1)}, bf16[16,7296]{1,0:T(8,128)(2,1)S(1)}, u32[]{:S(2)}, u32[]{:S(2)}) collective-permute-start(bf16[16,7296]{1,0:T(8,128)(2,1)S(1)} %get-tuple-element.46), channel_id=1, source_target_pairs={{0,16},{1,65},{2,18},{3,67},{4,20},{5,69},{6,22},{7,71},{8,24},{9,... | collective-permute-start | bytes 700424 | tf_op jit(solution)/shard_map/ppermute | solution.py:47
  97.8 7.2 %collective-permute-start.14 = (bf16[16,7296]{1,0:T(8,128)(2,1)S(1)}, bf16[16,7296]{1,0:T(8,128)(2,1)S(1)}, u32[]{:S(2)}, u32[]{:S(2)}) collective-permute-start(bf16[16,7296]{1,0:T(8,128)(2,1)S(1)} %get-tuple-element.47), channel_id=1, source_target_pairs={{0,8},{1,33},{2,10},{3,35},{4,12},{5,37},{6,14},{7,39},{8,0},{9,41... | collective-permute-start | bytes 700424 | tf_op jit(solution)/shard_map/ppermute | solution.py:47
  98.5 7.9 %collective-permute-start.15 = (bf16[16,7296]{1,0:T(8,128)(2,1)S(1)}, bf16[16,7296]{1,0:T(8,128)(2,1)S(1)}, u32[]{:S(2)}, u32[]{:S(2)}) collective-permute-start(bf16[16,7296]{1,0:T(8,128)(2,1)S(1)} %get-tuple-element.48), channel_id=1, source_target_pairs={{0,24},{1,97},{2,26},{3,99},{4,28},{5,101},{6,30},{7,103},{8,16},{... | collective-permute-start | bytes 700424 | tf_op jit(solution)/shard_map/ppermute | solution.py:47
  106.6 6.1 %collective-permute-start.18 = (bf16[16,3584]{1,0:T(8,128)(2,1)S(1)}, bf16[16,3584]{1,0:T(8,128)(2,1)S(1)}, u32[]{:S(2)}, u32[]{:S(2)}) collective-permute-start(bf16[16,3584]{1,0:T(8,128)(2,1)S(1)} %shard_map.135.refs_0_), channel_id=1, source_target_pairs={{0,24},{1,97},{2,26},{3,99},{4,28},{5,101},{6,30},{7,103},{8,16},{... | collective-permute-start | bytes 344072 | tf_op jit(solution)/shard_map/ppermute | solution.py:47
  108.0 6.3 %collective-permute-start.17 = (bf16[16,3584]{1,0:T(8,128)(2,1)S(1)}, bf16[16,3584]{1,0:T(8,128)(2,1)S(1)}, u32[]{:S(2)}, u32[]{:S(2)}) collective-permute-start(bf16[16,3584]{1,0:T(8,128)(2,1)S(1)} %shard_map.135.refs_0_), channel_id=1, source_target_pairs={{0,16},{1,65},{2,18},{3,67},{4,20},{5,69},{6,22},{7,71},{8,24},{9,... | collective-permute-start | bytes 344072 | tf_op jit(solution)/shard_map/ppermute | solution.py:47
  109.3 6.4 %collective-permute-start.16 = (bf16[16,3584]{1,0:T(8,128)(2,1)S(1)}, bf16[16,3584]{1,0:T(8,128)(2,1)S(1)}, u32[]{:S(2)}, u32[]{:S(2)}) collective-permute-start(bf16[16,3584]{1,0:T(8,128)(2,1)S(1)} %shard_map.135.refs_0_), channel_id=1, source_target_pairs={{0,8},{1,33},{2,10},{3,35},{4,12},{5,37},{6,14},{7,39},{8,0},{9,41... | collective-permute-start | bytes 344072 | tf_op jit(solution)/shard_map/ppermute | solution.py:47
  115.7 10.2 %collective-permute-start.21 = (bf16[64,3584]{1,0:T(8,128)(2,1)S(1)}, bf16[64,3584]{1,0:T(8,128)(2,1)S(1)}, u32[]{:S(2)}, u32[]{:S(2)}) collective-permute-start(bf16[64,3584]{1,0:T(8,128)(2,1)S(1)} %shard_map.136.own), channel_id=1, source_target_pairs={{0,64},{1,17},{2,66},{3,19},{4,68},{5,21},{6,70},{7,23},{8,72},{9,... | collective-permute-start | bytes 1376264 | tf_op jit(solution)/shard_map/ppermute | solution.py:47
  117.4 12.9 %collective-permute-start.20 = (bf16[64,3584]{1,0:T(8,128)(2,1)S(1)}, bf16[64,3584]{1,0:T(8,128)(2,1)S(1)}, u32[]{:S(2)}, u32[]{:S(2)}) collective-permute-start(bf16[64,3584]{1,0:T(8,128)(2,1)S(1)} %shard_map.136.own), channel_id=1, source_target_pairs={{0,32},{1,9},{2,34},{3,11},{4,36},{5,13},{6,38},{7,15},{8,40},{9,1... | collective-permute-start | bytes 1376264 | tf_op jit(solution)/shard_map/ppermute | solution.py:47
  118.9 11.7 %collective-permute-start.19 = (bf16[64,3584]{1,0:T(8,128)(2,1)S(1)}, bf16[64,3584]{1,0:T(8,128)(2,1)S(1)}, u32[]{:S(2)}, u32[]{:S(2)}) collective-permute-start(bf16[64,3584]{1,0:T(8,128)(2,1)S(1)} %shard_map.136.own), channel_id=1, source_target_pairs={{0,96},{1,25},{2,98},{3,27},{4,100},{5,29},{6,102},{7,31},{8,104},... | collective-permute-start | bytes 1376264 | tf_op jit(solution)/shard_map/ppermute | solution.py:47
  133.4 5.7 %collective-permute-start.23 = (bf16[32,512]{1,0:T(8,128)(2,1)S(1)}, bf16[32,512]{1,0:T(8,128)(2,1)S(1)}, u32[]{:S(2)}, u32[]{:S(2)}) collective-permute-start(bf16[32,512]{1,0:T(8,128)(2,1)S(1)} %get-tuple-element.52), channel_id=1, source_target_pairs={{0,4},{1,5},{2,6},{3,7},{4,0},{5,1},{6,2},{7,3},{8,12},{9,13},{10,... | collective-permute-start | bytes 98312 | tf_op jit(solution)/shard_map/ppermute | solution.py:38
  135.0 4.0 %collective-permute-start.24 = (bf16[32,512]{1,0:T(8,128)(2,1)S(1)}, bf16[32,512]{1,0:T(8,128)(2,1)S(1)}, u32[]{:S(2)}, u32[]{:S(2)}) collective-permute-start(bf16[32,512]{1,0:T(8,128)(2,1)S(1)} %get-tuple-element.53), channel_id=1, source_target_pairs={{0,2},{1,3},{2,0},{3,1},{4,6},{5,7},{6,4},{7,5},{8,10},{9,11},{10,... | collective-permute-start | bytes 98312 | tf_op jit(solution)/shard_map/ppermute | solution.py:38
  136.7 5.1 %collective-permute-start.25 = (bf16[32,512]{1,0:T(8,128)(2,1)S(1)}, bf16[32,512]{1,0:T(8,128)(2,1)S(1)}, u32[]{:S(2)}, u32[]{:S(2)}) collective-permute-start(bf16[32,512]{1,0:T(8,128)(2,1)S(1)} %get-tuple-element.54), channel_id=1, source_target_pairs={{0,6},{1,7},{2,4},{3,5},{4,2},{5,3},{6,0},{7,1},{8,14},{9,15},{10,... | collective-permute-start | bytes 98312 | tf_op jit(solution)/shard_map/ppermute | solution.py:38
  (8 other events, 179.6 us)
